TPU v7x, 32 devices: a whole 2x2x4 slice. The times are simulated.
32 devices in a mesh: gx: 4 (over z), gy: 8 (over y, x, core).
Axes of the slice: x: 2, y: 2, z: 4, core: 2. Of those that a mesh axis runs over, the one named last changes fastest.
Arguments:
- initial_state: float32 [2, 16, 48, 1024], P(None, 'gx', None, 'gy'), may hold values from -6 to 6
- eddy_diffusivity: float32 [16, 48, 1024], P('gx', None, 'gy'), may hold values from 0.02 to 0.12
- velocity: float32 [3, 16, 48, 1024], P(None, 'gx', None, 'gy'), may hold values from -0.08 to 0.08
- target: float32 [2, 16, 48, 1024], P(None, 'gx', None, 'gy'), may hold values from -6 to 6
- sensor_cell: int32 [2048], P(('gx', 'gy')), may hold values from 0 to 24575
- sensor_owner: int32 [2048, 1], P(('gx', 'gy')), may hold values from 0 to 31; in each aligned block of 64 rows (0 to 63, 64 to 127, ...) at most 4 rows name the same one
- observations: float32 [2048, 2, 4], P(('gx', 'gy')), may hold values from -6 to 6
- actuator_block: int32 [512], P(('gx', 'gy')), may hold values from 0 to 191
- actuator_owner: int32 [512, 1], P(('gx', 'gy')), may hold values from 0 to 7; in each aligned block of 16 rows (0 to 15, 16 to 31, ...) at most 4 rows name the same one
- controls: float32 [512, 2], P(('gx', 'gy')), may hold values from -6 to 6
- footprint: float32 [512, 128], P(('gx', 'gy')), may hold values from 0 to 1
Outputs:
- final_state: float32 [2, 16, 48, 1024], P(None, 'gx', None, 'gy')
- initial_sensitivity: float32 [2, 16, 48, 1024], P(None, 'gx', None, 'gy')
- actuator_gradient: float32 [512, 2], P(('gx', 'gy'))
Inputs may be any that keep to these rules, and one draw needn't show every extreme that they name: `sensor_owner`: among the 64 rows of one device, no owner is named more than 4 times, a bound that some block reaches. `actuator_owner`: among the 16 rows of one device, no owner is named more than 4 times, a bound that some block reaches.
All inputs are finite; a program needn't handle non-finite values.
Results may differ from a plain program's by a relative error of at most 0.00002.
Values sent between devices are 32-bit elements; how exact they have to be, the bound alone decides.
No kernel may reach another device: no remote copies, remote signals or barrier semaphores. Data moves between devices by JAX's collectives and lax.ppermute only.
A program may use at most 128 MiB of HBM per device.

v0:
```python
import functools

import jax
import jax.numpy as jnp
from jax import lax
from jax.experimental import pallas as pl
from jax.experimental.pallas import tpu as pltpu
from jax.sharding import PartitionSpec as P

FX = 4
FZ = 8
FY = 4
CAPS = 4
CAPA = 4
FOOT = 128
RIM = 8
LANES = 128
SLOT_ROWS = 16
OBS_AT = 0
CELL_AT = 8
CTRL_AT = 16
BLOCK_AT = 18
PRANDTL = 0.85
SCALES = (1.0, 1.0 / PRANDTL)
F32 = jnp.float32
BF16 = jnp.bfloat16
VMEM_BYTES = 48 * 1024 * 1024


def iota(shape, dim):
    return lax.broadcasted_iota(jnp.int32, shape, dim)


def pieces(values, count=3):
    out = []
    for _ in range(count):
        part = values.astype(BF16)
        out.append(part)
        values = values - part.astype(F32)
    return out


def dot(a, b, dims=((1,), (0,))):
    return lax.dot_general(a, b, (dims, ((), ())), preferred_element_type=F32)


def pick(choice, values, dims=((1,), (0,)), count=3):
    total = None
    for part in pieces(values, count):
        term = dot(choice, part, dims)
        total = term if total is None else total + term
    return total


def spread(choice, values, dims=((1,), (0,)), count=3):
    total = None
    for part in pieces(values, count):
        term = dot(part, choice, dims)
        total = term if total is None else total + term
    return total


def roll(values, amount, axis):
    size = values.shape[axis]
    amount = amount % size
    if amount == 0:
        return values
    return pltpu.roll(values, amount, axis)


def swaps(count):
    even = [(i, i ^ 1) for i in range(count) if (i ^ 1) < count]
    odd = [(i, i + 1 if i % 2 else i - 1) for i in range(1, count) if (i % 2 == 0) or i + 1 < count]
    return even, odd


def exchange(values, axis):
    even, odd = swaps(lax.axis_size(axis))
    return lax.ppermute(values, axis, even), lax.ppermute(values, axis, odd)


def low_high(even, odd, is_odd):
    return jnp.where(is_odd, even, odd), jnp.where(is_odd, odd, even)


def call(body, out_shape, scratch, *args):
    return pl.pallas_call(
        body,
        out_shape=out_shape,
        scratch_shapes=scratch,
        compiler_params=pltpu.CompilerParams(vmem_limit_bytes=VMEM_BYTES),
    )(*args)


def rank_row(owner_col, owner_row):
    rows = owner_col.shape[0]
    same = (owner_col == owner_row) & (iota((rows, rows), 0) < iota((rows, rows), 1))
    return jnp.sum(same.astype(F32), axis=0, keepdims=True).astype(jnp.int32)


def rank_col(owner_col, owner_row):
    rows = owner_col.shape[0]
    same = (owner_col == owner_row) & (iota((rows, rows), 1) < iota((rows, rows), 0))
    return jnp.sum(same.astype(F32), axis=1, keepdims=True).astype(jnp.int32)


def strips_body(n_fields, state, kappa, vel, target, out):
    lane = iota((state.shape[2], LANES), 1)
    planes = []
    for ref, count in ((state, 2), (kappa, None), (vel, 3), (target, 2)):
        for f in range(count or 1):
            for p in range(FX):
                planes.append(ref[p] if count is None else ref[f, p])
    for tile in range(n_fields // 2):
        packed = jnp.zeros(lane.shape, F32)
        for g in range(2 * FX):
            moved = roll(planes[tile * 2 * FX + g], RIM + 2 * RIM * g, 1)
            packed = jnp.where(lane // (2 * RIM) == g, moved, packed)
        out[tile] = packed


def records_body(
    n_gx, n_gy, cell, s_owner, s_owner_row, obs, block, a_owner, a_owner_row, ctrl, foot, out, s_meta, a_meta
):
    sens, acts = cell.shape[0], block.shape[0]
    owners = n_gx * n_gy
    s_meta[...] = jnp.zeros((sens, LANES), F32)
    s_meta[:, OBS_AT : OBS_AT + 8] = obs[...]
    s_meta[:, CELL_AT : CELL_AT + 1] = (cell[...] + 1).astype(F32)
    a_meta[...] = jnp.zeros((acts, LANES), F32)
    a_meta[:, CTRL_AT : CTRL_AT + 2] = ctrl[...]
    a_meta[:, BLOCK_AT : BLOCK_AT + 1] = (block[...] + 1).astype(F32)
    s_row, a_row = s_owner_row[...], a_owner_row[...]
    s_rank = rank_row(s_owner[...], s_row)
    a_rank = rank_row(a_owner[...], a_row)
    s_all, a_all, f_all = s_meta[...], a_meta[...], foot[...]
    sens_rows = jnp.zeros((owners, LANES), F32)
    act_rows = jnp.zeros((n_gy, LANES), F32)
    foot_rows = []
    for k in range(CAPS):
        choice = ((s_row == iota((owners, sens), 0)) & (s_rank == k)).astype(BF16)
        sens_rows = sens_rows + roll(pick(choice, s_all), 32 * k, 1)
        choice = ((a_row == iota((n_gy, acts), 0)) & (a_rank == k)).astype(BF16)
        act_rows = act_rows + roll(pick(choice, a_all), 32 * k, 1)
        foot_rows.append(pick(choice, f_all))
    gy_of = iota((n_gy, LANES), 0)
    meta = jnp.concatenate(
        [sens_rows[i * n_gy : (i + 1) * n_gy] + act_rows for i in range(n_gx)], axis=0
    )
    meta_gy = iota((owners, LANES), 0) % n_gy
    for t in range(3):
        def moved(values, at):
            if t == 0:
                return jnp.where(at == 0, 0.0, roll(values, 1, 0))
            if t == 2:
                return jnp.where(at == n_gy - 1, 0.0, roll(values, values.shape[0] - 1, 0))
            return values
        for k in range(CAPA):
            rows = moved(foot_rows[k], gy_of)
            for i in range(n_gx):
                out[i * n_gy : (i + 1) * n_gy, 4 * t + k, :] = rows
        out[:, 12 + t, :] = moved(meta, meta_gy)
    out[:, 15, :] = jnp.zeros((owners, LANES), F32)


def rim_body(even, odd, out):
    is_odd = lax.rem(lax.axis_index("gy"), 2) == 1
    for tile in range(out.shape[0]):
        left, right = low_high(even[tile], odd[tile], is_odd)
        lane = iota(left.shape, 1)
        out[tile] = jnp.where(lane % (2 * RIM) < RIM, roll(right, -RIM, 1), roll(left, RIM, 1))


def source_body(n_gx, n_gy, height, wide_y, got, source, own_foot, own_meta, table, stacked, placing):
    records = n_gy * SLOT_ROWS
    blocks_y = wide_y // FY
    row_id = lax.axis_index("gx")
    r_of, r_to = iota((records, records), 0), iota((records, records), 1)
    slot = r_of % SLOT_ROWS
    moves = [
        (
            (slot < 12) & (slot % 4 == k) & (r_to == r_of - slot + 12 + slot // 4)
        ).astype(BF16)
        for k in range(CAPA)
    ]
    q_of, l_of = iota((FOOT, FOOT), 0), iota((FOOT, FOOT), 1)
    unpack = (l_of == (q_of % 32) * FY + q_of // 32).astype(BF16)
    for q in range(3):
        row = row_id + (q - 1)
        inside = (row >= 0) & (row < n_gx)
        base = jnp.clip(row, 0, n_gx - 1) * n_gy
        records_in = got[pl.ds(base, n_gy)].reshape(records, LANES)
        meta = jnp.zeros((records, LANES), F32)
        for k in range(CAPA):
            meta = meta + pick(moves[k], roll(records_in, -32 * k, 1))
        meta = jnp.where(inside, meta, 0.0)
        meta_t = meta.T
        block_row = meta_t[BLOCK_AT : BLOCK_AT + 1, :].astype(jnp.int32) - 1
        bz_row = block_row // blocks_y
        foot_t = pick(unpack, records_in, ((1,), (1,)))
        block_col = meta[:, BLOCK_AT : BLOCK_AT + 1].astype(jnp.int32) - 1
        by = block_col % blocks_y
        side = (iota((records, 1), 0) % SLOT_ROWS) // 4
        usable = (block_col >= 0) & (
            (side == 1)
            | ((side == 0) & (by * FY >= wide_y - RIM))
            | ((side == 2) & (by * FY < RIM))
        )
        start = jnp.where(side == 1, by * FY, wide_y + by * FY)
        start = jnp.where(usable, start, -FY)
        for fy in range(FY):
            placing[fy * records : (fy + 1) * records, :] = (
                iota((records, 2 * wide_y), 1) == start + fy
            ).astype(BF16)
        for s in range(2):
            force = meta_t[CTRL_AT + s : CTRL_AT + s + 1, :]
            for fy in range(FY):
                for x in range(FX):
                    piece = foot_t[fy * 32 + x * FZ : fy * 32 + (x + 1) * FZ, :]
                    scaled = piece * force
                    for bz in range(height // FZ):
                        rows = slice(x * height + bz * FZ, x * height + (bz + 1) * FZ)
                        stacked[rows, fy * records : (fy + 1) * records] = jnp.where(
                            bz_row == bz, scaled, 0.0
                        )
                        if q == 1 and s == 0:
                            own_foot[fy, rows, :] = jnp.where(bz_row == bz, piece, 0.0)
            source[s, q] = spread(placing[...], stacked[...])
        if q == 1:
            own_meta[...] = jnp.where((side == 1) & (block_col >= 0), meta, 0.0)
    devices = got.shape[0]
    for n, t in enumerate((1, 0, 2)):
        rows = got[:, 12 + t, :]
        for k in range(CAPS):
            at = (n * CAPS + k) * devices
            table[at : at + devices, :] = roll(rows, -32 * k, 1)


def rim_tile(packed, group):
    lane = iota(packed.shape, 1)
    right = roll(packed, -2 * RIM * group, 1)
    left = roll(packed, LANES - 2 * RIM - 2 * RIM * group, 1)
    return jnp.where(lane < RIM, right, jnp.where(lane >= LANES - RIM, left, 0.0))


def extended(field, main, main_e, main_o, rim, rim_e, rim_o, is_odd, x):
    tile, group = field // 2, (field % 2) * FX + x % FX
    if x // FX == 1:
        centre, halo = main[field, x % FX], rim[tile]
    elif x // FX == 0:
        centre = jnp.where(is_odd, main_e[field, x], main_o[field, x])
        halo = jnp.where(is_odd, rim_e[tile], rim_o[tile])
    else:
        centre = jnp.where(is_odd, main_o[field, x - 2 * FX], main_e[field, x - 2 * FX])
        halo = jnp.where(is_odd, rim_o[tile], rim_e[tile])
    return centre, rim_tile(halo, group)


def build_coeffs(n_gx, n_gy, refs, half_k, half_u, coeffs):
    main, main_e, main_o, rim, rim_e, rim_o = refs
    row_id, col_id = lax.axis_index("gx"), lax.axis_index("gy")
    is_odd = lax.rem(row_id, 2) == 1
    wide = 3 * FX
    for x in range(wide):
        for field in range(2, 6):
            centre, halo = extended(field, *refs, is_odd, x)
            dest = half_k.at[x] if field == 2 else half_u.at[field - 3, x]
            dest[:, :LANES] = 0.5 * centre
            dest[:, LANES:] = 0.5 * halo
    height = half_k.shape[1]
    shape = (height, 2 * LANES)
    lane, z = iota(shape, 1), iota(shape, 0)

    def lane_in(at):
        return (
            (at < LANES)
            | ((at < LANES + RIM) & (col_id < n_gy - 1))
            | ((at >= 2 * LANES - RIM) & (col_id > 0))
        )

    here = lane_in(lane)
    ahead = here & lane_in((lane + 1) % (2 * LANES))
    behind = here & lane_in((lane + 2 * LANES - 1) % (2 * LANES))

    def plane_in(x):
        return (
            ((x >= FX) | (row_id > 0)) & ((x < 2 * FX) | (row_id < n_gx - 1))
        )

    def one(x, carry):
        k = half_k[x]
        before, after = half_k[jnp.maximum(x - 1, 0)], half_k[jnp.minimum(x + 1, wide - 1)]
        inside = plane_in(x)
        faces = (
            k + after,
            k + before,
            k + roll(k, -1, 1),
            k + roll(k, 1, 1),
            k + jnp.where(z == height - 1, 0.0, roll(k, -1, 0)),
            k + jnp.where(z == 0, 0.0, roll(k, 1, 0)),
        )
        masks = (
            here & inside & plane_in(x + 1),
            here & inside & plane_in(x - 1),
            ahead & inside,
            behind & inside,
            here & inside & (z < height - 1),
            here & inside & (z > 0),
        )
        total = (faces[0] + faces[1]) + (faces[2] + faces[3]) + (faces[4] + faces[5])
        for s in range(2):
            coeffs[s, 6, x] = 1.0 - SCALES[s] * total
            for side in range(6):
                drift = half_u[side // 2, x]
                value = SCALES[s] * faces[side]
                value = value - drift if side % 2 == 0 else value + drift
                coeffs[s, side, x] = jnp.where(masks[side], value, 0.0)
        return carry

    lax.fori_loop(0, wide, one, 0)


def cell_parts(table_col, own_count, wide_y):
    cell = table_col.astype(jnp.int32) - 1
    return cell // wide_y, cell % wide_y, cell >= 0


def forward_body(n_gx, n_gy, steps, main, main_e, main_o, rim, rim_e, rim_o, source, table, target, final, sent, half_k, half_u, coeffs, cur):
    refs = (main, main_e, main_o, rim, rim_e, rim_o)
    is_odd = lax.rem(lax.axis_index("gx"), 2) == 1
    height = half_k.shape[1]
    build_coeffs(n_gx, n_gy, refs, half_k, half_u, coeffs)
    wide = 3 * FX
    for x in range(wide):
        for s in range(2):
            centre, halo = extended(s, *refs, is_odd, x)
            cur[0, s, x, :, :LANES] = centre
            cur[0, s, x, :, LANES:] = halo
    slots = table.shape[0]
    own = slots // 3
    records = table[...]
    cell = records[:, CELL_AT : CELL_AT + 1].astype(jnp.int32) - 1
    spot = cell // LANES
    at_y = cell % LANES
    slot_id = iota((slots, 1), 0)
    live = (cell >= 0) & (
        (slot_id < own)
        | ((slot_id < 2 * own) & (at_y >= LANES - RIM))
        | ((slot_id >= 2 * own) & (at_y < RIM))
    )
    cells = FX * height
    rows_hot = ((iota((slots, cells), 1) == spot) & live).astype(BF16)
    lane_hot = (iota((slots, LANES), 1) == at_y) & live
    rows_hot_t = None
    lane = iota((slots, LANES), 1)
    residuals = jnp.where(lane == CELL_AT, jnp.where(live, records, 0.0), 0.0)
    for n in range(steps):
        now, later = n % 2, (n + 1) % 2

        def one(x, carry):
            for s in range(2):
                c = cur[now, s, x]
                value = coeffs[s, 6, x] * c + source[s, x]
                value = value + coeffs[s, 0, x] * cur[now, s, x + 1]
                value = value + coeffs[s, 1, x] * cur[now, s, x - 1]
                value = value + coeffs[s, 2, x] * roll(c, -1, 1)
                value = value + coeffs[s, 3, x] * roll(c, 1, 1)
                value = value + coeffs[s, 4, x] * roll(c, -1, 0)
                value = value + coeffs[s, 5, x] * roll(c, 1, 0)
                cur[later, s, x] = value
            return carry

        lax.fori_loop(n + 1, wide - n - 1, one, 0)
        for s in range(2):
            field = cur[later, s, FX : 2 * FX].reshape(cells, 2 * LANES)
            got = jnp.concatenate(
                [
                    pick(rows_hot[:own], field[:, :LANES]),
                    pick(rows_hot[own:], field[:, LANES:]),
                ],
                axis=0,
            )
            value = jnp.sum(jnp.where(lane_hot, got, 0.0), axis=1, keepdims=True)
            at = OBS_AT + s * steps + n
            value = jnp.where(live, value - records[:, at : at + 1], 0.0)
            residuals = jnp.where(lane == at, value, residuals)
    last = steps % 2
    spot_row = residuals.T[CELL_AT : CELL_AT + 1, :].astype(jnp.int32) - 1
    spot_row = jnp.where(spot_row >= 0, spot_row // LANES, -1)
    rows_hot_t = (iota((cells, slots), 0) == spot_row).astype(BF16)
    sent_rim = jnp.zeros((height, LANES), F32)
    rim_lane = iota((height, LANES), 1)
    for s in range(2):
        at = OBS_AT + s * steps + steps - 1
        value = jnp.where(lane_hot, residuals[:, at : at + 1], 0.0)
        put_main = pick(rows_hot_t[:, :own], value[:own])
        put_rim = pick(rows_hot_t[:, own:], value[own:])
        for p in range(FX):
            rows = slice(p * height, (p + 1) * height)
            got = cur[last, s, FX + p]
            final[s, p] = got[:, :LANES]
            sent[(s * FX + p) * height : (s * FX + p + 1) * height, :] = (
                got[:, :LANES] - target[s, p] + put_main[rows]
            )
            halo = got[:, LANES:] - rim_tile(rim[3], s * FX + p) + put_rim[rows]
            g = s * FX + p
            inner = rim_lane - 2 * RIM * g
            right = roll(halo, 2 * RIM * g, 1)
            left = roll(halo, 2 * RIM * g + 2 * RIM, 1)
            sent_rim = jnp.where((inner >= 0) & (inner < RIM), right, sent_rim)
            sent_rim = jnp.where((inner >= RIM) & (inner < 2 * RIM), left, sent_rim)
    base = 2 * FX * height
    sent[base : base + height, :] = sent_rim
    rows = slots // 8
    packed = jnp.zeros((rows, LANES), F32)
    pack_lane = iota((rows, LANES), 1)
    for b in range(8):
        packed = jnp.where(
            pack_lane // 16 == b, roll(residuals[b * rows : (b + 1) * rows], 16 * b, 1), packed
        )
    sent[base + height : base + height + rows, :] = packed


def adjoint_body(n_gx, n_gy, steps, main, main_e, main_o, rim, rim_e, rim_o, sent, sent_e, sent_o, own_foot, own_meta, first, gradient, half_k, half_u, coeffs, cur, puts, summed):
    refs = (main, main_e, main_o, rim, rim_e, rim_o)
    is_odd = lax.rem(lax.axis_index("gx"), 2) == 1
    height = half_k.shape[1]
    build_coeffs(n_gx, n_gy, refs, half_k, half_u, coeffs)
    wide = 3 * FX
    cells = FX * height
    base = 2 * FX * height
    rows = sent.shape[0] - base - height
    slots = rows * 8
    own = slots // 3
    for q in range(3):
        def take(lo, hi):
            if q == 1:
                return sent[lo:hi, :]
            if q == 0:
                return jnp.where(is_odd, sent_e[lo:hi, :], sent_o[lo:hi, :])
            return jnp.where(is_odd, sent_o[lo:hi, :], sent_e[lo:hi, :])
        packed_rim = take(base, base + height)
        for s in range(2):
            for p in range(FX):
                g = s * FX + p
                cur[0, s, q * FX + p, :, :LANES] = take(g * height, (g + 1) * height)
                cur[0, s, q * FX + p, :, LANES:] = rim_tile(packed_rim, g)
        packed = take(base + height, base + height + rows)
        records = jnp.concatenate([roll(packed, -16 * b, 1) for b in range(8)], axis=0)
        cell = records[:, CELL_AT : CELL_AT + 1].astype(jnp.int32) - 1
        live = cell >= 0
        lane_hot = (iota((slots, LANES), 1) == cell % LANES) & live
        cell_row = records.T[CELL_AT : CELL_AT + 1, :].astype(jnp.int32) - 1
        cell_row = jnp.where(cell_row >= 0, cell_row // LANES, -1)
        hot_t = (iota((cells, slots), 0) == cell_row).astype(BF16)
        for n in range(steps - 1):
            for s in range(2):
                at = OBS_AT + s * steps + n
                value = jnp.where(lane_hot, records[:, at : at + 1], 0.0)
                for side, part in enumerate((slice(0, own), slice(own, slots))):
                    put = pick(hot_t[:, part], value[part])
                    puts[n, s, q * FX : (q + 1) * FX, :, side * LANES : (side + 1) * LANES] = (
                        put.reshape(FX, height, LANES)
                    )
    for s in range(2):
        summed[s] = cur[0, s, FX : 2 * FX, :, :LANES]
    for turn in range(steps):
        now, later = turn % 2, (turn + 1) % 2
        n = steps - 2 - turn

        def one(x, carry):
            for s in range(2):
                w = cur[now, s, x]
                value = coeffs[s, 6, x] * w
                if n >= 0:
                    value = value + puts[n, s, x]
                value = value + coeffs[s, 1, x + 1] * cur[now, s, x + 1]
                value = value + coeffs[s, 0, x - 1] * cur[now, s, x - 1]
                value = value + roll(coeffs[s, 3, x] * w, -1, 1)
                value = value + roll(coeffs[s, 2, x] * w, 1, 1)
                value = value + roll(coeffs[s, 5, x] * w, -1, 0)
                value = value + roll(coeffs[s, 4, x] * w, 1, 0)
                cur[later, s, x] = value
            return carry

        lax.fori_loop(turn + 1, wide - turn - 1, one, 0)
        for s in range(2):
            if n >= 0:
                summed[s] = summed[s] + cur[later, s, FX : 2 * FX, :, :LANES]
            else:
                first[s] = cur[later, s, FX : 2 * FX, :, :LANES]
    records = own_meta.shape[0]
    block = own_meta[:, BLOCK_AT : BLOCK_AT + 1].astype(jnp.int32) - 1
    start = jnp.where(block >= 0, (block % (LANES // FY)) * FY, -FY)
    lane = iota((records, LANES), 1)
    out_row = iota((n_gy, records), 0)
    out_from = iota((n_gy, records), 1) // SLOT_ROWS
    for s in range(2):
        field = summed[s].reshape(cells, LANES)
        total = jnp.zeros((1, records), F32)
        for fy in range(FY):
            hot = (lane == start + fy).astype(BF16)
            seen = spread(hot, field, ((1,), (1,)))
            total = total + jnp.sum(seen * own_foot[fy], axis=0, keepdims=True)
        gradient[:, s, :] = jnp.where(out_row == out_from, total, 0.0)


def returned_body(got, owner, owner_row, out):
    acts = owner.shape[0]
    n_gy, _, records = got.shape
    rank = rank_col(owner[...], owner_row[...])
    choice = (owner[...] == iota((acts, n_gy), 1)).astype(BF16)
    at = lax.axis_index("gy") * SLOT_ROWS + CAPA + rank
    hot = iota((acts, records), 1) == at
    for s in range(2):
        rows = pick(choice, got[:, s, :])
        out[:, s : s + 1] = jnp.sum(jnp.where(hot, rows, 0.0), axis=1, keepdims=True)


def per_device(
    initial_state,
    eddy_diffusivity,
    velocity,
    target,
    sensor_cell,
    sensor_owner,
    observations,
    actuator_block,
    actuator_owner,
    controls,
    footprint,
):
    _, wide_x, height, wide_y = initial_state.shape
    steps = observations.shape[2]
    n_gx, n_gy = lax.axis_size("gx"), lax.axis_size("gy")
    devices = n_gx * n_gy
    sens, acts = sensor_cell.shape[0], actuator_block.shape[0]
    records = n_gy * SLOT_ROWS
    shape = jax.ShapeDtypeStruct
    vmem = pltpu.VMEM
    s_owner_row = sensor_owner.reshape(1, sens)
    a_owner_row = actuator_owner.reshape(1, acts)

    main = jnp.concatenate([initial_state, eddy_diffusivity[None], velocity], axis=0)
    outgoing = call(
        functools.partial(records_body, n_gx, n_gy),
        shape((devices, SLOT_ROWS, LANES), F32),
        [vmem((sens, LANES), F32), vmem((acts, LANES), F32)],
        sensor_cell.reshape(sens, 1),
        sensor_owner,
        s_owner_row,
        observations.reshape(sens, 2 * steps),
        actuator_block.reshape(acts, 1),
        actuator_owner,
        a_owner_row,
        controls,
        footprint,
    )
    strips = call(
        functools.partial(strips_body, 8),
        shape((4, height, LANES), F32),
        [],
        initial_state,
        eddy_diffusivity,
        velocity,
        target,
    )
    got = lax.all_to_all(outgoing, ("gx", "gy"), split_axis=0, concat_axis=0, tiled=True)
    main_e, main_o = exchange(main, "gx")
    strips_e, strips_o = exchange(strips, "gy")
    rim = call(rim_body, shape((4, height, LANES), F32), [], strips_e, strips_o)
    rim_e, rim_o = exchange(rim[:3], "gx")
    source, own_foot, own_meta, table = call(
        functools.partial(source_body, n_gx, n_gy, height, wide_y),
        (
            shape((2, 3, FX * height, 2 * LANES), F32),
            shape((FY, FX * height, records), F32),
            shape((records, LANES), F32),
            shape((3 * CAPS * devices, LANES), F32),
        ),
        [vmem((FX * height, FY * records), F32), vmem((FY * records, 2 * LANES), BF16)],
        got,
    )
    source = source.reshape(2, 3 * FX, height, 2 * LANES)
    slots = 3 * CAPS * devices
    sent_rows = 2 * FX * height + height + slots // 8
    fields = [
        vmem((3 * FX, height, 2 * LANES), F32),
        vmem((3, 3 * FX, height, 2 * LANES), F32),
        vmem((2, 7, 3 * FX, height, 2 * LANES), F32),
        vmem((2, 2, 3 * FX, height, 2 * LANES), F32),
    ]
    final, sent = call(
        functools.partial(forward_body, n_gx, n_gy, steps),
        (shape((2, FX, height, LANES), F32), shape((sent_rows, LANES), F32)),
        fields,
        main, main_e, main_o, rim, rim_e, rim_o, source, table, target,
    )
    sent_e, sent_o = exchange(sent, "gx")
    first, gradient = call(
        functools.partial(adjoint_body, n_gx, n_gy, steps),
        (shape((2, FX, height, LANES), F32), shape((n_gy, 2, records), F32)),
        fields
        + [
            vmem((steps - 1, 2, 3 * FX, height, 2 * LANES), F32),
            vmem((2, FX, height, LANES), F32),
        ],
        main, main_e, main_o, rim, rim_e, rim_o, sent, sent_e, sent_o, own_foot, own_meta,
    )
    back = lax.all_to_all(gradient, "gy", split_axis=0, concat_axis=0, tiled=True)
    returned = call(
        returned_body, shape((acts, 2), F32), [], back, actuator_owner, a_owner_row
    )
    return (final, first, returned)


def solution(mesh):
    in_specs = (
        P(None, "gx", None, "gy"),
        P("gx", None, "gy"),
        P(None, "gx", None, "gy"),
        P(None, "gx", None, "gy"),
        P(("gx", "gy")),
        P(("gx", "gy"), None),
        P(("gx", "gy"), None, None),
        P(("gx", "gy")),
        P(("gx", "gy"), None),
        P(("gx", "gy"), None),
        P(("gx", "gy"), None),
    )
    out_specs = (P(None, "gx", None, "gy"), P(None, "gx", None, "gy"), P(("gx", "gy"), None))
    return jax.shard_map(
        per_device, mesh=mesh, in_specs=in_specs, out_specs=out_specs, check_vma=False
    )
```

profile of v0, /device:TPU:0, one launch (start us, length us, event | category | flops | bytes accessed | tf_op | source)
XLA Modules:
  0.0 71.5 jit_solution(2881955277126488033)
XLA Ops:
  0.6 0.0 copy-start
  0.6 0.0 copy-start.1
  0.7 0.0 copy-start.3
  0.7 0.0 copy-start.5
  0.7 0.0 copy-start.10
  0.7 0.0 copy-start.8
  0.7 0.0 copy-start.9
  0.7 0.0 copy-start.7
  0.7 0.0 copy-start.6
  0.7 0.0 copy-start.4
  0.7 0.0 copy-start.2
  0.7 1.3 %pad_maximum_fusion.main = f32[6,4,48,128]{3,2,1,0:T(8,128)S(1)} fusion(f32[3,4,48,128]{3,2,1,0:T(8,128)} %vel.1, f32[1,4,48,128]{3,2,1,0:T(8,128)} %bitcast.8, f32[2,4,48,128]{3,2,1,0:T(8,128)} %state.1), kind=kLoop, calls=%fused_computation | loop fusion | flops 294912 | bytes 1179648 | tf_op jit(solution)/shard_map/concatenate | solution.py:544
  2.0 0.7 collective-permute-start.1
  2.7 5.9 %collective-permute-start = (f32[6,4,48,128]{3,2,1,0:T(8,128)S(1)}, f32[6,4,48,128]{3,2,1,0:T(8,128)S(1)}, u32[]{:S(2)}, u32[]{:S(2)}) collective-permute-start(f32[6,4,48,128]{3,2,1,0:T(8,128)S(1)} %pad_maximum_fusion.main), channel_id=1, source_target_pairs={{0,8},{8,0},{16,24},{24,16},{1,9},{9,1},{17,25},{25,17},{2,10},{10... | collective-permute-start | bytes 1769480 | tf_op jit(solution)/shard_map/ppermute | solution.py:79
  8.6 0.0 copy-done.5
  8.6 0.1 copy.26.a_owner.owner
  8.7 0.0 copy-done.10
  8.7 0.1 copy.25.block
  8.8 0.0 copy-done.8
  8.8 0.1 copy.27.ctrl
  8.9 0.0 copy-done.9
  8.9 0.1 copy.22.cell
  9.0 0.0 copy-done.7
  9.0 0.1 copy.24.obs
  9.1 0.0 copy-done.6
  9.1 0.1 copy.23.s_owner
  9.2 0.0 copy-done.4
  9.2 1.2 %shard_map.132 = f32[32,16,128]{2,1,0:T(8,128)} custom-call(s32[64,1]{1,0:T(8,128)S(1)} %copy.22.cell, s32[64,1]{1,0:T(8,128)S(1)} %copy.23.s_owner, s32[1,64]{1,0:T(1,128)S(1)} %bitcast.11, f32[64,8]{1,0:T(8,128)S(1)} %copy.24.obs, s32[16,1]{1,0:T(8,128)S(1)} %copy.25.block, s32[16,1]{1,0:T(8,128)S(1)} %copy.26.a_owner.owner, s32[1,16]{1,0:T(1,128)S(1)} %bitcast.9, ...), custom_call_target="tpu_custom_call" | custom-call | tf_op jit(solution)/shard_map/pallas_call | solution.py:87
  10.3 3.6 %all-to-all-start = ((f32[32,16,128]{2,1,0:T(8,128)}), f32[32,16,128]{2,1,0:T(8,128)S(1)}, u32[]{:S(2)}, u32[]{:S(2)}) async-start(f32[32,16,128]{2,1,0:T(8,128)} %shard_map.132), calls=%async_computation | async-start | bytes 524288 | tf_op jit(solution)/shard_map/all_to_all | solution.py:568
  13.9 0.0 copy-done
  13.9 0.0 copy-done.1
  13.9 0.0 copy-done.3
  14.0 0.0 copy-done.2
  14.0 0.3 shard_map.130
  14.2 0.7 collective-permute-start.3
  14.9 3.2 %collective-permute-start.2 = (f32[4,48,128]{2,1,0:T(8,128)S(1)}, f32[4,48,128]{2,1,0:T(8,128)S(1)}, u32[]{:S(2)}, u32[]{:S(2)}) collective-permute-start(f32[4,48,128]{2,1,0:T(8,128)S(1)} %shard_map.130), channel_id=1, source_target_pairs={{0,1},{1,0},{2,3},{3,2},{4,5},{5,4},{6,7},{7,6},{8,9},{9,8},{10,11... | collective-permute-start | bytes 294920 | tf_op jit(solution)/shard_map/ppermute | solution.py:79
  18.1 0.0 collective-permute-done.3.odd
  18.1 0.9 %collective-permute-done.2.even = f32[4,48,128]{2,1,0:T(8,128)S(1)} collective-permute-done((f32[4,48,128]{2,1,0:T(8,128)S(1)}, f32[4,48,128]{2,1,0:T(8,128)S(1)}, u32[]{:S(2)}, u32[]{:S(2)}) %collective-permute-start.2) | collective-permute-done | bytes 98336 | tf_op jit(solution)/shard_map/ppermute | solution.py:79
  19.0 0.1 shard_map.131.rim
  19.2 0.7 collective-permute-start.5
  19.9 4.2 %collective-permute-start.4 = (f32[3,48,128]{2,1,0:T(8,128)S(1)}, f32[3,48,128]{2,1,0:T(8,128)S(1)}, u32[]{:S(2)}, u32[]{:S(2)}) collective-permute-start(f32[3,48,128]{2,1,0:T(8,128)S(1)} %slice.4), channel_id=1, source_target_pairs={{0,8},{8,0},{16,24},{24,16},{1,9},{9,1},{17,25},{25,17},{2,10},{10... | collective-permute-start | bytes 221192 | tf_op jit(solution)/shard_map/ppermute | solution.py:79
  24.1 4.6 %all-to-all-done.got = f32[32,16,128]{2,1,0:T(8,128)S(1)} async-done(((f32[32,16,128]{2,1,0:T(8,128)}), f32[32,16,128]{2,1,0:T(8,128)S(1)}, u32[]{:S(2)}, u32[]{:S(2)}) %all-to-all-start) | async-done | bytes 262176 | tf_op jit(solution)/shard_map/all_to_all | solution.py:568
  28.7 2.7 %shard_map.133 = (f32[2,3,192,256]{3,2,1,0:T(8,128)S(1)}, f32[4,192,128]{2,1,0:T(8,128)S(1)}, f32[128,128]{1,0:T(8,128)S(1)}, f32[384,128]{1,0:T(8,128)S(1)}) custom-call(f32[32,16,128]{2,1,0:T(8,128)S(1)} %all-to-all-done.got), custom_call_target="tpu_custom_call" | custom-call | tf_op jit(solution)/shard_map/pallas_call | solution.py:87
  31.4 0.0 collective-permute-done.5.rim_o
  31.4 0.0 collective-permute-done.4.rim_e
  31.4 0.0 collective-permute-done.1.main_o
  31.4 0.0 collective-permute-done.main_e
  31.5 11.0 %shard_map.134 = (f32[2,4,48,128]{3,2,1,0:T(8,128)}, f32[480,128]{1,0:T(8,128)S(1)}) custom-call(f32[6,4,48,128]{3,2,1,0:T(8,128)S(1)} %pad_maximum_fusion.main, f32[6,4,48,128]{3,2,1,0:T(8,128)S(1)} %collective-permute-done.main_e, f32[6,4,48,128]{3,2,1,0:T(8,128)S(1)} %collective-permute-done.1.main_o, f32[4,48,128]{2,1,0:T(8,128)S(1)} %shard_map.131.rim, ...), custom_call_target="tpu_custom_call" | custom-call | tf_op jit(solution)/shard_map/pallas_call | solution.py:87
  42.5 0.8 %collective-permute-start.7 = (f32[480,128]{1,0:T(8,128)S(1)}, f32[480,128]{1,0:T(8,128)S(1)}, u32[]{:S(2)}, u32[]{:S(2)}) collective-permute-start(f32[480,128]{1,0:T(8,128)S(1)} %get-tuple-element.14.sent), channel_id=1, source_target_pairs={{8,16},{16,8},{9,17},{17,9},{10,18},{18,10},{11,19},{19,11},{12,20... | collective-permute-start | bytes 737288 | tf_op jit(solution)/shard_map/ppermute | solution.py:79
  43.3 3.7 %collective-permute-start.6 = (f32[480,128]{1,0:T(8,128)S(1)}, f32[480,128]{1,0:T(8,128)S(1)}, u32[]{:S(2)}, u32[]{:S(2)}) collective-permute-start(f32[480,128]{1,0:T(8,128)S(1)} %get-tuple-element.14.sent), channel_id=1, source_target_pairs={{0,8},{8,0},{16,24},{24,16},{1,9},{9,1},{17,25},{25,17},{2,10},{10... | collective-permute-start | bytes 737288 | tf_op jit(solution)/shard_map/ppermute | solution.py:79
  47.0 0.0 collective-permute-done.7.sent_o
  47.0 6.4 %collective-permute-done.6.sent_e = f32[480,128]{1,0:T(8,128)S(1)} collective-permute-done((f32[480,128]{1,0:T(8,128)S(1)}, f32[480,128]{1,0:T(8,128)S(1)}, u32[]{:S(2)}, u32[]{:S(2)}) %collective-permute-start.6) | collective-permute-done | bytes 245792 | tf_op jit(solution)/shard_map/ppermute | solution.py:79
  53.4 10.1 %shard_map.135 = (f32[2,4,48,128]{3,2,1,0:T(8,128)}, f32[8,2,128]{2,1,0:T(2,128)S(1)}) custom-call(f32[6,4,48,128]{3,2,1,0:T(8,128)S(1)} %pad_maximum_fusion.main, f32[6,4,48,128]{3,2,1,0:T(8,128)S(1)} %collective-permute-done.main_e, f32[6,4,48,128]{3,2,1,0:T(8,128)S(1)} %collective-permute-done.1.main_o, f32[4,48,128]{2,1,0:T(8,128)S(1)} %shard_map.131.rim, ...), custom_call_target="tpu_custom_call" | custom-call | tf_op jit(solution)/shard_map/pallas_call | solution.py:87
  63.5 7.1 %all_to_all.10.got = f32[8,2,128]{2,1,0:T(2,128)S(1)} all-to-all(f32[8,2,128]{2,1,0:T(2,128)S(1)} %get-tuple-element.18), channel_id=1, replica_groups=mesh['gx'=4,'gy'=8] {'gy'}, dimensions={0} | all-to-all | bytes 16384 | tf_op jit(solution)/shard_map/all_to_all | solution.py:610
  70.6 0.3 shard_map.136
  70.9 0.7 copy.29
  (1 shorter events, 0.0 us)
Async XLA Ops:
  0.6 13.3 %copy-start = (f32[3,4,48,128]{3,2,1,0:T(8,128)S(1)}, f32[3,4,48,128]{3,2,1,0:T(8,128)}, u32[]{:S(2)}) copy-start(f32[3,4,48,128]{3,2,1,0:T(8,128)} %vel.1) | copy-start | bytes 884740
  0.6 13.3 %copy-start.1 = (f32[2,4,48,128]{3,2,1,0:T(8,128)S(1)}, f32[2,4,48,128]{3,2,1,0:T(8,128)}, u32[]{:S(2)}) copy-start(f32[2,4,48,128]{3,2,1,0:T(8,128)} %state.1) | copy-start | bytes 589828
  0.7 13.3 %copy-start.3 = (f32[4,48,128]{2,1,0:T(8,128)S(1)}, f32[4,48,128]{2,1,0:T(8,128)}, u32[]{:S(2)}) copy-start(f32[4,48,128]{2,1,0:T(8,128)} %kappa.1) | copy-start | bytes 294916
  0.7 8.0 %copy-start.5 = (s32[16,1]{0,1:T(1,128)S(1)}, s32[16,1]{0,1:T(1,128)}, u32[]{:S(2)}) copy-start(s32[16,1]{0,1:T(1,128)} %param.19) | copy-start | bytes 196
  0.7 8.0 %copy-start.10 = (s32[16]{0:T(128)S(1)}, s32[16]{0:T(128)}, u32[]{:S(2)}) copy-start(s32[16]{0:T(128)} %param.18) | copy-start | bytes 196
  0.7 8.1 %copy-start.8 = (f32[16,2]{0,1:T(2,128)S(1)}, f32[16,2]{0,1:T(2,128)}, u32[]{:S(2)}) copy-start(f32[16,2]{0,1:T(2,128)} %param.20) | copy-start | bytes 388
  0.7 8.2 %copy-start.9 = (s32[64]{0:T(128)S(1)}, s32[64]{0:T(128)}, u32[]{:S(2)}) copy-start(s32[64]{0:T(128)} %param.15) | copy-start | bytes 772
  0.7 8.3 %copy-start.7 = (f32[64,2,4]{0,2,1:T(4,128)S(1)}, f32[64,2,4]{0,2,1:T(4,128)}, u32[]{:S(2)}) copy-start(f32[64,2,4]{0,2,1:T(4,128)} %param.17) | copy-start | bytes 6148
  0.7 8.3 %copy-start.6 = (s32[64,1]{0,1:T(1,128)S(1)}, s32[64,1]{0,1:T(1,128)}, u32[]{:S(2)}) copy-start(s32[64,1]{0,1:T(1,128)} %param.16) | copy-start | bytes 772
  0.7 8.4 %copy-start.4 = (f32[16,128]{1,0:T(8,128)S(1)}, f32[16,128]{1,0:T(8,128)}, u32[]{:S(2)}) copy-start(f32[16,128]{1,0:T(8,128)} %foot.1) | copy-start | bytes 24580
  0.7 13.2 %copy-start.2 = (f32[2,4,48,128]{3,2,1,0:T(8,128)S(1)}, f32[2,4,48,128]{3,2,1,0:T(8,128)}, u32[]{:S(2)}) copy-start(f32[2,4,48,128]{3,2,1,0:T(8,128)} %target.3) | copy-start | bytes 589828
  2.0 29.4 %collective-permute-start.1 = (f32[6,4,48,128]{3,2,1,0:T(8,128)S(1)}, f32[6,4,48,128]{3,2,1,0:T(8,128)S(1)}, u32[]{:S(2)}, u32[]{:S(2)}) collective-permute-start(f32[6,4,48,128]{3,2,1,0:T(8,128)S(1)} %pad_maximum_fusion.main), channel_id=1, source_target_pairs={{8,16},{16,8},{9,17},{17,9},{10,18},{18,10},{11,19},{19,11},{12,20... | collective-permute-start | bytes 1769480 | tf_op jit(solution)/shard_map/ppermute | solution.py:79
  2.7 28.7 %collective-permute-start = (f32[6,4,48,128]{3,2,1,0:T(8,128)S(1)}, f32[6,4,48,128]{3,2,1,0:T(8,128)S(1)}, u32[]{:S(2)}, u32[]{:S(2)}) collective-permute-start(f32[6,4,48,128]{3,2,1,0:T(8,128)S(1)} %pad_maximum_fusion.main), channel_id=1, source_target_pairs={{0,8},{8,0},{16,24},{24,16},{1,9},{9,1},{17,25},{25,17},{2,10},{10... | collective-permute-start | bytes 1769480 | tf_op jit(solution)/shard_map/ppermute | solution.py:79
  10.3 18.4 %all-to-all-start = ((f32[32,16,128]{2,1,0:T(8,128)}), f32[32,16,128]{2,1,0:T(8,128)S(1)}, u32[]{:S(2)}, u32[]{:S(2)}) async-start(f32[32,16,128]{2,1,0:T(8,128)} %shard_map.132), calls=%async_computation | async-start | bytes 524288 | tf_op jit(solution)/shard_map/all_to_all | solution.py:568
  14.2 3.9 %collective-permute-start.3 = (f32[4,48,128]{2,1,0:T(8,128)S(1)}, f32[4,48,128]{2,1,0:T(8,128)S(1)}, u32[]{:S(2)}, u32[]{:S(2)}) collective-permute-start(f32[4,48,128]{2,1,0:T(8,128)S(1)} %shard_map.130), channel_id=1, source_target_pairs={{1,2},{2,1},{3,4},{4,3},{5,6},{6,5},{9,10},{10,9},{11,12},{12,11},... | collective-permute-start | bytes 294920 | tf_op jit(solution)/shard_map/ppermute | solution.py:79
  14.9 4.1 %collective-permute-start.2 = (f32[4,48,128]{2,1,0:T(8,128)S(1)}, f32[4,48,128]{2,1,0:T(8,128)S(1)}, u32[]{:S(2)}, u32[]{:S(2)}) collective-permute-start(f32[4,48,128]{2,1,0:T(8,128)S(1)} %shard_map.130), channel_id=1, source_target_pairs={{0,1},{1,0},{2,3},{3,2},{4,5},{5,4},{6,7},{7,6},{8,9},{9,8},{10,11... | collective-permute-start | bytes 294920 | tf_op jit(solution)/shard_map/ppermute | solution.py:79
  19.2 12.2 %collective-permute-start.5 = (f32[3,48,128]{2,1,0:T(8,128)S(1)}, f32[3,48,128]{2,1,0:T(8,128)S(1)}, u32[]{:S(2)}, u32[]{:S(2)}) collective-permute-start(f32[3,48,128]{2,1,0:T(8,128)S(1)} %slice.4), channel_id=1, source_target_pairs={{8,16},{16,8},{9,17},{17,9},{10,18},{18,10},{11,19},{19,11},{12,20... | collective-permute-start | bytes 221192 | tf_op jit(solution)/shard_map/ppermute | solution.py:79
  19.9 11.6 %collective-permute-start.4 = (f32[3,48,128]{2,1,0:T(8,128)S(1)}, f32[3,48,128]{2,1,0:T(8,128)S(1)}, u32[]{:S(2)}, u32[]{:S(2)}) collective-permute-start(f32[3,48,128]{2,1,0:T(8,128)S(1)} %slice.4), channel_id=1, source_target_pairs={{0,8},{8,0},{16,24},{24,16},{1,9},{9,1},{17,25},{25,17},{2,10},{10... | collective-permute-start | bytes 221192 | tf_op jit(solution)/shard_map/ppermute | solution.py:79
  42.5 4.5 %collective-permute-start.7 = (f32[480,128]{1,0:T(8,128)S(1)}, f32[480,128]{1,0:T(8,128)S(1)}, u32[]{:S(2)}, u32[]{:S(2)}) collective-permute-start(f32[480,128]{1,0:T(8,128)S(1)} %get-tuple-element.14.sent), channel_id=1, source_target_pairs={{8,16},{16,8},{9,17},{17,9},{10,18},{18,10},{11,19},{19,11},{12,20... | collective-permute-start | bytes 737288 | tf_op jit(solution)/shard_map/ppermute | solution.py:79
  43.3 10.1 %collective-permute-start.6 = (f32[480,128]{1,0:T(8,128)S(1)}, f32[480,128]{1,0:T(8,128)S(1)}, u32[]{:S(2)}, u32[]{:S(2)}) collective-permute-start(f32[480,128]{1,0:T(8,128)S(1)} %get-tuple-element.14.sent), channel_id=1, source_target_pairs={{0,8},{8,0},{16,24},{24,16},{1,9},{9,1},{17,25},{25,17},{2,10},{10... | collective-permute-start | bytes 737288 | tf_op jit(solution)/shard_map/ppermute | solution.py:79
where the time goes:
time: 71.8 us; the launch traced here: 71.5 us
  Pallas kernels  25.7 us (36%)
  starting transfers between devices  23.4 us (33%)
  waiting for transfers between devices  12 us (17%)
  blocking collectives  7.06 us (10%)
  other arithmetic  1.28 us (2%)
  local copies, waits for them, and re-layouts  1.23 us (2%)
  between operations  0.87 us (1%)
    pallas_call x7, Pallas kernels, call(): pl.pallas_call(body, out_shape=out_shape, scratch_shapes=scratch, compile...  25.7 us
    ppermute x8, starting transfers between devices, exchange(): return (lax.ppermute(values, axis, even), lax.ppermute(values, axis, odd))  19.8 us
    ppermute x8, waiting for transfers between devices, exchange(): return (lax.ppermute(values, axis, even), lax.ppermute(values, axis, odd))  7.39 us
    all_to_all x1, blocking collectives, per_device(): lax.all_to_all(gradient, 'gy', split_axis=0, concat_axis=0, tiled=True)  7.06 us
    all_to_all x1, waiting for transfers between devices, per_device(): lax.all_to_all(outgoing, ('gx', 'gy'), split_axis=0, concat_axis=0, tiled...  4.58 us
    all_to_all x1, starting transfers between devices, per_device(): lax.all_to_all(outgoing, ('gx', 'gy'), split_axis=0, concat_axis=0, tiled...  3.6 us
  transfers between devices with their start and end apart: 9, of which 3 were waited for; matrix products, arithmetic and copies ran while one was open for 1% of the time, Pallas kernels for 6%

commit v1 on v0

v1 whole, which is shorter than its diff:
```python
import functools

import jax
import jax.numpy as jnp
from jax import lax
from jax.experimental import pallas as pl
from jax.experimental.pallas import tpu as pltpu
from jax.sharding import PartitionSpec as P

FX = 4
FZ = 8
FY = 4
CAPS = 4
CAPA = 4
FOOT = 128
RIM = 8
LANES = 128
SLOT_ROWS = 16
OBS_AT = 0
CELL_AT = 8
CTRL_AT = 16
BLOCK_AT = 18
PRANDTL = 0.85
SCALES = (1.0, 1.0 / PRANDTL)
F32 = jnp.float32
BF16 = jnp.bfloat16
COST = pl.CostEstimate(flops=0, transcendentals=0, bytes_accessed=60 * 1024 * 1024)
VMEM_BYTES = 20 * 1024 * 1024


def iota(shape, dim):
    return lax.broadcasted_iota(jnp.int32, shape, dim)


def pieces(values, count=3):
    out = []
    for _ in range(count):
        part = values.astype(BF16)
        out.append(part)
        values = values - part.astype(F32)
    return out


def dot(a, b, dims=((1,), (0,))):
    return lax.dot_general(a, b, (dims, ((), ())), preferred_element_type=F32)


def pick(choice, values, dims=((1,), (0,)), count=3):
    total = None
    for part in pieces(values, count):
        term = dot(choice, part, dims)
        total = term if total is None else total + term
    return total


def spread(choice, values, dims=((1,), (0,)), count=3):
    total = None
    for part in pieces(values, count):
        term = dot(part, choice, dims)
        total = term if total is None else total + term
    return total


def roll(values, amount, axis):
    size = values.shape[axis]
    amount = amount % size
    if amount == 0:
        return values
    return pltpu.roll(values, amount, axis)


def swaps(count):
    even = [(i, i ^ 1) for i in range(count) if (i ^ 1) < count]
    odd = [(i, i + 1 if i % 2 else i - 1) for i in range(1, count) if (i % 2 == 0) or i + 1 < count]
    return even, odd


def exchange(values, axis):
    even, odd = swaps(lax.axis_size(axis))
    return lax.ppermute(values, axis, even), lax.ppermute(values, axis, odd)


def low_high(even, odd, is_odd):
    return jnp.where(is_odd, even, odd), jnp.where(is_odd, odd, even)


def call(body, out_shape, scratch, *args, cost=None):
    return pl.pallas_call(
        body,
        cost_estimate=cost,
        out_shape=out_shape,
        scratch_shapes=scratch,
        compiler_params=pltpu.CompilerParams(vmem_limit_bytes=VMEM_BYTES),
    )(*args)


def slot_choices(owner_row, owners, count):
    records = owner_row.shape[1]
    named = owner_row == iota((owners, records), 0)
    earlier = (iota((records, records), 0) < iota((records, records), 1)).astype(BF16)
    rank = dot(named.astype(BF16), earlier)
    return [(named & (rank == k)).astype(BF16) for k in range(count)]


def records_out_body(n_gx, n_gy, cell, s_owner, obs, block, a_owner, ctrl, foot, out, s_meta, a_meta):
    owners = n_gx * n_gy
    steps = obs.shape[1]
    s_meta[...] = jnp.zeros(s_meta.shape, F32)
    for s in range(2):
        s_meta[OBS_AT + s * steps : OBS_AT + (s + 1) * steps, :] = obs[s]
    s_meta[CELL_AT : CELL_AT + 1, :] = (cell[...] + 1).astype(F32)
    a_meta[...] = jnp.zeros(a_meta.shape, F32)
    a_meta[CTRL_AT : CTRL_AT + 2, :] = ctrl[...]
    a_meta[BLOCK_AT : BLOCK_AT + 1, :] = (block[...] + 1).astype(F32)
    s_all, a_all, f_all = s_meta[...], a_meta[...], foot[...]
    s_choice = slot_choices(s_owner[...], owners, CAPS)
    a_choice = slot_choices(a_owner[...], n_gy, CAPA)
    sens_rows = jnp.zeros((owners, LANES), F32)
    act_rows = jnp.zeros((n_gy, LANES), F32)
    foot_rows = []
    for k in range(CAPS):
        sens_rows = sens_rows + roll(pick(s_choice[k], s_all, ((1,), (1,))), 32 * k, 1)
        act_rows = act_rows + roll(pick(a_choice[k], a_all, ((1,), (1,))), 32 * k, 1)
        foot_rows.append(pick(a_choice[k], f_all))
    gy_of = iota((n_gy, LANES), 0)
    meta = jnp.concatenate(
        [sens_rows[i * n_gy : (i + 1) * n_gy] + act_rows for i in range(n_gx)], axis=0
    )
    meta_gy = iota((owners, LANES), 0) % n_gy
    for t in range(3):
        def moved(values, at):
            if t == 0:
                return jnp.where(at == 0, 0.0, roll(values, 1, 0))
            if t == 2:
                return jnp.where(at == n_gy - 1, 0.0, roll(values, values.shape[0] - 1, 0))
            return values
        for k in range(CAPA):
            rows = moved(foot_rows[k], gy_of)
            for i in range(n_gx):
                out[i * n_gy : (i + 1) * n_gy, 4 * t + k, :] = rows
        out[:, 12 + t, :] = moved(meta, meta_gy)
    out[:, 15, :] = jnp.zeros((owners, LANES), F32)


def strips_body(state, kappa, vel, target, out):
    lane = iota((state.shape[2], LANES), 1)
    fields = [state.at[0], state.at[1], kappa, vel.at[0], vel.at[1], vel.at[2], target.at[0], target.at[1]]
    for tile in range(4):
        packed = jnp.zeros(lane.shape, F32)
        for g in range(2 * FX):
            plane = fields[2 * tile + g // FX][g % FX]
            packed = jnp.where(lane // (2 * RIM) == g, roll(plane, RIM + 2 * RIM * g, 1), packed)
        out[tile] = packed


def rim_body(even, odd, out):
    is_odd = lax.rem(lax.axis_index("gy"), 2) == 1
    for tile in range(out.shape[0]):
        left, right = low_high(even[tile], odd[tile], is_odd)
        lane = iota(left.shape, 1)
        out[tile] = jnp.where(lane % (2 * RIM) < RIM, roll(right, -RIM, 1), roll(left, RIM, 1))


def rim_tile(packed, group):
    lane = iota(packed.shape, 1)
    right = roll(packed, -2 * RIM * group, 1)
    left = roll(packed, LANES - 2 * RIM - 2 * RIM * group, 1)
    return jnp.where(lane < RIM, right, jnp.where(lane >= LANES - RIM, left, 0.0))


def extended(field, main, main_e, main_o, rim, rim_e, rim_o, is_odd, x):
    tile, group = field // 2, (field % 2) * FX + x % FX
    if x // FX == 1:
        centre, halo = main[field, x % FX], rim[tile]
    elif x // FX == 0:
        centre = jnp.where(is_odd, main_e[field, x], main_o[field, x])
        halo = jnp.where(is_odd, rim_e[tile], rim_o[tile])
    else:
        centre = jnp.where(is_odd, main_o[field, x - 2 * FX], main_e[field, x - 2 * FX])
        halo = jnp.where(is_odd, rim_o[tile], rim_e[tile])
    return centre, rim_tile(halo, group)


def records_in_body(
    n_gx, n_gy, height, wide_y, got, source, foot_hot, foot_own, spot_hot, lane_hot, readings, stacked, placing, table
):
    records = n_gy * SLOT_ROWS
    devices = n_gx * n_gy
    blocks_y = wide_y // FY
    row_id = lax.axis_index("gx")
    r_of, r_to = iota((records, records), 0), iota((records, records), 1)
    slot = r_of % SLOT_ROWS
    moves = [
        ((slot < 12) & (slot % 4 == k) & (r_to == r_of - slot + 12 + slot // 4)).astype(BF16)
        for k in range(CAPA)
    ]
    q_of, l_of = iota((FOOT, FOOT), 0), iota((FOOT, FOOT), 1)
    unpack = (l_of == (q_of % 32) * FY + q_of // 32).astype(BF16)
    side = (iota((records, 1), 0) % SLOT_ROWS) // 4
    wide_lane = iota((records, 2 * wide_y), 1)
    for q in range(3):
        row = row_id + (q - 1)
        inside = (row >= 0) & (row < n_gx)
        base = jnp.clip(row, 0, n_gx - 1) * n_gy
        records_in = got[pl.ds(base, n_gy)].reshape(records, LANES)
        meta = jnp.zeros((records, LANES), F32)
        for k in range(CAPA):
            meta = meta + pick(moves[k], roll(records_in, -32 * k, 1))
        meta = jnp.where(inside, meta, 0.0)
        meta_t = meta.T
        block_row = meta_t[BLOCK_AT : BLOCK_AT + 1, :].astype(jnp.int32) - 1
        bz_row = block_row // blocks_y
        foot_t = pick(unpack, records_in, ((1,), (1,)))
        block_col = meta[:, BLOCK_AT : BLOCK_AT + 1].astype(jnp.int32) - 1
        by = block_col % blocks_y
        usable = (block_col >= 0) & (
            (side == 1)
            | ((side == 0) & (by * FY >= wide_y - RIM))
            | ((side == 2) & (by * FY < RIM))
        )
        start = jnp.where(side == 1, by * FY, wide_y + by * FY)
        start = jnp.where(usable, start, -FY)
        for fy in range(FY):
            hot = (wide_lane == start + fy).astype(BF16)
            placing[fy * records : (fy + 1) * records, :] = hot
            if q == 1:
                own_start = jnp.where((side == 1) & usable, start, -FY)
                own = (iota((records, wide_y), 1) == own_start + fy).astype(BF16)
                foot_hot[fy * records : (fy + 1) * records, :] = own
        for s in range(2):
            force = meta_t[CTRL_AT + s : CTRL_AT + s + 1, :]
            for fy in range(FY):
                lanes = slice(fy * records, (fy + 1) * records)
                for x in range(FX):
                    piece = foot_t[fy * 32 + x * FZ : fy * 32 + (x + 1) * FZ, :]
                    scaled = piece * force
                    for bz in range(height // FZ):
                        rows = slice(x * height + bz * FZ, x * height + (bz + 1) * FZ)
                        stacked[rows, lanes] = jnp.where(bz_row == bz, scaled, 0.0)
                        if q == 1 and s == 0:
                            foot_own[rows, lanes] = jnp.where(bz_row == bz, piece, 0.0)
            source[s, q] = spread(placing[...], stacked[...], count=2)
    slots = 3 * CAPS * devices
    for n, t in enumerate((1, 0, 2)):
        rows = got[:, 12 + t, :]
        for k in range(CAPS):
            at = (n * CAPS + k) * devices
            table[at : at + devices, :] = roll(rows, -32 * k, 1)
    for part in range(slots // LANES):
        lanes = slice(part * LANES, (part + 1) * LANES)
        turned = table[lanes, :].T
        cell = turned[CELL_AT : CELL_AT + 1, :].astype(jnp.int32) - 1
        at_y = cell % LANES
        slot_id = iota((1, LANES), 1) + part * LANES
        live = (cell >= 0) & (
            (slot_id < slots // 3)
            | ((slot_id < slots // 3 * 2) & (at_y >= LANES - RIM))
            | ((slot_id >= slots // 3 * 2) & (at_y < RIM))
        )
        cell = jnp.where(live, cell, -1)
        readings[0:8, lanes] = turned[OBS_AT : OBS_AT + 8]
        readings[8:16, lanes] = jnp.broadcast_to((cell + 1).astype(F32), (8, LANES))
        spot, lane = hot_pair(cell, FX * height)
        spot_hot[:, lanes] = spot
        lane_hot[:, lanes] = lane


def hot_pair(cell, cells):
    spot = jnp.where(cell >= 0, cell // LANES, -1)
    at_y = jnp.where(cell >= 0, cell % LANES, -1)
    slots = cell.shape[1]
    return (
        (iota((cells, slots), 0) == spot).astype(BF16),
        (iota((LANES, slots), 0) == at_y).astype(BF16),
    )


def coeffs_body(main, main_e, main_o, rim, rim_e, rim_o, coeffs, start, half_k):
    refs = (main, main_e, main_o, rim, rim_e, rim_o)
    is_odd = lax.rem(lax.axis_index("gx"), 2) == 1
    wide = 3 * FX
    height = half_k.shape[1]
    shape = (height, 2 * LANES)
    z = iota(shape, 0)
    for x in range(wide):
        centre, halo = extended(2, *refs, is_odd, x)
        half_k[x, :, :LANES] = 0.5 * centre
        half_k[x, :, LANES:] = 0.5 * halo
        for s in range(2):
            centre, halo = extended(s, *refs, is_odd, x)
            start[s, x, :, :LANES] = centre
            start[s, x, :, LANES:] = halo
    for x in range(wide):
        k = half_k[x]
        faces = (
            k + half_k[min(x + 1, wide - 1)],
            k + half_k[max(x - 1, 0)],
            k + roll(k, -1, 1),
            k + roll(k, 1, 1),
            k + jnp.where(z == height - 1, 0.0, roll(k, -1, 0)),
            k + jnp.where(z == 0, 0.0, roll(k, 1, 0)),
        )
        total = (faces[0] + faces[1]) + (faces[2] + faces[3]) + (faces[4] + faces[5])
        drift = []
        for axis in range(3):
            centre, halo = extended(3 + axis, *refs, is_odd, x)
            drift.append(0.5 * jnp.concatenate([centre, halo], axis=1))
        for s in range(2):
            coeffs[s, 6, x] = 1.0 - SCALES[s] * total
            for face in range(6):
                value = faces[face] if s == 0 else SCALES[s] * faces[face]
                value = value - drift[face // 2] if face % 2 == 0 else value + drift[face // 2]
                if face == 4:
                    value = jnp.where(z == height - 1, 0.0, value)
                if face == 5:
                    value = jnp.where(z == 0, 0.0, value)
                coeffs[s, face, x] = value


def inside_rows(n_gx, n_gy):
    row_id, col_id = lax.axis_index("gx"), lax.axis_index("gy")
    lane = iota((1, 2 * LANES), 1)
    lanes_in = (
        (lane < LANES)
        | ((lane < LANES + RIM) & (col_id < n_gy - 1))
        | ((lane >= 2 * LANES - RIM) & (col_id > 0))
    ).astype(F32)
    low = jnp.where(row_id > 0, lanes_in, 0.0)
    high = jnp.where(row_id < n_gx - 1, lanes_in, 0.0)
    return lambda x: low if x < FX else (lanes_in if x < 2 * FX else high)


def forward_body(n_gx, n_gy, steps, coeffs, start, rim, source, spot_hot, lane_hot, readings, target, final, sent, residuals, cur):
    height = start.shape[2]
    wide = 3 * FX
    cells = FX * height
    slots = readings.shape[1]
    own = slots // 3
    inside = inside_rows(n_gx, n_gy)
    fields = [start, cur.at[0], cur.at[1], cur.at[0], cur.at[1]]
    residuals[...] = jnp.zeros(residuals.shape, F32)
    live = (readings[8:9, :] > 0.5).astype(F32)
    for n in range(steps):
        before, after = fields[n], fields[n + 1]
        for x in range(n + 1, wide - n - 1):
            row = inside(x)
            for s in range(2):
                c = before[s, x]
                value = coeffs[s, 6, x] * c + source[s, x]
                value = value + coeffs[s, 0, x] * before[s, x + 1]
                value = value + coeffs[s, 1, x] * before[s, x - 1]
                value = value + coeffs[s, 2, x] * roll(c, -1, 1)
                value = value + coeffs[s, 3, x] * roll(c, 1, 1)
                value = value + coeffs[s, 4, x] * roll(c, -1, 0)
                value = value + coeffs[s, 5, x] * roll(c, 1, 0)
                after[s, x] = value * row
        for s in range(2):
            field = after[s, FX : 2 * FX].reshape(cells, 2 * LANES)
            at = s * steps + n
            for half, lanes in enumerate((slice(0, own), slice(own, slots))):
                seen = spread(lane_hot[:, lanes], field[:, half * LANES : (half + 1) * LANES])
                seen = seen * spot_hot[:, lanes].astype(F32)
                value = jnp.sum(seen, axis=0, keepdims=True) - readings[at : at + 1, lanes]
                residuals[at : at + 1, lanes] = value * live[:, lanes]
    residuals[8:16, :] = readings[8:16, :]
    last = fields[steps]
    for s in range(2):
        at = s * steps + steps - 1
        put_main = inject(spot_hot[:, :own], lane_hot[:, :own], residuals[at : at + 1, :own])
        put_rim = inject(spot_hot[:, own:], lane_hot[:, own:], residuals[at : at + 1, own:])
        for p in range(FX):
            rows = slice(p * height, (p + 1) * height)
            got = last[s, FX + p]
            final[s, p] = got[:, :LANES]
            g = s * FX + p
            sent[g * height : (g + 1) * height, :] = got[:, :LANES] - target[s, p] + put_main[rows]
            halo = got[:, LANES:] - rim_tile(rim[3], g) + put_rim[rows]
            at_lane = iota((height, LANES), 1) - 2 * RIM * g
            right = roll(halo, 2 * RIM * g, 1)
            left = roll(halo, 2 * RIM * g + 2 * RIM, 1)
            packed = jnp.where((at_lane >= 0) & (at_lane < RIM), right, 0.0 if g == 0 else packed)
            packed = jnp.where((at_lane >= RIM) & (at_lane < 2 * RIM), left, packed)
    base = 2 * FX * height
    sent[base : base + height, :] = packed
    base = base + height
    for part in range(slots // LANES):
        lanes = slice(part * LANES, (part + 1) * LANES)
        rows = [residuals[s * steps + n : s * steps + n + 1, lanes] for s in range(2) for n in range(steps - 1)]
        for i, values in enumerate(rows + [residuals[8:9, lanes]] * (8 - len(rows))):
            sent[base + 8 * part + i : base + 8 * part + i + 1, :] = values


def inject(spot, lane, values):
    total = None
    for part in pieces(lane.astype(F32) * values, 2):
        term = dot(spot, part, ((1,), (1,)))
        total = term if total is None else total + term
    return total


def own_puts_body(steps, spot_hot, lane_hot, residuals, puts):
    slots = residuals.shape[1]
    own = slots // 3
    _, _, planes, height, _ = puts.shape
    for n in range(steps - 1):
        for s in range(2):
            at = s * steps + n
            for half, lanes in enumerate((slice(0, own), slice(own, slots))):
                put = inject(spot_hot[:, lanes], lane_hot[:, lanes], residuals[at : at + 1, lanes])
                puts[n, s, :, :, half * LANES : (half + 1) * LANES] = put.reshape(planes, height, LANES)


def adjoint_body(n_gx, n_gy, steps, coeffs, sent, sent_e, sent_o, own_puts, foot_hot, foot_own, gradient, second, cur, puts, summed):
    is_odd = lax.rem(lax.axis_index("gx"), 2) == 1
    height = coeffs.shape[3]
    wide = 3 * FX
    cells = FX * height
    base = 2 * FX * height
    table = base + height
    slots = (sent.shape[0] - table) // 8 * LANES
    own = slots // 3
    inside = inside_rows(n_gx, n_gy)
    for q in (1, 0, 2):
        def take(lo, hi):
            if q == 1:
                return sent[lo:hi, :]
            if q == 0:
                return jnp.where(is_odd, sent_e[lo:hi, :], sent_o[lo:hi, :])
            return jnp.where(is_odd, sent_o[lo:hi, :], sent_e[lo:hi, :])
        packed_rim = take(base, base + height)
        for s in range(2):
            for p in range(FX):
                g = s * FX + p
                cur[0, s, q * FX + p, :, :LANES] = take(g * height, (g + 1) * height)
                cur[0, s, q * FX + p, :, LANES:] = rim_tile(packed_rim, g)
        if q == 1:
            continue
        rows = jnp.concatenate(
            [take(table + 8 * i, table + 8 * i + 8) for i in range(slots // LANES)], axis=1
        )
        cell = rows[7:8, :].astype(jnp.int32) - 1
        spot, lane = hot_pair(cell, cells)
        for n in range(steps - 1):
            reach = (n + 1) * height
            part = slice(cells - reach, cells) if q == 0 else slice(0, reach)
            first = (FX - n - 1) if q == 0 else 2 * FX
            for s in range(2):
                at = s * (steps - 1) + n
                for half, lanes in enumerate((slice(0, own), slice(own, slots))):
                    put = inject(spot[part, lanes], lane[:, lanes], rows[at : at + 1, lanes])
                    puts[n, s, first : first + n + 1, :, half * LANES : (half + 1) * LANES] = (
                        put.reshape(n + 1, height, LANES)
                    )
    for s in range(2):
        summed[s * cells : (s + 1) * cells, :] = sent[s * cells : (s + 1) * cells, :]
    for turn in range(steps - 1):
        now, later = turn % 2, (turn + 1) % 2
        n = steps - 2 - turn
        for x in range(turn + 1, wide - turn - 1):
            for s in range(2):
                put = own_puts[n, s, x - FX] if FX <= x < 2 * FX else puts[n, s, x]
                value = adjoint_value(coeffs, cur.at[now], s, x, 0) + put
                value = value * inside(x)
                if turn == steps - 2:
                    second[s, x - steps + 1] = value
                else:
                    cur[later, s, x] = value
                if FX <= x < 2 * FX:
                    at = s * cells + (x - FX) * height
                    summed[at : at + height, :] = summed[at : at + height, :] + value[:, :LANES]
    seen = spread(foot_hot[...], summed[...], ((1,), (1,)), count=2)
    records = foot_own.shape[1] // FY
    out_row = iota((n_gy, records), 0)
    out_from = iota((n_gy, records), 1) // SLOT_ROWS
    for s in range(2):
        total = jnp.sum(seen[s * cells : (s + 1) * cells] * foot_own[...], axis=0, keepdims=True)
        row = total[:, :records]
        for fy in range(1, FY):
            row = row + total[:, fy * records : (fy + 1) * records]
        gradient[:, s, :] = jnp.where(out_row == out_from, row, 0.0)


def adjoint_value(coeffs, field, s, x, shift):
    w = field[s, x - shift]
    value = coeffs[s, 6, x] * w
    value = value + coeffs[s, 1, x + 1] * field[s, x + 1 - shift]
    value = value + coeffs[s, 0, x - 1] * field[s, x - 1 - shift]
    value = value + roll(coeffs[s, 3, x] * w, -1, 1)
    value = value + roll(coeffs[s, 2, x] * w, 1, 1)
    value = value + roll(coeffs[s, 5, x] * w, -1, 0)
    return value + roll(coeffs[s, 4, x] * w, 1, 0)


def last_body(steps, coeffs, second, first):
    for x in range(FX, 2 * FX):
        for s in range(2):
            first[s, x - FX] = adjoint_value(coeffs, second, s, x, steps - 1)[:, :LANES]


def returned_body(got, owner, out):
    n_gy, _, records = got.shape
    base = lax.axis_index("gy") * SLOT_ROWS + CAPA
    choice = slot_choices(owner[...], n_gy, CAPA)
    lane = iota((n_gy, records), 1)
    for s in range(2):
        rows = got[:, s, :]
        total = jnp.zeros(choice[0].shape, F32)
        for k in range(CAPA):
            column = jnp.sum(jnp.where(lane == base + k, rows, 0.0), axis=1, keepdims=True)
            total = total + choice[k].astype(F32) * column
        out[s : s + 1, :] = jnp.sum(total, axis=0, keepdims=True)


def per_device(
    initial_state,
    eddy_diffusivity,
    velocity,
    target,
    sensor_cell,
    sensor_owner,
    observations,
    actuator_block,
    actuator_owner,
    controls,
    footprint,
):
    _, wide_x, height, wide_y = initial_state.shape
    steps = observations.shape[2]
    n_gx, n_gy = lax.axis_size("gx"), lax.axis_size("gy")
    devices = n_gx * n_gy
    sens, acts = sensor_cell.shape[0], actuator_block.shape[0]
    records = n_gy * SLOT_ROWS
    slots = 3 * CAPS * devices
    cells = FX * height
    wide = 3 * FX
    shape = jax.ShapeDtypeStruct
    vmem = pltpu.VMEM
    a_owner_row = actuator_owner.reshape(1, acts)
    main = jnp.concatenate([initial_state, eddy_diffusivity[None], velocity], axis=0)
    outgoing = call(
        functools.partial(records_out_body, n_gx, n_gy),
        shape((devices, SLOT_ROWS, LANES), F32),
        [vmem((LANES, sens), F32), vmem((LANES, acts), F32)],
        sensor_cell.reshape(1, sens),
        sensor_owner.reshape(1, sens),
        observations.transpose(1, 2, 0),
        actuator_block.reshape(1, acts),
        a_owner_row,
        controls.T,
        footprint,
    )
    strips = call(
        strips_body,
        shape((4, height, LANES), F32),
        [],
        initial_state,
        eddy_diffusivity,
        velocity,
        target,
    )
    got = lax.all_to_all(outgoing, ("gx", "gy"), split_axis=0, concat_axis=0, tiled=True)
    main_e, main_o = exchange(main, "gx")
    strips_e, strips_o = exchange(strips, "gy")
    rim = call(rim_body, shape((4, height, LANES), F32), [], strips_e, strips_o)
    rim_e, rim_o = exchange(rim[:3], "gx")
    coeffs, start = call(
        coeffs_body,
        (
            shape((2, 7, wide, height, 2 * LANES), F32),
            shape((2, wide, height, 2 * LANES), F32),
        ),
        [vmem((wide, height, 2 * LANES), F32)],
        main, main_e, main_o, rim, rim_e, rim_o,
    )
    source, foot_hot, foot_own, spot_hot, lane_hot, readings = call(
        functools.partial(records_in_body, n_gx, n_gy, height, wide_y),
        (
            shape((2, 3, cells, 2 * LANES), F32),
            shape((FY * records, LANES), BF16),
            shape((cells, FY * records), F32),
            shape((cells, slots), BF16),
            shape((LANES, slots), BF16),
            shape((16, slots), F32),
        ),
        [
            vmem((cells, FY * records), F32),
            vmem((FY * records, 2 * LANES), BF16),
            vmem((slots, LANES), F32),
        ],
        got,
        cost=COST,
    )
    source = source.reshape(2, wide, height, 2 * LANES)
    sent_rows = 2 * cells + height + slots // LANES * 8
    final, sent, residuals = call(
        functools.partial(forward_body, n_gx, n_gy, steps),
        (
            shape((2, FX, height, LANES), F32),
            shape((sent_rows, LANES), F32),
            shape((16, slots), F32),
        ),
        [vmem((2, 2, wide, height, 2 * LANES), F32)],
        coeffs, start, rim, source, spot_hot, lane_hot, readings, target,
    )
    sent_e, sent_o = exchange(sent, "gx")
    own_puts = call(
        functools.partial(own_puts_body, steps),
        shape((steps - 1, 2, FX, height, 2 * LANES), F32),
        [],
        spot_hot, lane_hot, residuals,
    )
    gradient, second = call(
        functools.partial(adjoint_body, n_gx, n_gy, steps),
        (
            shape((n_gy, 2, records), F32),
            shape((2, wide - 2 * steps + 2, height, 2 * LANES), F32),
        ),
        [
            vmem((2, 2, wide, height, 2 * LANES), F32),
            vmem((steps - 1, 2, wide, height, 2 * LANES), F32),
            vmem((2 * cells, LANES), F32),
        ],
        coeffs, sent, sent_e, sent_o, own_puts, foot_hot, foot_own,
    )
    back = lax.all_to_all(gradient, "gy", split_axis=0, concat_axis=0, tiled=True)
    first = call(
        functools.partial(last_body, steps),
        shape((2, FX, height, LANES), F32),
        [],
        coeffs, second,
    )
    returned = call(returned_body, shape((2, acts), F32), [], back, a_owner_row)
    return (final, first, returned.T)


def solution(mesh):
    in_specs = (
        P(None, "gx", None, "gy"),
        P("gx", None, "gy"),
        P(None, "gx", None, "gy"),
        P(None, "gx", None, "gy"),
        P(("gx", "gy")),
        P(("gx", "gy"), None),
        P(("gx", "gy"), None, None),
        P(("gx", "gy")),
        P(("gx", "gy"), None),
        P(("gx", "gy"), None),
        P(("gx", "gy"), None),
    )
    out_specs = (P(None, "gx", None, "gy"), P(None, "gx", None, "gy"), P(("gx", "gy"), None))
    return jax.shard_map(
        per_device, mesh=mesh, in_specs=in_specs, out_specs=out_specs, check_vma=False
    )
```

time: 71.8 us -> 59.3 us (0.83)
  the two profiles are of different devices: /device:TPU:0 before, /device:TPU:20 now
where the time goes in v1:
time: 59.3 us; the launch traced here: 58.7 us
  starting transfers between devices  23.4 us (39%)
  Pallas kernels  16.2 us (27%)
  waiting for transfers between devices  13.4 us (23%)
  local copies, waits for them, and re-layouts  3.4 us (6%)
  other arithmetic  1.28 us (2%)
  between operations  0.93 us (2%)
    pallas_call x10, Pallas kernels, call(): pl.pallas_call(body, cost_estimate=cost, out_shape=out_shape, scratch_sha...  16.2 us
    ppermute x8, starting transfers between devices, exchange(): return (lax.ppermute(values, axis, even), lax.ppermute(values, axis, odd))  14 us
    ppermute x8, waiting for transfers between devices, exchange(): return (lax.ppermute(values, axis, even), lax.ppermute(values, axis, odd))  12.1 us
    all_to_all x1, starting transfers between devices, per_device(): lax.all_to_all(outgoing, ('gx', 'gy'), split_axis=0, concat_axis=0, tiled...  5.43 us
    all_to_all x1, starting transfers between devices, per_device(): lax.all_to_all(gradient, 'gy', split_axis=0, concat_axis=0, tiled=True)  3.96 us
    unnamed x26, local copies, waits for them, and re-layouts  3.39 us
    all_to_all x1, waiting for transfers between devices, per_device(): lax.all_to_all(outgoing, ('gx', 'gy'), split_axis=0, concat_axis=0, tiled...  1.35 us
    concatenate x1, other arithmetic, per_device(): jnp.concatenate([initial_state, eddy_diffusivity[None], velocity], axis=0)  1.28 us
  transfers between devices with their start and end apart: 10, of which 5 were waited for; matrix products, arithmetic and copies ran while one was open for 0% of the time, Pallas kernels for 10%

profile of v1, /device:TPU:20, one launch (start us, length us, event | category | flops | bytes accessed | tf_op | source)
XLA Modules:
  0.0 58.7 jit_solution(10327530083130575679)
XLA Ops:
  0.6 0.0 copy-start.3
  0.6 0.0 copy-start.2
  0.7 0.0 copy-start.5
  0.7 0.0 copy-start.8
  0.7 0.0 copy-start.10
  0.7 0.0 copy-start.11
  0.7 0.0 copy-start.7
  0.7 0.0 copy-start.12
  0.7 0.0 copy-start.9
  0.7 0.0 copy-start.6
  0.7 0.0 copy-start.4
  0.7 1.3 %pad_maximum_fusion.main = f32[6,4,48,128]{3,2,1,0:T(8,128)S(1)} fusion(f32[3,4,48,128]{3,2,1,0:T(8,128)} %vel.1, f32[1,4,48,128]{3,2,1,0:T(8,128)} %bitcast.10, f32[2,4,48,128]{3,2,1,0:T(8,128)} %state.1), kind=kLoop, calls=%fused_computation | loop fusion | flops 294912 | bytes 1179648 | tf_op jit(solution)/shard_map/concatenate | solution.py:539
  2.0 1.6 %collective-permute-start = (f32[6,4,48,128]{3,2,1,0:T(8,128)S(1)}, f32[6,4,48,128]{3,2,1,0:T(8,128)S(1)}, u32[]{:S(2)}, u32[]{:S(2)}) collective-permute-start(f32[6,4,48,128]{3,2,1,0:T(8,128)S(1)} %pad_maximum_fusion.main), channel_id=1, source_target_pairs={{0,8},{8,0},{16,24},{24,16},{1,9},{9,1},{17,25},{25,17},{2,10},{10... | collective-permute-start | bytes 1769480 | tf_op jit(solution)/shard_map/ppermute | solution.py:80
  3.7 1.9 %collective-permute-start.1 = (f32[6,4,48,128]{3,2,1,0:T(8,128)S(1)}, f32[6,4,48,128]{3,2,1,0:T(8,128)S(1)}, u32[]{:S(2)}, u32[]{:S(2)}) collective-permute-start(f32[6,4,48,128]{3,2,1,0:T(8,128)S(1)} %pad_maximum_fusion.main), channel_id=1, source_target_pairs={{8,16},{16,8},{9,17},{17,9},{10,18},{18,10},{11,19},{19,11},{12,20... | collective-permute-start | bytes 1769480 | tf_op jit(solution)/shard_map/ppermute | solution.py:80
  5.6 0.0 copy-done.8
  5.6 0.0 copy-done.10
  5.6 0.0 copy-done.11
  5.6 0.0 copy-done.7
  5.6 0.0 copy-done.12
  5.6 0.0 copy-done.9
  5.6 0.0 copy-done.6
  5.7 1.5 %shard_map.133 = f32[32,16,128]{2,1,0:T(8,128)} custom-call(s32[1,64]{1,0:T(1,128)S(1)} %bitcast.15, s32[1,64]{1,0:T(1,128)S(1)} %bitcast.16, f32[2,4,64]{2,1,0:T(4,128)S(1)} %bitcast.11, s32[1,16]{1,0:T(1,128)S(1)} %bitcast.17, s32[1,16]{1,0:T(1,128)S(1)} %bitcast.12, f32[2,16]{1,0:T(2,128)S(1)} %bitcast.14, f32[16,128]{1,0:T(8,128)S(1)} %copy-done.6), custom_call_target="tpu_custom_call" | custom-call | tf_op jit(solution)/shard_map/pallas_call | solution.py:88
  7.2 5.4 %all-to-all-start = ((f32[32,16,128]{2,1,0:T(8,128)}), f32[32,16,128]{2,1,0:T(8,128)S(1)}, u32[]{:S(2)}, u32[]{:S(2)}) async-start(f32[32,16,128]{2,1,0:T(8,128)} %shard_map.133), calls=%async_computation | async-start | bytes 524288 | tf_op jit(solution)/shard_map/all_to_all | solution.py:561
  12.6 0.0 copy-done.3
  12.6 0.0 copy-done.2
  12.6 0.0 copy-done.5
  12.7 0.0 copy-done.4
  12.7 0.3 shard_map.130
  12.9 0.2 collective-permute-start.2
  13.1 3.3 %collective-permute-start.3 = (f32[4,48,128]{2,1,0:T(8,128)S(1)}, f32[4,48,128]{2,1,0:T(8,128)S(1)}, u32[]{:S(2)}, u32[]{:S(2)}) collective-permute-start(f32[4,48,128]{2,1,0:T(8,128)S(1)} %shard_map.130), channel_id=1, source_target_pairs={{1,2},{2,1},{3,4},{4,3},{5,6},{6,5},{9,10},{10,9},{11,12},{12,11},... | collective-permute-start | bytes 294920 | tf_op jit(solution)/shard_map/ppermute | solution.py:80
  16.5 0.0 collective-permute-done.2.even
  16.5 5.1 %collective-permute-done.3.odd = f32[4,48,128]{2,1,0:T(8,128)S(1)} collective-permute-done((f32[4,48,128]{2,1,0:T(8,128)S(1)}, f32[4,48,128]{2,1,0:T(8,128)S(1)}, u32[]{:S(2)}, u32[]{:S(2)}) %collective-permute-start.3) | collective-permute-done | bytes 98336 | tf_op jit(solution)/shard_map/ppermute | solution.py:80
  21.5 0.1 shard_map.131.rim
  21.7 1.5 %collective-permute-start.4 = (f32[3,48,128]{2,1,0:T(8,128)S(1)}, f32[3,48,128]{2,1,0:T(8,128)S(1)}, u32[]{:S(2)}, u32[]{:S(2)}) collective-permute-start(f32[3,48,128]{2,1,0:T(8,128)S(1)} %slice.4), channel_id=1, source_target_pairs={{0,8},{8,0},{16,24},{24,16},{1,9},{9,1},{17,25},{25,17},{2,10},{10... | collective-permute-start | bytes 221192 | tf_op jit(solution)/shard_map/ppermute | solution.py:80
  23.1 1.9 %collective-permute-start.5 = (f32[3,48,128]{2,1,0:T(8,128)S(1)}, f32[3,48,128]{2,1,0:T(8,128)S(1)}, u32[]{:S(2)}, u32[]{:S(2)}) collective-permute-start(f32[3,48,128]{2,1,0:T(8,128)S(1)} %slice.4), channel_id=1, source_target_pairs={{8,16},{16,8},{9,17},{17,9},{10,18},{18,10},{11,19},{19,11},{12,20... | collective-permute-start | bytes 221192 | tf_op jit(solution)/shard_map/ppermute | solution.py:80
  25.0 1.4 %all-to-all-done.got = f32[32,16,128]{2,1,0:T(8,128)S(1)} async-done(((f32[32,16,128]{2,1,0:T(8,128)}), f32[32,16,128]{2,1,0:T(8,128)S(1)}, u32[]{:S(2)}, u32[]{:S(2)}) %all-to-all-start) | async-done | bytes 262176 | tf_op jit(solution)/shard_map/all_to_all | solution.py:561
  26.4 2.5 %shard_map.134 = (f32[2,3,192,256]{3,2,1,0:T(8,128)S(1)}, bf16[512,128]{1,0:T(8,128)(2,1)S(1)}, f32[192,512]{1,0:T(8,128)S(1)}, bf16[192,384]{1,0:T(8,128)(2,1)S...) custom-call(f32[32,16,128]{2,1,0:T(8,128)S(1)} %all-to-all-done.got), custom_call_target="tpu_custom_call" | custom-call | bytes 62914560 | tf_op jit(solution)/shard_map/pallas_call | solution.py:88
  28.9 0.0 collective-permute-done.4.rim_e
  28.9 0.5 collective-permute-done.5.rim_o
  29.4 0.0 collective-permute-done.main_e
  29.4 0.0 collective-permute-done.1.main_o
  29.4 1.5 %shard_map.132 = (f32[2,7,12,48,256]{4,3,2,1,0:T(8,128)S(1)}, f32[2,12,48,256]{3,2,1,0:T(8,128)S(1)}) custom-call(f32[6,4,48,128]{3,2,1,0:T(8,128)S(1)} %pad_maximum_fusion.main, f32[6,4,48,128]{3,2,1,0:T(8,128)S(1)} %collective-permute-done.main_e, f32[6,4,48,128]{3,2,1,0:T(8,128)S(1)} %collective-permute-done.1.main_o, f32[4,48,128]{2,1,0:T(8,128)S(1)} %shard_map.131.rim, ...), custom_call_target="tpu_custom_call" | custom-call | tf_op jit(solution)/shard_map/pallas_call | solution.py:88
  30.9 0.0 copy-start
  30.9 4.5 %shard_map.135 = (f32[2,4,48,128]{3,2,1,0:T(8,128)}, f32[456,128]{1,0:T(8,128)S(1)}, f32[16,384]{1,0:T(8,128)S(1)}) custom-call(f32[2,7,12,48,256]{4,3,2,1,0:T(8,128)S(1)} %get-tuple-element.16.coeffs, f32[2,12,48,256]{3,2,1,0:T(8,128)S(1)} %get-tuple-element.17.start, f32[4,48,128]{2,1,0:T(8,128)S(1)} %shard_map.131.rim, f32[2,12,48,256]{3,2,1,0:T(8,128)S(1)} %bitcast.9, ...), custom_call_target="tpu_custom_call" | custom-call | tf_op jit(solution)/shard_map/pallas_call | solution.py:88
  35.5 1.1 %collective-permute-start.6 = (f32[456,128]{1,0:T(8,128)S(1)}, f32[456,128]{1,0:T(8,128)S(1)}, u32[]{:S(2)}, u32[]{:S(2)}) collective-permute-start(f32[456,128]{1,0:T(8,128)S(1)} %get-tuple-element.23.sent), channel_id=1, source_target_pairs={{0,8},{8,0},{16,24},{24,16},{1,9},{9,1},{17,25},{25,17},{2,10},{10... | collective-permute-start | bytes 700424 | tf_op jit(solution)/shard_map/ppermute | solution.py:80
  36.6 2.4 %collective-permute-start.7 = (f32[456,128]{1,0:T(8,128)S(1)}, f32[456,128]{1,0:T(8,128)S(1)}, u32[]{:S(2)}, u32[]{:S(2)}) collective-permute-start(f32[456,128]{1,0:T(8,128)S(1)} %get-tuple-element.23.sent), channel_id=1, source_target_pairs={{8,16},{16,8},{9,17},{17,9},{10,18},{18,10},{11,19},{19,11},{12,20... | collective-permute-start | bytes 700424 | tf_op jit(solution)/shard_map/ppermute | solution.py:80
  39.0 0.7 %shard_map.136.own_puts = f32[3,2,4,48,256]{4,3,2,1,0:T(8,128)S(1)} custom-call(bf16[192,384]{1,0:T(8,128)(2,1)S(1)} %get-tuple-element.19.spot_hot, bf16[128,384]{1,0:T(8,128)(2,1)S(1)} %get-tuple-element.20.lane_hot, f32[16,384]{1,0:T(8,128)S(1)} %get-tuple-element.24.residuals), custom_call_target="tpu_custom_call" | custom-call | tf_op jit(solution)/shard_map/pallas_call | solution.py:88
  39.7 3.3 %collective-permute-done.6.sent_e = f32[456,128]{1,0:T(8,128)S(1)} collective-permute-done((f32[456,128]{1,0:T(8,128)S(1)}, f32[456,128]{1,0:T(8,128)S(1)}, u32[]{:S(2)}, u32[]{:S(2)}) %collective-permute-start.6) | collective-permute-done | bytes 233504 | tf_op jit(solution)/shard_map/ppermute | solution.py:80
  43.0 3.3 %collective-permute-done.7.sent_o = f32[456,128]{1,0:T(8,128)S(1)} collective-permute-done((f32[456,128]{1,0:T(8,128)S(1)}, f32[456,128]{1,0:T(8,128)S(1)}, u32[]{:S(2)}, u32[]{:S(2)}) %collective-permute-start.7) | collective-permute-done | bytes 233504 | tf_op jit(solution)/shard_map/ppermute | solution.py:80
  46.3 0.0 copy-done
  46.3 3.4 %shard_map.137 = (f32[8,2,128]{2,1,0:T(2,128)}, f32[2,6,48,256]{3,2,1,0:T(8,128)S(1)}) custom-call(f32[2,7,12,48,256]{4,3,2,1,0:T(8,128)S(1)} %get-tuple-element.16.coeffs, f32[456,128]{1,0:T(8,128)S(1)} %get-tuple-element.23.sent, f32[456,128]{1,0:T(8,128)S(1)} %collective-permute-done.6.sent_e, f32[456,128]{1,0:T(8,128)S(1)} %collective-permute-done.7.sent_o, ...), custom_call_target="tpu_custom_call" | custom-call | tf_op jit(solution)/shard_map/pallas_call | solution.py:88
  49.7 4.0 %all-to-all-start.1 = ((f32[8,2,128]{2,1,0:T(2,128)}), f32[8,2,128]{2,1,0:T(2,128)S(1)}, u32[]{:S(2)}, u32[]{:S(2)}) async-start(f32[8,2,128]{2,1,0:T(2,128)} %get-tuple-element.28), calls=%async_computation.1 | async-start | bytes 16384 | tf_op jit(solution)/shard_map/all_to_all | solution.py:625
  53.7 0.0 copy-start.1
  53.7 3.3 %copy-done.1 = f32[2,7,12,48,256]{4,3,2,1,0:T(8,128)S(1)} copy-done((f32[2,7,12,48,256]{4,3,2,1,0:T(8,128)S(1)}, f32[2,7,12,48,256]{4,3,2,1,0:T(8,128)}, u32[]{:S(2)}) %copy-start.1) | copy-done | bytes 8257560
  57.0 1.0 %shard_map.138 = f32[2,4,48,128]{3,2,1,0:T(8,128)} custom-call(f32[2,7,12,48,256]{4,3,2,1,0:T(8,128)S(1)} %copy-done.1, f32[2,6,48,256]{3,2,1,0:T(8,128)S(1)} %get-tuple-element.27.second), custom_call_target="tpu_custom_call" | custom-call | tf_op jit(solution)/shard_map/pallas_call | solution.py:88
  58.0 0.0 all-to-all-done.1.got
  58.0 0.7 %shard_map.139 = f32[2,16]{1,0:T(2,128)} custom-call(f32[8,2,128]{2,1,0:T(2,128)S(1)} %all-to-all-done.1.got, s32[1,16]{1,0:T(1,128)S(1)} %bitcast.13), custom_call_target="tpu_custom_call" | custom-call | tf_op jit(solution)/shard_map/pallas_call | solution.py:88
  (1 shorter events, 0.0 us)
Async XLA Ops:
  0.6 12.0 %copy-start.3 = (f32[2,4,48,128]{3,2,1,0:T(8,128)S(1)}, f32[2,4,48,128]{3,2,1,0:T(8,128)}, u32[]{:S(2)}) copy-start(f32[2,4,48,128]{3,2,1,0:T(8,128)} %state.1) | copy-start | bytes 589828
  0.6 12.0 %copy-start.2 = (f32[3,4,48,128]{3,2,1,0:T(8,128)S(1)}, f32[3,4,48,128]{3,2,1,0:T(8,128)}, u32[]{:S(2)}) copy-start(f32[3,4,48,128]{3,2,1,0:T(8,128)} %vel.1) | copy-start | bytes 884740
  0.7 12.0 %copy-start.5 = (f32[4,48,128]{2,1,0:T(8,128)S(1)}, f32[4,48,128]{2,1,0:T(8,128)}, u32[]{:S(2)}) copy-start(f32[4,48,128]{2,1,0:T(8,128)} %kappa.1) | copy-start | bytes 294916
  0.7 4.9 %copy-start.8 = (s32[16,1]{0,1:T(1,128)S(1)}, s32[16,1]{0,1:T(1,128)}, u32[]{:S(2)}) copy-start(s32[16,1]{0,1:T(1,128)} %param.19) | copy-start | bytes 196
  0.7 4.9 %copy-start.10 = (s32[64]{0:T(128)S(1)}, s32[64]{0:T(128)}, u32[]{:S(2)}) copy-start(s32[64]{0:T(128)} %param.15) | copy-start | bytes 772
  0.7 4.9 %copy-start.11 = (s32[64,1]{0,1:T(1,128)S(1)}, s32[64,1]{0,1:T(1,128)}, u32[]{:S(2)}) copy-start(s32[64,1]{0,1:T(1,128)} %param.16) | copy-start | bytes 772
  0.7 4.9 %copy-start.7 = (f32[64,2,4]{0,2,1:T(4,128)S(1)}, f32[64,2,4]{0,2,1:T(4,128)}, u32[]{:S(2)}) copy-start(f32[64,2,4]{0,2,1:T(4,128)} %param.17) | copy-start | bytes 6148
  0.7 4.9 %copy-start.12 = (s32[16]{0:T(128)S(1)}, s32[16]{0:T(128)}, u32[]{:S(2)}) copy-start(s32[16]{0:T(128)} %param.18) | copy-start | bytes 196
  0.7 4.9 %copy-start.9 = (f32[16,2]{0,1:T(2,128)S(1)}, f32[16,2]{0,1:T(2,128)}, u32[]{:S(2)}) copy-start(f32[16,2]{0,1:T(2,128)} %param.20) | copy-start | bytes 388
  0.7 4.9 %copy-start.6 = (f32[16,128]{1,0:T(8,128)S(1)}, f32[16,128]{1,0:T(8,128)}, u32[]{:S(2)}) copy-start(f32[16,128]{1,0:T(8,128)} %foot.1) | copy-start | bytes 24580
  0.7 11.9 %copy-start.4 = (f32[2,4,48,128]{3,2,1,0:T(8,128)S(1)}, f32[2,4,48,128]{3,2,1,0:T(8,128)}, u32[]{:S(2)}) copy-start(f32[2,4,48,128]{3,2,1,0:T(8,128)} %target.3) | copy-start | bytes 589828
  2.0 27.3 %collective-permute-start = (f32[6,4,48,128]{3,2,1,0:T(8,128)S(1)}, f32[6,4,48,128]{3,2,1,0:T(8,128)S(1)}, u32[]{:S(2)}, u32[]{:S(2)}) collective-permute-start(f32[6,4,48,128]{3,2,1,0:T(8,128)S(1)} %pad_maximum_fusion.main), channel_id=1, source_target_pairs={{0,8},{8,0},{16,24},{24,16},{1,9},{9,1},{17,25},{25,17},{2,10},{10... | collective-permute-start | bytes 1769480 | tf_op jit(solution)/shard_map/ppermute | solution.py:80
  3.7 25.7 %collective-permute-start.1 = (f32[6,4,48,128]{3,2,1,0:T(8,128)S(1)}, f32[6,4,48,128]{3,2,1,0:T(8,128)S(1)}, u32[]{:S(2)}, u32[]{:S(2)}) collective-permute-start(f32[6,4,48,128]{3,2,1,0:T(8,128)S(1)} %pad_maximum_fusion.main), channel_id=1, source_target_pairs={{8,16},{16,8},{9,17},{17,9},{10,18},{18,10},{11,19},{19,11},{12,20... | collective-permute-start | bytes 1769480 | tf_op jit(solution)/shard_map/ppermute | solution.py:80
  7.2 19.2 %all-to-all-start = ((f32[32,16,128]{2,1,0:T(8,128)}), f32[32,16,128]{2,1,0:T(8,128)S(1)}, u32[]{:S(2)}, u32[]{:S(2)}) async-start(f32[32,16,128]{2,1,0:T(8,128)} %shard_map.133), calls=%async_computation | async-start | bytes 524288 | tf_op jit(solution)/shard_map/all_to_all | solution.py:561
  12.9 3.5 %collective-permute-start.2 = (f32[4,48,128]{2,1,0:T(8,128)S(1)}, f32[4,48,128]{2,1,0:T(8,128)S(1)}, u32[]{:S(2)}, u32[]{:S(2)}) collective-permute-start(f32[4,48,128]{2,1,0:T(8,128)S(1)} %shard_map.130), channel_id=1, source_target_pairs={{0,1},{1,0},{2,3},{3,2},{4,5},{5,4},{6,7},{7,6},{8,9},{9,8},{10,11... | collective-permute-start | bytes 294920 | tf_op jit(solution)/shard_map/ppermute | solution.py:80
  13.1 8.4 %collective-permute-start.3 = (f32[4,48,128]{2,1,0:T(8,128)S(1)}, f32[4,48,128]{2,1,0:T(8,128)S(1)}, u32[]{:S(2)}, u32[]{:S(2)}) collective-permute-start(f32[4,48,128]{2,1,0:T(8,128)S(1)} %shard_map.130), channel_id=1, source_target_pairs={{1,2},{2,1},{3,4},{4,3},{5,6},{6,5},{9,10},{10,9},{11,12},{12,11},... | collective-permute-start | bytes 294920 | tf_op jit(solution)/shard_map/ppermute | solution.py:80
  21.7 7.2 %collective-permute-start.4 = (f32[3,48,128]{2,1,0:T(8,128)S(1)}, f32[3,48,128]{2,1,0:T(8,128)S(1)}, u32[]{:S(2)}, u32[]{:S(2)}) collective-permute-start(f32[3,48,128]{2,1,0:T(8,128)S(1)} %slice.4), channel_id=1, source_target_pairs={{0,8},{8,0},{16,24},{24,16},{1,9},{9,1},{17,25},{25,17},{2,10},{10... | collective-permute-start | bytes 221192 | tf_op jit(solution)/shard_map/ppermute | solution.py:80
  23.1 6.2 %collective-permute-start.5 = (f32[3,48,128]{2,1,0:T(8,128)S(1)}, f32[3,48,128]{2,1,0:T(8,128)S(1)}, u32[]{:S(2)}, u32[]{:S(2)}) collective-permute-start(f32[3,48,128]{2,1,0:T(8,128)S(1)} %slice.4), channel_id=1, source_target_pairs={{8,16},{16,8},{9,17},{17,9},{10,18},{18,10},{11,19},{19,11},{12,20... | collective-permute-start | bytes 221192 | tf_op jit(solution)/shard_map/ppermute | solution.py:80
  30.9 15.4 %copy-start = (f32[2,7,12,48,256]{4,3,2,1,0:T(8,128)}, f32[2,7,12,48,256]{4,3,2,1,0:T(8,128)S(1)}, u32[]{:S(2)}) copy-start(f32[2,7,12,48,256]{4,3,2,1,0:T(8,128)S(1)} %get-tuple-element.16.coeffs) | copy-start | bytes 24772612
  35.5 7.6 %collective-permute-start.6 = (f32[456,128]{1,0:T(8,128)S(1)}, f32[456,128]{1,0:T(8,128)S(1)}, u32[]{:S(2)}, u32[]{:S(2)}) collective-permute-start(f32[456,128]{1,0:T(8,128)S(1)} %get-tuple-element.23.sent), channel_id=1, source_target_pairs={{0,8},{8,0},{16,24},{24,16},{1,9},{9,1},{17,25},{25,17},{2,10},{10... | collective-permute-start | bytes 700424 | tf_op jit(solution)/shard_map/ppermute | solution.py:80
  36.6 9.7 %collective-permute-start.7 = (f32[456,128]{1,0:T(8,128)S(1)}, f32[456,128]{1,0:T(8,128)S(1)}, u32[]{:S(2)}, u32[]{:S(2)}) collective-permute-start(f32[456,128]{1,0:T(8,128)S(1)} %get-tuple-element.23.sent), channel_id=1, source_target_pairs={{8,16},{16,8},{9,17},{17,9},{10,18},{18,10},{11,19},{19,11},{12,20... | collective-permute-start | bytes 700424 | tf_op jit(solution)/shard_map/ppermute | solution.py:80
  49.7 8.3 %all-to-all-start.1 = ((f32[8,2,128]{2,1,0:T(2,128)}), f32[8,2,128]{2,1,0:T(2,128)S(1)}, u32[]{:S(2)}, u32[]{:S(2)}) async-start(f32[8,2,128]{2,1,0:T(2,128)} %get-tuple-element.28), calls=%async_computation.1 | async-start | bytes 16384 | tf_op jit(solution)/shard_map/all_to_all | solution.py:625
  53.7 3.3 %copy-start.1 = (f32[2,7,12,48,256]{4,3,2,1,0:T(8,128)S(1)}, f32[2,7,12,48,256]{4,3,2,1,0:T(8,128)}, u32[]{:S(2)}) copy-start(f32[2,7,12,48,256]{4,3,2,1,0:T(8,128)} %copy-done) | copy-start | bytes 24772612

commit v2 on v1

v2 whole, which is shorter than its diff:
```python
import functools

import jax
import jax.numpy as jnp
from jax import lax
from jax.experimental import pallas as pl
from jax.experimental.pallas import tpu as pltpu
from jax.sharding import PartitionSpec as P

FX = 4
FZ = 8
FY = 4
CAPS = 4
CAPA = 4
FOOT = 128
RIM = 8
LANES = 128
SLOT_ROWS = 16
OBS_AT = 0
CELL_AT = 8
PITCH = 10
CTRL_AT = 16
BLOCK_AT = 18
PRANDTL = 0.85
SCALES = (1.0, 1.0 / PRANDTL)
F32 = jnp.float32
BF16 = jnp.bfloat16
VMEM_BYTES = 20 * 1024 * 1024


def iota(shape, dim):
    return lax.broadcasted_iota(jnp.int32, shape, dim)


def pieces(values, count=3):
    out = []
    for _ in range(count):
        part = values.astype(BF16)
        out.append(part)
        values = values - part.astype(F32)
    return out


def dot(a, b, dims=((1,), (0,))):
    return lax.dot_general(a, b, (dims, ((), ())), preferred_element_type=F32)


def pick(choice, values, dims=((1,), (0,)), count=3):
    total = None
    for part in pieces(values, count):
        term = dot(choice, part, dims)
        total = term if total is None else total + term
    return total


def spread(choice, values, dims=((1,), (0,)), count=3):
    total = None
    for part in pieces(values, count):
        term = dot(part, choice, dims)
        total = term if total is None else total + term
    return total


def roll(values, amount, axis):
    size = values.shape[axis]
    amount = amount % size
    if amount == 0:
        return values
    return pltpu.roll(values, amount, axis)


def swaps(count):
    even = [(i, i ^ 1) for i in range(count) if (i ^ 1) < count]
    odd = [(i, i + 1 if i % 2 else i - 1) for i in range(1, count) if (i % 2 == 0) or i + 1 < count]
    return even, odd


def exchange(values, axis):
    even, odd = swaps(lax.axis_size(axis))
    return lax.ppermute(values, axis, even), lax.ppermute(values, axis, odd)


def low_high(even, odd, is_odd):
    return jnp.where(is_odd, even, odd), jnp.where(is_odd, odd, even)


def call(body, out_shape, scratch, *args, us=0.2):
    return pl.pallas_call(
        body,
        cost_estimate=pl.CostEstimate(
            flops=0, transcendentals=0, bytes_accessed=int(us * 3.6e6)
        ),
        out_shape=out_shape,
        scratch_shapes=scratch,
        compiler_params=pltpu.CompilerParams(vmem_limit_bytes=VMEM_BYTES),
    )(*args)


def slot_choices(owner_row, owners, count):
    records = owner_row.shape[1]
    named = owner_row == iota((owners, records), 0)
    earlier = (iota((records, records), 0) < iota((records, records), 1)).astype(BF16)
    rank = dot(named.astype(BF16), earlier)
    return [(named & (rank == k)).astype(BF16) for k in range(count)]


class row_slots:
    def __init__(self, ref, base, rows):
        self.ref, self.base, self.rows = ref, base, rows
        self.shape = ((ref.shape[0] - base) // rows, rows, ref.shape[1])

    def __getitem__(self, at):
        return self.ref[self.base + at * self.rows : self.base + (at + 1) * self.rows, :]

    def __setitem__(self, at, value):
        self.ref[self.base + at * self.rows : self.base + (at + 1) * self.rows, :] = value


class split_planes:
    def __init__(self, inner, outer):
        self.inner, self.outer = inner, outer

    def place(self, x):
        if FX - 1 <= x <= 2 * FX:
            return self.inner, x - FX + 1
        return self.outer, x if x < FX else x - FX - 2

    def __getitem__(self, at):
        ref, x = self.place(at[2])
        return ref[at[0], at[1], x]

    def __setitem__(self, at, value):
        ref, x = self.place(at[2])
        ref[at[0], at[1], x] = value


def without_bit(slot, bit):
    return (slot >> (bit + 1) << bit) | (slot & ((1 << bit) - 1))


def bit_of(axis, bit):
    return lax.rem(lax.axis_index(axis) >> bit, 2)


def split_slots(slots, axis, bit, send, keep):
    mine = bit_of(axis, bit) == 1
    for d, low in enumerate(slots):
        if d >> bit & 1:
            continue
        high = slots[d | 1 << bit]
        at = without_bit(d, bit)
        send[at] = jnp.where(mine, low, high)
        keep[at] = jnp.where(mine, high, low)


def join_slots(keep, got, axis, bit):
    mine = bit_of(axis, bit)
    return [
        jnp.where(mine == (d >> bit & 1), keep[without_bit(d, bit)], got[without_bit(d, bit)])
        for d in range(2 * keep.shape[0])
    ]


def route_body(axis, bit, keep, got, next_send, next_keep):
    got = row_slots(got, got.shape[0] - keep.shape[0] * keep.shape[1], keep.shape[1])
    next_send = row_slots(next_send, 0, keep.shape[1])
    split_slots(join_slots(keep, got, axis, bit), axis, bit + 1, next_send, next_keep)


def swap(values, axis, bit):
    count = lax.axis_size(axis)
    return lax.ppermute(values, axis, [(i, i ^ 1 << bit) for i in range(count)])


def route(keep, got, axis, after=None):
    bits = lax.axis_size(axis).bit_length() - 1
    for bit in range(bits - 1):
        send = jax.ShapeDtypeStruct((keep.shape[0] * keep.shape[1], LANES), F32)
        half = jax.ShapeDtypeStruct(keep.shape, F32)
        send, keep = call(functools.partial(route_body, axis, bit), (send, half), [], keep, got)
        if after is not None:
            send, after = lax.optimization_barrier((send, after))
        got = swap(send, axis, bit + 1)
    return keep, got


def records_out_body(n_gx, n_gy, cell, s_owner, obs, block, a_owner, ctrl, foot, send, keep, s_meta, a_meta, out):
    owners = n_gx * n_gy
    steps = obs.shape[1]
    s_meta[...] = jnp.zeros(s_meta.shape, F32)
    for s in range(2):
        s_meta[OBS_AT + s * steps : OBS_AT + (s + 1) * steps, :] = obs[s]
    s_meta[CELL_AT : CELL_AT + 1, :] = (cell[...] + 1).astype(F32)
    a_meta[...] = jnp.zeros(a_meta.shape, F32)
    a_meta[CTRL_AT : CTRL_AT + 2, :] = ctrl[...]
    a_meta[BLOCK_AT : BLOCK_AT + 1, :] = (block[...] + 1).astype(F32)
    s_all, a_all, f_all = s_meta[...], a_meta[...], foot[...]
    s_choice = slot_choices(s_owner[...], owners, CAPS)
    a_choice = slot_choices(a_owner[...], n_gy, CAPA)
    act_rows = jnp.zeros((n_gy, LANES), F32)
    sens_rows, foot_rows = [], []
    for k in range(CAPS):
        sens_rows.append(pick(s_choice[k], s_all, ((1,), (1,))))
        act_rows = act_rows + roll(pick(a_choice[k], a_all, ((1,), (1,))), 32 * k, 1)
        foot_rows.append(pick(a_choice[k], f_all))

    def moved(values, t):
        at = iota(values.shape, 0) % n_gy
        if t == 0:
            return jnp.where(at == 0, 0.0, roll(values, 1, 0))
        if t == 2:
            return jnp.where(at == n_gy - 1, 0.0, roll(values, values.shape[0] - 1, 0))
        return values

    packed = jnp.zeros((owners, LANES), F32)
    for t in range(3):
        for k in range(CAPS):
            out[:, 4 * t + k, :] = moved(foot_rows[k], t)
            packed = packed + roll(moved(sens_rows[k], t), PITCH * (CAPS * t + k), 1)
        out[:, 12 + t, :] = moved(act_rows, t)
    out[:, 15:, :] = jnp.zeros((n_gy, out.shape[1] - 15, LANES), F32)
    for d in range(n_gy):
        for i in range(n_gx):
            out[d, SLOT_ROWS + i : SLOT_ROWS + i + 1, :] = packed[i * n_gy + d : i * n_gy + d + 1]
    split_slots([out[d] for d in range(n_gy)], "gy", 0, row_slots(send, 0, out.shape[1]), keep)


def strips_body(state, kappa, vel, target, out):
    lane = iota((state.shape[2], LANES), 1)
    fields = [state.at[0], state.at[1], kappa, vel.at[0], vel.at[1], vel.at[2], target.at[0], target.at[1]]
    for tile in range(4):
        packed = jnp.zeros(lane.shape, F32)
        for g in range(2 * FX):
            plane = fields[2 * tile + g // FX][g % FX]
            packed = jnp.where(lane // (2 * RIM) == g, roll(plane, RIM + 2 * RIM * g, 1), packed)
        out[tile * lane.shape[0] : (tile + 1) * lane.shape[0], :] = packed


def rim_body(n_gx, even, odd, keep, got, sent, rim_target, sens_keep):
    is_odd = lax.rem(lax.axis_index("gy"), 2) == 1
    height = rim_target.shape[0]
    tiles = odd.shape[0] // height
    for tile in range(tiles):
        rows = slice(tile * height, (tile + 1) * height)
        left, right = low_high(even[rows, :], odd[rows, :], is_odd)
        lane = iota(left.shape, 1)
        value = jnp.where(lane % (2 * RIM) < RIM, roll(right, -RIM, 1), roll(left, RIM, 1))
        if tile == tiles - 1:
            rim_target[...] = value
        else:
            sent[rows, :] = value
    base = (tiles - 1) * height
    n_gy = 2 * keep.shape[0]
    rows = keep.shape[1]
    got = row_slots(got, got.shape[0] - keep.shape[0] * rows, rows)
    slots = join_slots(keep, got, "gy", n_gy.bit_length() - 2)
    for d in range(n_gy):
        sent[base + d * SLOT_ROWS : base + (d + 1) * SLOT_ROWS, :] = slots[d][:SLOT_ROWS]
    base = base + n_gy * SLOT_ROWS
    rows = [
        jnp.concatenate([slots[d][SLOT_ROWS + i : SLOT_ROWS + i + 1] for d in range(n_gy)], axis=0)
        for i in range(n_gx)
    ]
    split_slots(rows, "gx", 0, row_slots(sent, base, n_gy), sens_keep)


def rim_tile(packed, group):
    lane = iota(packed.shape, 1)
    right = roll(packed, -2 * RIM * group, 1)
    left = roll(packed, LANES - 2 * RIM - 2 * RIM * group, 1)
    return jnp.where(lane < RIM, right, jnp.where(lane >= LANES - RIM, left, 0.0))


def extended(field, main, main_e, main_o, rim, rim_e, rim_o, is_odd, x):
    height = main.shape[2]
    at, group = pl.ds(field // 2 * height, height), (field % 2) * FX + x % FX
    if x // FX == 1:
        centre, halo = main[field, x % FX], rim[at]
    elif x // FX == 0:
        centre = jnp.where(is_odd, main_e[field, x], main_o[field, x])
        halo = jnp.where(is_odd, rim_e[at], rim_o[at])
    else:
        centre = jnp.where(is_odd, main_o[field, x - 2 * FX], main_e[field, x - 2 * FX])
        halo = jnp.where(is_odd, rim_o[at], rim_e[at])
    return centre, rim_tile(halo, group)


def source_tile(n_gy, height, wide_y, records_in, planes, out, stacked, placing):
    records = n_gy * SLOT_ROWS
    blocks_y = wide_y // FY
    r_of, r_to = iota((records, records), 0), iota((records, records), 1)
    slot = r_of % SLOT_ROWS
    meta = jnp.zeros((records, LANES), F32)
    for k in range(CAPA):
        move = (slot < 12) & (slot % 4 == k) & (r_to == r_of - slot + 12 + slot // 4)
        meta = meta + pick(move.astype(BF16), roll(records_in, -32 * k, 1))
    q_of, l_of = iota((FOOT, FOOT), 0), iota((FOOT, FOOT), 1)
    unpack = (l_of == (q_of % 32) * FY + q_of // 32).astype(BF16)
    side = (iota((records, 1), 0) % SLOT_ROWS) // 4
    meta_t = meta.T
    block_row = meta_t[BLOCK_AT : BLOCK_AT + 1, :].astype(jnp.int32) - 1
    bz_row = block_row // blocks_y
    foot_t = pick(unpack, records_in, ((1,), (1,)), 2)
    block_col = meta[:, BLOCK_AT : BLOCK_AT + 1].astype(jnp.int32) - 1
    by = block_col % blocks_y
    usable = (block_col >= 0) & (
        (side == 1)
        | ((side == 0) & (by * FY >= wide_y - RIM))
        | ((side == 2) & (by * FY < RIM))
    )
    start = jnp.where(side == 1, by * FY, wide_y + by * FY)
    start = jnp.where(usable, start, -FY)
    wide_lane = iota((records, 2 * wide_y), 1)
    for fy in range(FY):
        placing[fy * records : (fy + 1) * records, :] = (wide_lane == start + fy).astype(BF16)
    rows_out = len(planes) * height
    for s in range(2):
        force = meta_t[CTRL_AT + s : CTRL_AT + s + 1, :]
        for fy in range(FY):
            lanes = slice(fy * records, (fy + 1) * records)
            for i, x in enumerate(planes):
                scaled = foot_t[fy * 32 + x * FZ : fy * 32 + (x + 1) * FZ, :] * force
                for bz in range(height // FZ):
                    at = i * height + bz * FZ
                    stacked[at : at + FZ, lanes] = jnp.where(bz_row == bz, scaled, 0.0)
        value = spread(placing[...], stacked[:rows_out, :], count=2)
        for i in range(len(planes)):
            out[s, i] = value[i * height : (i + 1) * height]
    return meta, meta_t


def own_source_body(n_gy, height, wide_y, got, source, foot_hot, foot_own, stacked, placing):
    records = n_gy * SLOT_ROWS
    blocks_y = wide_y // FY
    base = 3 * height
    records_in = got[base : base + records, :]
    meta, meta_t = source_tile(
        n_gy, height, wide_y, records_in, range(FX), source, stacked, placing
    )
    held = n_gy * CAPA
    r_of, r_to = iota((held, records), 0), iota((held, records), 1)
    own = (r_to == r_of // CAPA * SLOT_ROWS + CAPA + r_of % CAPA).astype(BF16)
    block_row = spread(own, meta_t[CTRL_AT : CTRL_AT + 8], ((1,), (1,)))[BLOCK_AT - CTRL_AT :]
    bz_row = (block_row[:1].astype(jnp.int32) - 1) // blocks_y
    block_col = pick(own, meta)[:, BLOCK_AT : BLOCK_AT + 1].astype(jnp.int32) - 1
    start = jnp.where(block_col >= 0, block_col % blocks_y * FY, -FY)
    q_of, l_of = iota((FOOT, FOOT), 0), iota((FOOT, FOOT), 1)
    unpack = (l_of == (q_of % 32) * FY + q_of // 32).astype(BF16)
    foot_t = pick(unpack, pick(own, records_in), ((1,), (1,)))
    lane = iota((held, wide_y), 1)
    for fy in range(FY):
        lanes = slice(fy * held, (fy + 1) * held)
        foot_hot[lanes, :] = (lane == start + fy).astype(BF16)
        for x in range(FX):
            piece = foot_t[fy * 32 + x * FZ : fy * 32 + (x + 1) * FZ, :]
            for bz in range(height // FZ):
                at = x * height + bz * FZ
                foot_own[at : at + FZ, lanes] = jnp.where(bz_row == bz, piece, 0.0)


def side_source_body(n_gy, height, wide_y, got_e, got_o, source, stacked, placing):
    is_odd = lax.rem(lax.axis_index("gx"), 2) == 1
    rows = slice(3 * height, 3 * height + n_gy * SLOT_ROWS)
    low, high = low_high(got_e[rows, :], got_o[rows, :], is_odd)
    for q, (records_in, planes) in enumerate(((low, range(1, FX)), (high, range(FX - 1)))):
        source_tile(n_gy, height, wide_y, records_in, planes, source.at[q], stacked, placing)


def sensors_body(height, keep, got, spot_hot, lane_hot, z_hot, rim_hot, readings, table):
    n_gx = 2 * keep.shape[0]
    got = row_slots(got, got.shape[0] - keep.shape[0] * keep.shape[1], keep.shape[1])
    rows = jnp.concatenate(join_slots(keep, got, "gx", n_gx.bit_length() - 2), axis=0)
    devices = rows.shape[0]
    slots = 3 * CAPS * devices
    own = slots // 3
    for n, t in enumerate((1, 0, 2)):
        for k in range(CAPS):
            at = (n * CAPS + k) * devices
            table[at : at + devices, :] = roll(rows, -PITCH * (CAPS * t + k), 1)
    cells = []
    for part in range(slots // LANES):
        lanes = slice(part * LANES, (part + 1) * LANES)
        turned = table[lanes, :].T
        cell = turned[CELL_AT : CELL_AT + 1, :].astype(jnp.int32) - 1
        at_y = cell % LANES
        slot_id = iota((1, LANES), 1) + part * LANES
        live = (cell >= 0) & (
            (slot_id < own)
            | ((slot_id < 2 * own) & (at_y >= LANES - RIM))
            | ((slot_id >= 2 * own) & (at_y < RIM))
        )
        cell = jnp.where(live, cell, -1)
        readings[0:8, lanes] = turned[OBS_AT : OBS_AT + 8]
        readings[8:16, lanes] = jnp.broadcast_to((cell + 1).astype(F32), (8, LANES))
        cells.append(cell)
    cell = jnp.concatenate(cells, axis=1)
    spot, lane = own_hot(cell[:, :own], height)
    spot_hot[...] = spot
    lane_hot[...] = lane
    z, rim = rim_hot_pair(cell[:, own:], height)
    z_hot[...] = z
    rim_hot[...] = rim


def own_hot(cell, height):
    spot = jnp.where(cell >= 0, cell // LANES, -1)
    at_y = jnp.where(cell >= 0, cell % LANES, -1)
    slots = cell.shape[1]
    return (
        (iota((FX * height, slots), 0) == spot).astype(BF16),
        (iota((LANES, slots), 0) == at_y).astype(BF16),
    )


def rim_hot_pair(cell, height):
    spot, at_y = cell // LANES, cell % LANES
    z = jnp.where(cell >= 0, spot % height, -1)
    lane = jnp.where(at_y < RIM, at_y, at_y - LANES + 2 * RIM)
    lane = jnp.where(cell >= 0, spot // height * 2 * RIM + lane, -1)
    slots = cell.shape[1]
    return (
        (iota((height, slots), 0) == z).astype(BF16),
        (iota((2 * RIM * FX, slots), 0) == lane).astype(BF16),
    )


def paired(hot):
    blank = jnp.zeros_like(hot)
    return jnp.concatenate(
        [jnp.concatenate([hot, blank], axis=1), jnp.concatenate([blank, hot], axis=1)], axis=0
    )


def inject(row_hot, lane_hot, values):
    placed = jnp.concatenate([lane_hot.astype(F32) * value for value in values], axis=0)
    total = None
    for part in pieces(placed, 2):
        term = dot(row_hot, part, ((1,), (1,)))
        total = term if total is None else total + term
    return total


def pack_rims(halos):
    packed = jnp.zeros(halos[0].shape, F32)
    lane = iota(packed.shape, 1)
    for g, halo in enumerate(halos):
        at = lane - 2 * RIM * g
        packed = jnp.where((at >= 0) & (at < RIM), roll(halo, 2 * RIM * g, 1), packed)
        packed = jnp.where(
            (at >= RIM) & (at < 2 * RIM), roll(halo, 2 * RIM * g + 2 * RIM, 1), packed
        )
    return packed


def coeffs_body(main, main_e, main_o, rim, rim_e, rim_o, coeffs, start, half_k):
    refs = (main, main_e, main_o, rim, rim_e, rim_o)
    is_odd = lax.rem(lax.axis_index("gx"), 2) == 1
    wide = 3 * FX
    height = half_k.shape[1]
    shape = (height, 2 * LANES)
    z = iota(shape, 0)
    for x in range(wide):
        centre, halo = extended(2, *refs, is_odd, x)
        half_k[x, :, :LANES] = 0.5 * centre
        half_k[x, :, LANES:] = 0.5 * halo
        for s in range(2):
            centre, halo = extended(s, *refs, is_odd, x)
            start[s, x, :, :LANES] = centre
            start[s, x, :, LANES:] = halo
    for x in range(wide):
        k = half_k[x]
        faces = (
            k + half_k[min(x + 1, wide - 1)],
            k + half_k[max(x - 1, 0)],
            k + roll(k, -1, 1),
            k + roll(k, 1, 1),
            k + jnp.where(z == height - 1, 0.0, roll(k, -1, 0)),
            k + jnp.where(z == 0, 0.0, roll(k, 1, 0)),
        )
        total = (faces[0] + faces[1]) + (faces[2] + faces[3]) + (faces[4] + faces[5])
        drift = []
        for axis in range(3):
            centre, halo = extended(3 + axis, *refs, is_odd, x)
            drift.append(0.5 * jnp.concatenate([centre, halo], axis=1))
        for s in range(2):
            coeffs[s, 6, x] = 1.0 - SCALES[s] * total
            for face in range(6):
                value = faces[face] if s == 0 else SCALES[s] * faces[face]
                value = value - drift[face // 2] if face % 2 == 0 else value + drift[face // 2]
                if face == 4:
                    value = jnp.where(z == height - 1, 0.0, value)
                if face == 5:
                    value = jnp.where(z == 0, 0.0, value)
                coeffs[s, face, x] = value


def inside_rows(n_gx, n_gy):
    row_id, col_id = lax.axis_index("gx"), lax.axis_index("gy")
    lane = iota((1, 2 * LANES), 1)
    lanes_in = (
        (lane < LANES)
        | ((lane < LANES + RIM) & (col_id < n_gy - 1))
        | ((lane >= 2 * LANES - RIM) & (col_id > 0))
    ).astype(F32)
    low = jnp.where(row_id > 0, lanes_in, 0.0)
    high = jnp.where(row_id < n_gx - 1, lanes_in, 0.0)
    return lambda x: low if x < FX else (lanes_in if x < 2 * FX else high)


def forward_body(n_gx, n_gy, steps, coeffs, start, rim_target, own_source, side_source, spot_hot, lane_hot, z_hot, rim_hot, readings, target, final, sent, residuals, cur):
    height = start.shape[2]
    wide = 3 * FX
    cells = FX * height
    slots = readings.shape[1]
    own = slots // 3
    rest = slots - own
    inside = inside_rows(n_gx, n_gy)
    fields = [start, cur.at[0], cur.at[1], cur.at[0], cur.at[1]]
    residuals[...] = jnp.zeros(residuals.shape, F32)
    live = (readings[8:9, :] > 0.5).astype(F32)
    lane_pair, rim_pair = paired(lane_hot[...]), paired(rim_hot[...])
    spots = spot_hot[...].astype(F32)
    heights = z_hot[...].astype(F32)

    def source(s, x):
        if x < FX:
            return side_source[0, s, x - 1]
        return own_source[s, x - FX] if x < 2 * FX else side_source[1, s, x - 2 * FX]

    for n in range(steps):
        before, after = fields[n], fields[n + 1]
        for x in range(n + 1, wide - n - 1):
            row = inside(x)
            for s in range(2):
                c = before[s, x]
                value = coeffs[s, 6, x] * c + source(s, x)
                value = value + coeffs[s, 0, x] * before[s, x + 1]
                value = value + coeffs[s, 1, x] * before[s, x - 1]
                value = value + coeffs[s, 2, x] * roll(c, -1, 1)
                value = value + coeffs[s, 3, x] * roll(c, 1, 1)
                value = value + coeffs[s, 4, x] * roll(c, -1, 0)
                value = value + coeffs[s, 5, x] * roll(c, 1, 0)
                after[s, x] = value * row
        both = jnp.concatenate(
            [after[s, FX : 2 * FX, :, :LANES].reshape(cells, LANES) for s in range(2)], axis=1
        )
        seen = spread(lane_pair, both)
        packed = pack_rims([after[s, FX + p, :, LANES:] for s in range(2) for p in range(FX)])
        seen_rim = spread(rim_pair, packed)
        for s in range(2):
            at = s * steps + n
            value = jnp.sum(seen[:, s * own : (s + 1) * own] * spots, axis=0, keepdims=True)
            value = (value - readings[at : at + 1, :own]) * live[:, :own]
            residuals[at : at + 1, :own] = value
            value = jnp.sum(seen_rim[:, s * rest : (s + 1) * rest] * heights, axis=0, keepdims=True)
            value = (value - readings[at : at + 1, own:]) * live[:, own:]
            residuals[at : at + 1, own:] = value
    residuals[8:16, :] = readings[8:16, :]
    last = fields[steps]
    ends = [residuals[s * steps + steps - 1 : (s + 1) * steps, :] for s in range(2)]
    put = inject(spot_hot[...], lane_hot[...], [end[:, :own] for end in ends])
    put_rim = inject(z_hot[...], rim_hot[...], [end[:, own:] for end in ends])
    for s in range(2):
        for p in range(FX):
            rows = slice(p * height, (p + 1) * height)
            got = last[s, FX + p, :, :LANES]
            final[s, p] = got
            g = s * FX + p
            sent[g * height : (g + 1) * height, :] = (
                got - target[s, p] + put[rows, s * LANES : (s + 1) * LANES]
            )
    base = 2 * FX * height
    sent[base : base + height, :] = packed - rim_target[...] + put_rim
    base = base + height
    for part in range(slots // LANES):
        lanes = slice(part * LANES, (part + 1) * LANES)
        rows = [residuals[s * steps + n : s * steps + n + 1, lanes] for s in range(2) for n in range(steps - 1)]
        for i, values in enumerate(rows + [residuals[8:9, lanes]] * (8 - len(rows))):
            sent[base + 8 * part + i : base + 8 * part + i + 1, :] = values


def own_puts_body(steps, spot_hot, lane_hot, z_hot, rim_hot, residuals, puts):
    slots = residuals.shape[1]
    own = slots // 3
    _, _, planes, height, _ = puts.shape
    for n in range(steps - 1):
        values = [residuals[s * steps + n : s * steps + n + 1, :] for s in range(2)]
        put = inject(spot_hot[...], lane_hot[...], [value[:, :own] for value in values])
        put_rim = inject(z_hot[...], rim_hot[...], [value[:, own:] for value in values])
        for s in range(2):
            for p in range(planes):
                rows = slice(p * height, (p + 1) * height)
                puts[n, s, p, :, :LANES] = put[rows, s * LANES : (s + 1) * LANES]
                puts[n, s, p, :, LANES:] = rim_tile(put_rim, s * FX + p)


def adjoint_body(n_gx, n_gy, steps, coeffs, sent, sent_e, sent_o, own_puts, foot_hot, foot_own, gradient, second, cur, puts, summed):
    is_odd = lax.rem(lax.axis_index("gx"), 2) == 1
    height = coeffs.shape[3]
    wide = 3 * FX
    cells = FX * height
    base = 2 * FX * height
    table = base + height
    slots = (sent.shape[0] - table) // 8 * LANES
    own = slots // 3
    inside = inside_rows(n_gx, n_gy)
    for q in (1, 0, 2):
        def take(lo, hi):
            if q == 1:
                return sent[lo:hi, :]
            if q == 0:
                return jnp.where(is_odd, sent_e[lo:hi, :], sent_o[lo:hi, :])
            return jnp.where(is_odd, sent_o[lo:hi, :], sent_e[lo:hi, :])
        packed_rim = take(base, base + height)
        for s in range(2):
            for p in range(FX):
                g = s * FX + p
                cur[0, s, q * FX + p, :, :LANES] = take(g * height, (g + 1) * height)
                cur[0, s, q * FX + p, :, LANES:] = rim_tile(packed_rim, g)
        if q == 1:
            continue
        rows = jnp.concatenate(
            [take(table + 8 * i, table + 8 * i + 8) for i in range(slots // LANES)], axis=1
        )
        cell = rows[7:8, :].astype(jnp.int32) - 1
        spot, lane = own_hot(cell[:, :own], height)
        z, rim = rim_hot_pair(cell[:, own:], height)
        for n in range(steps - 1):
            reach = (n + 1) * height
            part = slice(cells - reach, cells) if q == 0 else slice(0, reach)
            first = FX - n - 1 if q == 0 else 0
            values = [rows[s * (steps - 1) + n : s * (steps - 1) + n + 1, :] for s in range(2)]
            put = inject(spot[part], lane, [value[:, :own] for value in values])
            put_rim = inject(z, rim, [value[:, own:] for value in values])
            for s in range(2):
                for i in range(n + 1):
                    x = q * FX + first + i
                    puts[n, s, x, :, :LANES] = put[
                        i * height : (i + 1) * height, s * LANES : (s + 1) * LANES
                    ]
                    puts[n, s, x, :, LANES:] = rim_tile(put_rim, s * FX + first + i)
    for s in range(2):
        summed[s * cells : (s + 1) * cells, :] = sent[s * cells : (s + 1) * cells, :]
    for turn in range(steps - 1):
        now, later = turn % 2, (turn + 1) % 2
        n = steps - 2 - turn
        for x in range(turn + 1, wide - turn - 1):
            for s in range(2):
                put = own_puts[n, s, x - FX] if FX <= x < 2 * FX else puts[n, s, x]
                value = adjoint_value(coeffs, cur.at[now], s, x, 0) + put
                value = value * inside(x)
                if turn == steps - 2:
                    second[s, x - steps + 1] = value
                else:
                    cur[later, s, x] = value
                if FX <= x < 2 * FX:
                    at = s * cells + (x - FX) * height
                    summed[at : at + height, :] = summed[at : at + height, :] + value[:, :LANES]
    seen = spread(foot_hot[...], summed[...], ((1,), (1,)), count=2)
    width = foot_own.shape[1]
    held = width // FY
    out_row = iota((n_gy, width), 0)
    out_from = iota((n_gy, width), 1) // CAPA
    for s in range(2):
        row = jnp.sum(seen[s * cells : (s + 1) * cells] * foot_own[...], axis=0, keepdims=True)
        total = row
        for fy in range(1, FY):
            total = total + roll(row, -fy * held, 1)
        gradient[:, s, :] = jnp.where(out_row == out_from, total, 0.0)


def adjoint_value(coeffs, field, s, x, shift):
    w = field[s, x - shift]
    value = coeffs[s, 6, x] * w
    value = value + coeffs[s, 1, x + 1] * field[s, x + 1 - shift]
    value = value + coeffs[s, 0, x - 1] * field[s, x - 1 - shift]
    value = value + roll(coeffs[s, 3, x] * w, -1, 1)
    value = value + roll(coeffs[s, 2, x] * w, 1, 1)
    value = value + roll(coeffs[s, 5, x] * w, -1, 0)
    return value + roll(coeffs[s, 4, x] * w, 1, 0)


def last_body(steps, coeffs, second, first):
    for x in range(FX, 2 * FX):
        for s in range(2):
            first[s, x - FX] = adjoint_value(coeffs, second, s, x, steps - 1)[:, :LANES]


def returned_body(got, owner, out):
    n_gy, _, records = got.shape
    base = lax.axis_index("gy") * CAPA
    choice = slot_choices(owner[...], n_gy, CAPA)
    lane = iota((n_gy, records), 1)
    for s in range(2):
        rows = got[:, s, :]
        total = jnp.zeros(choice[0].shape, F32)
        for k in range(CAPA):
            column = jnp.sum(jnp.where(lane == base + k, rows, 0.0), axis=1, keepdims=True)
            total = total + choice[k].astype(F32) * column
        out[s : s + 1, :] = jnp.sum(total, axis=0, keepdims=True)


def per_device(
    initial_state,
    eddy_diffusivity,
    velocity,
    target,
    sensor_cell,
    sensor_owner,
    observations,
    actuator_block,
    actuator_owner,
    controls,
    footprint,
):
    _, wide_x, height, wide_y = initial_state.shape
    steps = observations.shape[2]
    n_gx, n_gy = lax.axis_size("gx"), lax.axis_size("gy")
    devices = n_gx * n_gy
    sens, acts = sensor_cell.shape[0], actuator_block.shape[0]
    records = n_gy * SLOT_ROWS
    slots = 3 * CAPS * devices
    cells = FX * height
    wide = 3 * FX
    shape = jax.ShapeDtypeStruct
    vmem = pltpu.VMEM
    a_owner_row = actuator_owner.reshape(1, acts)
    main = jnp.concatenate([initial_state, eddy_diffusivity[None], velocity], axis=0)
    slot_rows = SLOT_ROWS + -(-n_gx // 8) * 8
    half = shape((n_gy // 2, slot_rows, LANES), F32)
    sens_half = shape((n_gx // 2, n_gy, LANES), F32)
    strip_rows = 4 * height
    acts_send, acts_keep = call(
        functools.partial(records_out_body, n_gx, n_gy),
        (
            shape((n_gy // 2 * slot_rows, LANES), F32),
            half,
        ),
        [
            vmem((LANES, sens), F32),
            vmem((LANES, acts), F32),
            vmem((n_gy, slot_rows, LANES), F32),
        ],
        sensor_cell.reshape(1, sens),
        sensor_owner.reshape(1, sens),
        observations.transpose(1, 2, 0),
        actuator_block.reshape(1, acts),
        a_owner_row,
        controls.T,
        footprint,
    )
    strips = call(
        strips_body,
        shape((strip_rows, LANES), F32),
        [],
        initial_state,
        eddy_diffusivity,
        velocity,
        target,
    )
    main_e, main_o = exchange(main, "gx")
    strips_e, strips_o = exchange(strips, "gy")
    acts_keep, acts_got = route(acts_keep, swap(acts_send, "gy", 0), "gy")
    rim, rim_target, sens_keep = call(
        functools.partial(rim_body, n_gx),
        (
            shape((3 * height + records + n_gx // 2 * n_gy, LANES), F32),
            shape((height, LANES), F32),
            sens_half,
        ),
        [],
        strips_e, strips_o, acts_keep, acts_got,
    )
    rim_e, rim_o = exchange(rim, "gx")
    held = n_gy * CAPA
    scratch = [vmem((cells, FY * records), F32), vmem((FY * records, 2 * LANES), BF16)]
    own_source, foot_hot, foot_own = call(
        functools.partial(own_source_body, n_gy, height, wide_y),
        (
            shape((2, FX, height, 2 * LANES), F32),
            shape((FY * held, LANES), BF16),
            shape((cells, FY * held), F32),
        ),
        scratch,
        rim,
        us=1.5,
    )
    side_source = call(
        functools.partial(side_source_body, n_gy, height, wide_y),
        shape((2, 2, FX - 1, height, 2 * LANES), F32),
        scratch,
        rim_e, rim_o,
        us=1.5,
    )
    sens_keep, sens_got = route(sens_keep, rim_e, "gx", after=foot_hot)
    coeffs, start = call(
        coeffs_body,
        (
            shape((2, 7, wide, height, 2 * LANES), F32),
            shape((2, wide, height, 2 * LANES), F32),
        ),
        [vmem((wide, height, 2 * LANES), F32)],
        main, main_e, main_o, rim, rim_e, rim_o,
        us=1.6,
    )
    sens_keep, start = lax.optimization_barrier((sens_keep, start))
    own_slots = slots // 3
    rest = slots - own_slots
    *hots, readings = call(
        functools.partial(sensors_body, height),
        (
            shape((cells, own_slots), BF16),
            shape((LANES, own_slots), BF16),
            shape((height, rest), BF16),
            shape((2 * RIM * FX, rest), BF16),
            shape((16, slots), F32),
        ),
        [vmem((slots, LANES), F32)],
        sens_keep, sens_got,
    )
    sent_rows = 2 * cells + height + slots // LANES * 8
    final, sent, residuals = call(
        functools.partial(forward_body, n_gx, n_gy, steps),
        (
            shape((2, FX, height, LANES), F32),
            shape((sent_rows, LANES), F32),
            shape((16, slots), F32),
        ),
        [vmem((2, 2, wide, height, 2 * LANES), F32)],
        coeffs, start, rim_target, own_source, side_source, *hots, readings, target,
        us=5.0,
    )
    sent_e, sent_o = exchange(sent, "gx")
    own_puts = call(
        functools.partial(own_puts_body, steps),
        shape((steps - 1, 2, FX, height, 2 * LANES), F32),
        [],
        *hots, residuals,
        us=0.7,
    )
    gradient, second = call(
        functools.partial(adjoint_body, n_gx, n_gy, steps),
        (
            shape((n_gy, 2, FY * held), F32),
            shape((2, wide - 2 * steps + 2, height, 2 * LANES), F32),
        ),
        [
            vmem((2, 2, wide, height, 2 * LANES), F32),
            vmem((steps - 1, 2, wide, height, 2 * LANES), F32),
            vmem((2 * cells, LANES), F32),
        ],
        coeffs, sent, sent_e, sent_o, own_puts, foot_hot, foot_own,
        us=4.0,
    )
    back = lax.all_to_all(gradient, "gy", split_axis=0, concat_axis=0, tiled=True)
    first = call(
        functools.partial(last_body, steps),
        shape((2, FX, height, LANES), F32),
        [],
        coeffs, second,
        us=1.0,
    )
    returned = call(returned_body, shape((2, acts), F32), [], back, a_owner_row)
    return (final, first, returned.T)


def solution(mesh):
    in_specs = (
        P(None, "gx", None, "gy"),
        P("gx", None, "gy"),
        P(None, "gx", None, "gy"),
        P(None, "gx", None, "gy"),
        P(("gx", "gy")),
        P(("gx", "gy"), None),
        P(("gx", "gy"), None, None),
        P(("gx", "gy")),
        P(("gx", "gy"), None),
        P(("gx", "gy"), None),
        P(("gx", "gy"), None),
    )
    out_specs = (P(None, "gx", None, "gy"), P(None, "gx", None, "gy"), P(("gx", "gy"), None))
    return jax.shard_map(
        per_device, mesh=mesh, in_specs=in_specs, out_specs=out_specs, check_vma=False
    )
```

time: 59.3 us -> 55.7 us (0.939)
  waiting for transfers between devices: 13.4 us -> 11.4 us
  Pallas kernels: 16.2 us -> 14.9 us
  starting transfers between devices: 23.4 us -> 22.7 us
    all_to_all x1 -> x0, starting transfers between devices: 5.43 us -> none  [per_device(): lax.all_to_all(outgoing, ('gx', 'gy'), split_axis=0, concat_axis=0, tiled...]
    ppermute x0 -> x4, starting transfers between devices: none -> 3.33 us  [swap(): return lax.ppermute(values, axis, [(i, i ^ 1 << bit) for i in range(count)])]
    ppermute x8, waiting for transfers between devices: 12.1 us -> 10.2 us  [exchange(): return (lax.ppermute(values, axis, even), lax.ppermute(values, axis, odd))]
    all_to_all x1 -> x0, waiting for transfers between devices: 1.35 us -> none  [per_device(): lax.all_to_all(outgoing, ('gx', 'gy'), split_axis=0, concat_axis=0, tiled...]
    pallas_call x10 -> x15, Pallas kernels: 16.2 us -> 14.9 us  [call(): pl.pallas_call(body, cost_estimate=pl.CostEstimate(flops=0, transcendenta...]
    all_to_all x1, starting transfers between devices: 3.96 us -> 5.23 us  [per_device(): lax.all_to_all(gradient, 'gy', split_axis=0, concat_axis=0, tiled=True)]
    ppermute x0 -> x4, waiting for transfers between devices: none -> 1.23 us  [swap(): return lax.ppermute(values, axis, [(i, i ^ 1 << bit) for i in range(count)])]
  transfers between devices with their start and end apart: 10 -> 13, of which waited for: 5 -> 5; matrix products, arithmetic and copies ran while one was open for 0% -> 0% of each run, Pallas kernels for 10% -> 13%
where the time goes in v2:
time: 55.7 us; the launch traced here: 54.6 us
  starting transfers between devices  22.7 us (41%)
  Pallas kernels  14.9 us (27%)
  waiting for transfers between devices  11.4 us (20%)
  local copies, waits for them, and re-layouts  3.39 us (6%)
  other arithmetic  1.28 us (2%)
  between operations  0.98 us (2%)
    pallas_call x15, Pallas kernels, call(): pl.pallas_call(body, cost_estimate=pl.CostEstimate(flops=0, transcendenta...  14.9 us
    ppermute x8, starting transfers between devices, exchange(): return (lax.ppermute(values, axis, even), lax.ppermute(values, axis, odd))  14.1 us
    ppermute x8, waiting for transfers between devices, exchange(): return (lax.ppermute(values, axis, even), lax.ppermute(values, axis, odd))  10.2 us
    all_to_all x1, starting transfers between devices, per_device(): lax.all_to_all(gradient, 'gy', split_axis=0, concat_axis=0, tiled=True)  5.23 us
    unnamed x26, local copies, waits for them, and re-layouts  3.39 us
    ppermute x4, starting transfers between devices, swap(): return lax.ppermute(values, axis, [(i, i ^ 1 << bit) for i in range(count)])  3.33 us
    concatenate x1, other arithmetic, per_device(): jnp.concatenate([initial_state, eddy_diffusivity[None], velocity], axis=0)  1.28 us
    ppermute x4, waiting for transfers between devices, swap(): return lax.ppermute(values, axis, [(i, i ^ 1 << bit) for i in range(count)])  1.23 us
  transfers between devices with their start and end apart: 13, of which 5 were waited for; matrix products, arithmetic and copies ran while one was open for 0% of the time, Pallas kernels for 13%

profile of v2, /device:TPU:20, one launch (start us, length us, event | category | flops | bytes accessed | tf_op | source)
XLA Modules:
  0.0 54.6 jit_solution(1250475876261115782)
XLA Ops:
  0.6 0.0 copy-start.3
  0.6 0.0 copy-start.2
  0.7 0.0 copy-start.5
  0.7 0.0 copy-start.8
  0.7 0.0 copy-start.10
  0.7 0.0 copy-start.11
  0.7 0.0 copy-start.7
  0.7 0.0 copy-start.12
  0.7 0.0 copy-start.9
  0.7 0.0 copy-start.6
  0.7 0.0 copy-start.4
  0.7 1.3 %pad_maximum_fusion.main = f32[6,4,48,128]{3,2,1,0:T(8,128)S(1)} fusion(f32[3,4,48,128]{3,2,1,0:T(8,128)} %vel.1, f32[1,4,48,128]{3,2,1,0:T(8,128)} %bitcast.8, f32[2,4,48,128]{3,2,1,0:T(8,128)} %state.1), kind=kLoop, calls=%fused_computation | loop fusion | flops 294912 | bytes 1179648 | tf_op jit(solution)/shard_map/concatenate | solution.py:728
  2.0 1.6 %collective-permute-start = (f32[6,4,48,128]{3,2,1,0:T(8,128)S(1)}, f32[6,4,48,128]{3,2,1,0:T(8,128)S(1)}, u32[]{:S(2)}, u32[]{:S(2)}) collective-permute-start(f32[6,4,48,128]{3,2,1,0:T(8,128)S(1)} %pad_maximum_fusion.main), channel_id=1, source_target_pairs={{0,8},{8,0},{16,24},{24,16},{1,9},{9,1},{17,25},{25,17},{2,10},{10... | collective-permute-start | bytes 1769480 | tf_op jit(solution)/shard_map/ppermute | solution.py:80
  3.7 1.9 %collective-permute-start.1 = (f32[6,4,48,128]{3,2,1,0:T(8,128)S(1)}, f32[6,4,48,128]{3,2,1,0:T(8,128)S(1)}, u32[]{:S(2)}, u32[]{:S(2)}) collective-permute-start(f32[6,4,48,128]{3,2,1,0:T(8,128)S(1)} %pad_maximum_fusion.main), channel_id=1, source_target_pairs={{8,16},{16,8},{9,17},{17,9},{10,18},{18,10},{11,19},{19,11},{12,20... | collective-permute-start | bytes 1769480 | tf_op jit(solution)/shard_map/ppermute | solution.py:80
  5.6 0.0 copy-done.8
  5.6 0.0 copy-done.10
  5.6 0.0 copy-done.11
  5.6 0.0 copy-done.7
  5.6 0.0 copy-done.12
  5.6 0.0 copy-done.9
  5.6 0.0 copy-done.6
  5.7 0.8 %shard_map.131 = (f32[96,128]{1,0:T(8,128)S(1)}, f32[4,24,128]{2,1,0:T(8,128)S(1)}) custom-call(s32[1,64]{1,0:T(1,128)S(1)} %bitcast.13, s32[1,64]{1,0:T(1,128)S(1)} %bitcast.14, f32[2,4,64]{2,1,0:T(4,128)S(1)} %bitcast.9, s32[1,16]{1,0:T(1,128)S(1)} %bitcast.15, s32[1,16]{1,0:T(1,128)S(1)} %bitcast.10, f32[2,16]{1,0:T(2,128)S(1)} %bitcast.12, ...), custom_call_target="tpu_custom_call" | custom-call | bytes 720000 | tf_op jit(solution)/shard_map/pallas_call | solution.py:88
  6.4 0.1 collective-permute-start.4
  6.5 1.2 %collective-permute-done.4.got = f32[96,128]{1,0:T(8,128)S(1)} collective-permute-done((f32[96,128]{1,0:T(8,128)S(1)}, f32[96,128]{1,0:T(8,128)S(1)}, u32[]{:S(2)}, u32[]{:S(2)}) %collective-permute-start.4) | collective-permute-done | bytes 49184 | tf_op jit(solution)/shard_map/ppermute | solution.py:172
  7.8 1.6 %collective-permute-start.5 = (f32[96,128]{1,0:T(8,128)S(1)}, f32[96,128]{1,0:T(8,128)S(1)}, u32[]{:S(2)}, u32[]{:S(2)}) collective-permute-start(f32[96,128]{1,0:T(8,128)S(1)} %get-tuple-element.35), channel_id=1, source_target_pairs={{0,2},{1,3},{2,0},{3,1},{4,6},{5,7},{6,4},{7,5},{8,10},{9,11},{10,... | collective-permute-start | bytes 147464 | tf_op jit(solution)/shard_map/ppermute | solution.py:172
  9.3 0.0 copy-done.3
  9.3 0.0 copy-done.2
  9.3 0.0 copy-done.5
  9.3 0.0 copy-done.4
  9.3 0.3 shard_map.130
  9.6 0.1 collective-permute-start.2
  9.7 2.5 %collective-permute-start.3 = (f32[192,128]{1,0:T(8,128)S(1)}, f32[192,128]{1,0:T(8,128)S(1)}, u32[]{:S(2)}, u32[]{:S(2)}) collective-permute-start(f32[192,128]{1,0:T(8,128)S(1)} %shard_map.130), channel_id=1, source_target_pairs={{1,2},{2,1},{3,4},{4,3},{5,6},{6,5},{9,10},{10,9},{11,12},{12,11},... | collective-permute-start | bytes 294920 | tf_op jit(solution)/shard_map/ppermute | solution.py:80
  12.2 0.0 collective-permute-done.5.got
  12.2 0.3 collective-permute-start.6
  12.5 0.0 collective-permute-done.2.even
  12.5 4.8 %collective-permute-done.3.odd = f32[192,128]{1,0:T(8,128)S(1)} collective-permute-done((f32[192,128]{1,0:T(8,128)S(1)}, f32[192,128]{1,0:T(8,128)S(1)}, u32[]{:S(2)}, u32[]{:S(2)}) %collective-permute-start.3) | collective-permute-done | bytes 98336 | tf_op jit(solution)/shard_map/ppermute | solution.py:80
  17.3 0.0 collective-permute-done.6.got
  17.3 0.1 shard_map.134
  17.4 0.1 collective-permute-start.7
  17.5 3.9 %collective-permute-start.8 = (f32[288,128]{1,0:T(8,128)S(1)}, f32[288,128]{1,0:T(8,128)S(1)}, u32[]{:S(2)}, u32[]{:S(2)}) collective-permute-start(f32[288,128]{1,0:T(8,128)S(1)} %get-tuple-element.38.rim.got), channel_id=1, source_target_pairs={{8,16},{16,8},{9,17},{17,9},{10,18},{18,10},{11,19},{19,11},{12,20... | collective-permute-start | bytes 442376 | tf_op jit(solution)/shard_map/ppermute | solution.py:80
  21.4 1.3 %shard_map.137 = (f32[2,4,48,256]{3,2,1,0:T(8,128)S(1)}, bf16[128,128]{1,0:T(8,128)(2,1)S(1)}, f32[192,128]{1,0:T(8,128)S(1)}) custom-call(f32[288,128]{1,0:T(8,128)S(1)} %get-tuple-element.38.rim.got), custom_call_target="tpu_custom_call" | custom-call | bytes 5400000 | tf_op jit(solution)/shard_map/pallas_call | solution.py:88
  22.7 0.0 collective-permute-done.7.rim_e.got.got_e
  22.7 1.4 %collective-permute-start.9 = (f32[16,128]{1,0:T(8,128)S(1)}, f32[16,128]{1,0:T(8,128)S(1)}, u32[]{:S(2)}, u32[]{:S(2)}) collective-permute-start(f32[16,128]{1,0:T(8,128)S(1)} %get-tuple-element.49), channel_id=1, source_target_pairs={{0,16},{8,24},{16,0},{24,8},{1,17},{9,25},{17,1},{25,9},{2,18},{10... | collective-permute-start | bytes 24584 | tf_op jit(solution)/shard_map/ppermute | solution.py:172
  24.1 0.5 collective-permute-done.8.rim_o.got_o
  24.6 1.5 %shard_map.138.side_source = f32[2,2,3,48,256]{4,3,2,1,0:T(8,128)S(1)} custom-call(f32[288,128]{1,0:T(8,128)S(1)} %collective-permute-done.7.rim_e.got.got_e, f32[288,128]{1,0:T(8,128)S(1)} %collective-permute-done.8.rim_o.got_o), custom_call_target="tpu_custom_call" | custom-call | bytes 5400000 | tf_op jit(solution)/shard_map/pallas_call | solution.py:88
  26.1 0.0 collective-permute-done.main_e
  26.1 0.0 collective-permute-done.1.main_o
  26.2 1.5 %shard_map.135 = (f32[2,7,12,48,256]{4,3,2,1,0:T(8,128)S(1)}, f32[2,12,48,256]{3,2,1,0:T(8,128)S(1)}) custom-call(f32[6,4,48,128]{3,2,1,0:T(8,128)S(1)} %pad_maximum_fusion.main, f32[6,4,48,128]{3,2,1,0:T(8,128)S(1)} %collective-permute-done.main_e, f32[6,4,48,128]{3,2,1,0:T(8,128)S(1)} %collective-permute-done.1.main_o, ...), custom_call_target="tpu_custom_call" | custom-call | bytes 5760000 | tf_op jit(solution)/shard_map/pallas_call | solution.py:88
  27.7 0.0 copy-start
  27.7 0.0 collective-permute-done.9.got
  27.7 0.3 shard_map.139
  28.0 3.7 %shard_map.140 = (f32[2,4,48,128]{3,2,1,0:T(8,128)}, f32[456,128]{1,0:T(8,128)S(1)}, f32[16,384]{1,0:T(8,128)S(1)}) custom-call(f32[2,7,12,48,256]{4,3,2,1,0:T(8,128)S(1)} %get-tuple-element.39.coeffs, f32[2,12,48,256]{3,2,1,0:T(8,128)S(1)} %get-tuple-element.43.start, f32[48,128]{1,0:T(8,128)S(1)} %get-tuple-element.44.rim_target, ...), custom_call_target="tpu_custom_call" | custom-call | bytes 18000000 | tf_op jit(solution)/shard_map/pallas_call | solution.py:88
  31.6 1.5 %collective-permute-start.10 = (f32[456,128]{1,0:T(8,128)S(1)}, f32[456,128]{1,0:T(8,128)S(1)}, u32[]{:S(2)}, u32[]{:S(2)}) collective-permute-start(f32[456,128]{1,0:T(8,128)S(1)} %get-tuple-element.56.sent), channel_id=1, source_target_pairs={{0,8},{8,0},{16,24},{24,16},{1,9},{9,1},{17,25},{25,17},{2,10},{10... | collective-permute-start | bytes 700424 | tf_op jit(solution)/shard_map/ppermute | solution.py:80
  33.2 2.5 %collective-permute-start.11 = (f32[456,128]{1,0:T(8,128)S(1)}, f32[456,128]{1,0:T(8,128)S(1)}, u32[]{:S(2)}, u32[]{:S(2)}) collective-permute-start(f32[456,128]{1,0:T(8,128)S(1)} %get-tuple-element.56.sent), channel_id=1, source_target_pairs={{8,16},{16,8},{9,17},{17,9},{10,18},{18,10},{11,19},{19,11},{12,20... | collective-permute-start | bytes 700424 | tf_op jit(solution)/shard_map/ppermute | solution.py:80
  35.6 0.5 shard_map.141.own_puts
  36.2 1.5 %collective-permute-done.10.sent_e = f32[456,128]{1,0:T(8,128)S(1)} collective-permute-done((f32[456,128]{1,0:T(8,128)S(1)}, f32[456,128]{1,0:T(8,128)S(1)}, u32[]{:S(2)}, u32[]{:S(2)}) %collective-permute-start.10) | collective-permute-done | bytes 233504 | tf_op jit(solution)/shard_map/ppermute | solution.py:80
  37.7 3.4 %collective-permute-done.11.sent_o = f32[456,128]{1,0:T(8,128)S(1)} collective-permute-done((f32[456,128]{1,0:T(8,128)S(1)}, f32[456,128]{1,0:T(8,128)S(1)}, u32[]{:S(2)}, u32[]{:S(2)}) %collective-permute-start.11) | collective-permute-done | bytes 233504 | tf_op jit(solution)/shard_map/ppermute | solution.py:80
  41.1 0.0 copy-done
  41.1 3.3 %shard_map.142 = (f32[8,2,128]{2,1,0:T(2,128)}, f32[2,6,48,256]{3,2,1,0:T(8,128)S(1)}) custom-call(f32[2,7,12,48,256]{4,3,2,1,0:T(8,128)S(1)} %get-tuple-element.39.coeffs, f32[456,128]{1,0:T(8,128)S(1)} %get-tuple-element.56.sent, f32[456,128]{1,0:T(8,128)S(1)} %collective-permute-done.10.sent_e, f32[456,128]{1,0:T(8,128)S(1)} %collective-permute-done.11.sent_o, ...), custom_call_target="tpu_custom_call" | custom-call | bytes 14400000 | tf_op jit(solution)/shard_map/pallas_call | solution.py:88
  44.4 5.2 %all-to-all-start = ((f32[8,2,128]{2,1,0:T(2,128)}), f32[8,2,128]{2,1,0:T(2,128)S(1)}, u32[]{:S(2)}, u32[]{:S(2)}) async-start(f32[8,2,128]{2,1,0:T(2,128)} %get-tuple-element.60), calls=%async_computation | async-start | bytes 16384 | tf_op jit(solution)/shard_map/all_to_all | solution.py:855
  49.7 3.3 %copy-done.1 = f32[2,7,12,48,256]{4,3,2,1,0:T(8,128)S(1)} copy-done((f32[2,7,12,48,256]{4,3,2,1,0:T(8,128)S(1)}, f32[2,7,12,48,256]{4,3,2,1,0:T(8,128)}, u32[]{:S(2)}) %copy-start.1) | copy-done | bytes 8257560
  53.0 1.0 %shard_map.143 = f32[2,4,48,128]{3,2,1,0:T(8,128)} custom-call(f32[2,7,12,48,256]{4,3,2,1,0:T(8,128)S(1)} %copy-done.1, f32[2,6,48,256]{3,2,1,0:T(8,128)S(1)} %get-tuple-element.59.second), custom_call_target="tpu_custom_call" | custom-call | bytes 3600000 | tf_op jit(solution)/shard_map/pallas_call | solution.py:88
  53.9 0.0 all-to-all-done.got
  53.9 0.7 %shard_map.144 = f32[2,16]{1,0:T(2,128)} custom-call(f32[8,2,128]{2,1,0:T(2,128)S(1)} %all-to-all-done.got, s32[1,16]{1,0:T(1,128)S(1)} %bitcast.11), custom_call_target="tpu_custom_call" | custom-call | bytes 720000 | tf_op jit(solution)/shard_map/pallas_call | solution.py:88
  (4 shorter events, 0.1 us)
Async XLA Ops:
  0.6 8.7 %copy-start.3 = (f32[2,4,48,128]{3,2,1,0:T(8,128)S(1)}, f32[2,4,48,128]{3,2,1,0:T(8,128)}, u32[]{:S(2)}) copy-start(f32[2,4,48,128]{3,2,1,0:T(8,128)} %state.1) | copy-start | bytes 589828
  0.6 8.7 %copy-start.2 = (f32[3,4,48,128]{3,2,1,0:T(8,128)S(1)}, f32[3,4,48,128]{3,2,1,0:T(8,128)}, u32[]{:S(2)}) copy-start(f32[3,4,48,128]{3,2,1,0:T(8,128)} %vel.1) | copy-start | bytes 884740
  0.7 8.7 %copy-start.5 = (f32[4,48,128]{2,1,0:T(8,128)S(1)}, f32[4,48,128]{2,1,0:T(8,128)}, u32[]{:S(2)}) copy-start(f32[4,48,128]{2,1,0:T(8,128)} %kappa.1) | copy-start | bytes 294916
  0.7 4.9 %copy-start.8 = (s32[16,1]{0,1:T(1,128)S(1)}, s32[16,1]{0,1:T(1,128)}, u32[]{:S(2)}) copy-start(s32[16,1]{0,1:T(1,128)} %param.19) | copy-start | bytes 196
  0.7 4.9 %copy-start.10 = (s32[64]{0:T(128)S(1)}, s32[64]{0:T(128)}, u32[]{:S(2)}) copy-start(s32[64]{0:T(128)} %param.15) | copy-start | bytes 772
  0.7 4.9 %copy-start.11 = (s32[64,1]{0,1:T(1,128)S(1)}, s32[64,1]{0,1:T(1,128)}, u32[]{:S(2)}) copy-start(s32[64,1]{0,1:T(1,128)} %param.16) | copy-start | bytes 772
  0.7 4.9 %copy-start.7 = (f32[64,2,4]{0,2,1:T(4,128)S(1)}, f32[64,2,4]{0,2,1:T(4,128)}, u32[]{:S(2)}) copy-start(f32[64,2,4]{0,2,1:T(4,128)} %param.17) | copy-start | bytes 6148
  0.7 4.9 %copy-start.12 = (s32[16]{0:T(128)S(1)}, s32[16]{0:T(128)}, u32[]{:S(2)}) copy-start(s32[16]{0:T(128)} %param.18) | copy-start | bytes 196
  0.7 4.9 %copy-start.9 = (f32[16,2]{0,1:T(2,128)S(1)}, f32[16,2]{0,1:T(2,128)}, u32[]{:S(2)}) copy-start(f32[16,2]{0,1:T(2,128)} %param.20) | copy-start | bytes 388
  0.7 4.9 %copy-start.6 = (f32[16,128]{1,0:T(8,128)S(1)}, f32[16,128]{1,0:T(8,128)}, u32[]{:S(2)}) copy-start(f32[16,128]{1,0:T(8,128)} %foot.1) | copy-start | bytes 24580
  0.7 8.6 %copy-start.4 = (f32[2,4,48,128]{3,2,1,0:T(8,128)S(1)}, f32[2,4,48,128]{3,2,1,0:T(8,128)}, u32[]{:S(2)}) copy-start(f32[2,4,48,128]{3,2,1,0:T(8,128)} %target.3) | copy-start | bytes 589828
  2.0 24.1 %collective-permute-start = (f32[6,4,48,128]{3,2,1,0:T(8,128)S(1)}, f32[6,4,48,128]{3,2,1,0:T(8,128)S(1)}, u32[]{:S(2)}, u32[]{:S(2)}) collective-permute-start(f32[6,4,48,128]{3,2,1,0:T(8,128)S(1)} %pad_maximum_fusion.main), channel_id=1, source_target_pairs={{0,8},{8,0},{16,24},{24,16},{1,9},{9,1},{17,25},{25,17},{2,10},{10... | collective-permute-start | bytes 1769480 | tf_op jit(solution)/shard_map/ppermute | solution.py:80
  3.7 22.5 %collective-permute-start.1 = (f32[6,4,48,128]{3,2,1,0:T(8,128)S(1)}, f32[6,4,48,128]{3,2,1,0:T(8,128)S(1)}, u32[]{:S(2)}, u32[]{:S(2)}) collective-permute-start(f32[6,4,48,128]{3,2,1,0:T(8,128)S(1)} %pad_maximum_fusion.main), channel_id=1, source_target_pairs={{8,16},{16,8},{9,17},{17,9},{10,18},{18,10},{11,19},{19,11},{12,20... | collective-permute-start | bytes 1769480 | tf_op jit(solution)/shard_map/ppermute | solution.py:80
  6.4 1.3 %collective-permute-start.4 = (f32[96,128]{1,0:T(8,128)S(1)}, f32[96,128]{1,0:T(8,128)S(1)}, u32[]{:S(2)}, u32[]{:S(2)}) collective-permute-start(f32[96,128]{1,0:T(8,128)S(1)} %get-tuple-element.33), channel_id=1, source_target_pairs={{0,1},{1,0},{2,3},{3,2},{4,5},{5,4},{6,7},{7,6},{8,9},{9,8},{10,11... | collective-permute-start | bytes 147464 | tf_op jit(solution)/shard_map/ppermute | solution.py:172
  7.8 4.4 %collective-permute-start.5 = (f32[96,128]{1,0:T(8,128)S(1)}, f32[96,128]{1,0:T(8,128)S(1)}, u32[]{:S(2)}, u32[]{:S(2)}) collective-permute-start(f32[96,128]{1,0:T(8,128)S(1)} %get-tuple-element.35), channel_id=1, source_target_pairs={{0,2},{1,3},{2,0},{3,1},{4,6},{5,7},{6,4},{7,5},{8,10},{9,11},{10,... | collective-permute-start | bytes 147464 | tf_op jit(solution)/shard_map/ppermute | solution.py:172
  9.6 2.9 %collective-permute-start.2 = (f32[192,128]{1,0:T(8,128)S(1)}, f32[192,128]{1,0:T(8,128)S(1)}, u32[]{:S(2)}, u32[]{:S(2)}) collective-permute-start(f32[192,128]{1,0:T(8,128)S(1)} %shard_map.130), channel_id=1, source_target_pairs={{0,1},{1,0},{2,3},{3,2},{4,5},{5,4},{6,7},{7,6},{8,9},{9,8},{10,11... | collective-permute-start | bytes 294920 | tf_op jit(solution)/shard_map/ppermute | solution.py:80
  9.7 7.6 %collective-permute-start.3 = (f32[192,128]{1,0:T(8,128)S(1)}, f32[192,128]{1,0:T(8,128)S(1)}, u32[]{:S(2)}, u32[]{:S(2)}) collective-permute-start(f32[192,128]{1,0:T(8,128)S(1)} %shard_map.130), channel_id=1, source_target_pairs={{1,2},{2,1},{3,4},{4,3},{5,6},{6,5},{9,10},{10,9},{11,12},{12,11},... | collective-permute-start | bytes 294920 | tf_op jit(solution)/shard_map/ppermute | solution.py:80
  12.2 5.1 %collective-permute-start.6 = (f32[96,128]{1,0:T(8,128)S(1)}, f32[96,128]{1,0:T(8,128)S(1)}, u32[]{:S(2)}, u32[]{:S(2)}) collective-permute-start(f32[96,128]{1,0:T(8,128)S(1)} %get-tuple-element.37), channel_id=1, source_target_pairs={{0,4},{1,5},{2,6},{3,7},{4,0},{5,1},{6,2},{7,3},{8,12},{9,13},{10,... | collective-permute-start | bytes 147464 | tf_op jit(solution)/shard_map/ppermute | solution.py:172
  17.4 5.3 %collective-permute-start.7 = (f32[288,128]{1,0:T(8,128)S(1)}, f32[288,128]{1,0:T(8,128)S(1)}, u32[]{:S(2)}, u32[]{:S(2)}) collective-permute-start(f32[288,128]{1,0:T(8,128)S(1)} %get-tuple-element.38.rim.got), channel_id=1, source_target_pairs={{0,8},{8,0},{16,24},{24,16},{1,9},{9,1},{17,25},{25,17},{2,10},{10... | collective-permute-start | bytes 442376 | tf_op jit(solution)/shard_map/ppermute | solution.py:80
  17.5 7.1 %collective-permute-start.8 = (f32[288,128]{1,0:T(8,128)S(1)}, f32[288,128]{1,0:T(8,128)S(1)}, u32[]{:S(2)}, u32[]{:S(2)}) collective-permute-start(f32[288,128]{1,0:T(8,128)S(1)} %get-tuple-element.38.rim.got), channel_id=1, source_target_pairs={{8,16},{16,8},{9,17},{17,9},{10,18},{18,10},{11,19},{19,11},{12,20... | collective-permute-start | bytes 442376 | tf_op jit(solution)/shard_map/ppermute | solution.py:80
  22.7 5.0 %collective-permute-start.9 = (f32[16,128]{1,0:T(8,128)S(1)}, f32[16,128]{1,0:T(8,128)S(1)}, u32[]{:S(2)}, u32[]{:S(2)}) collective-permute-start(f32[16,128]{1,0:T(8,128)S(1)} %get-tuple-element.49), channel_id=1, source_target_pairs={{0,16},{8,24},{16,0},{24,8},{1,17},{9,25},{17,1},{25,9},{2,18},{10... | collective-permute-start | bytes 24584 | tf_op jit(solution)/shard_map/ppermute | solution.py:172
  27.7 13.4 %copy-start = (f32[2,7,12,48,256]{4,3,2,1,0:T(8,128)}, f32[2,7,12,48,256]{4,3,2,1,0:T(8,128)S(1)}, u32[]{:S(2)}) copy-start(f32[2,7,12,48,256]{4,3,2,1,0:T(8,128)S(1)} %get-tuple-element.39.coeffs) | copy-start | bytes 24772612
  31.6 6.1 %collective-permute-start.10 = (f32[456,128]{1,0:T(8,128)S(1)}, f32[456,128]{1,0:T(8,128)S(1)}, u32[]{:S(2)}, u32[]{:S(2)}) collective-permute-start(f32[456,128]{1,0:T(8,128)S(1)} %get-tuple-element.56.sent), channel_id=1, source_target_pairs={{0,8},{8,0},{16,24},{24,16},{1,9},{9,1},{17,25},{25,17},{2,10},{10... | collective-permute-start | bytes 700424 | tf_op jit(solution)/shard_map/ppermute | solution.py:80
  33.2 7.9 %collective-permute-start.11 = (f32[456,128]{1,0:T(8,128)S(1)}, f32[456,128]{1,0:T(8,128)S(1)}, u32[]{:S(2)}, u32[]{:S(2)}) collective-permute-start(f32[456,128]{1,0:T(8,128)S(1)} %get-tuple-element.56.sent), channel_id=1, source_target_pairs={{8,16},{16,8},{9,17},{17,9},{10,18},{18,10},{11,19},{19,11},{12,20... | collective-permute-start | bytes 700424 | tf_op jit(solution)/shard_map/ppermute | solution.py:80
  44.4 9.5 %all-to-all-start = ((f32[8,2,128]{2,1,0:T(2,128)}), f32[8,2,128]{2,1,0:T(2,128)S(1)}, u32[]{:S(2)}, u32[]{:S(2)}) async-start(f32[8,2,128]{2,1,0:T(2,128)} %get-tuple-element.60), calls=%async_computation | async-start | bytes 16384 | tf_op jit(solution)/shard_map/all_to_all | solution.py:855
  49.6 3.3 %copy-start.1 = (f32[2,7,12,48,256]{4,3,2,1,0:T(8,128)S(1)}, f32[2,7,12,48,256]{4,3,2,1,0:T(8,128)}, u32[]{:S(2)}) copy-start(f32[2,7,12,48,256]{4,3,2,1,0:T(8,128)} %copy-done) | copy-start | bytes 24772612

commit v3 on v2

--- a/solution.py
+++ b/solution.py
@@ -116,24 +116,6 @@
         self.ref[self.base + at * self.rows : self.base + (at + 1) * self.rows, :] = value
 
 
-class split_planes:
-    def __init__(self, inner, outer):
-        self.inner, self.outer = inner, outer
-
-    def place(self, x):
-        if FX - 1 <= x <= 2 * FX:
-            return self.inner, x - FX + 1
-        return self.outer, x if x < FX else x - FX - 2
-
-    def __getitem__(self, at):
-        ref, x = self.place(at[2])
-        return ref[at[0], at[1], x]
-
-    def __setitem__(self, at, value):
-        ref, x = self.place(at[2])
-        ref[at[0], at[1], x] = value
-
-
 def without_bit(slot, bit):
     return (slot >> (bit + 1) << bit) | (slot & ((1 << bit) - 1))
 
@@ -167,9 +149,9 @@
     split_slots(join_slots(keep, got, axis, bit), axis, bit + 1, next_send, next_keep)
 
 
-def swap(values, axis, bit):
+def swap(values, axis, pattern, low):
     count = lax.axis_size(axis)
-    return lax.ppermute(values, axis, [(i, i ^ 1 << bit) for i in range(count)])
+    return lax.ppermute(values, axis, [(i, i ^ pattern << low) for i in range(count)])
 
 
 def route(keep, got, axis, after=None):
@@ -180,8 +162,69 @@
         send, keep = call(functools.partial(route_body, axis, bit), (send, half), [], keep, got)
         if after is not None:
             send, after = lax.optimization_barrier((send, after))
-        got = swap(send, axis, bit + 1)
+        got = swap(send, axis, 1, bit + 1)
     return keep, got
+
+
+def choose(mine, values):
+    out = values[0]
+    for m in range(1, len(values)):
+        out = jnp.where(mine == m, values[m], out)
+    return out
+
+
+def group_slots(count, low, width):
+    span = 1 << width
+    rests = [d for d in range(count) if (d >> low) % span == 0]
+    return [[rest | p << low for p in range(span)] for rest in rests]
+
+
+def my_bits(axis, low, width):
+    return lax.rem(lax.axis_index(axis) >> low, 1 << width)
+
+
+def part_slots(slots, axis, low, width, outs):
+    mine = my_bits(axis, low, width)
+    span = 1 << width
+    for at, group in enumerate(group_slots(len(slots), low, width)):
+        for v in range(span):
+            outs[v][at] = choose(mine, [slots[group[m ^ v]] for m in range(span)])
+
+
+def merge_slots(parts, count, axis, low, width):
+    mine = my_bits(axis, low, width)
+    span = 1 << width
+    slots = [None] * count
+    for at, group in enumerate(group_slots(count, low, width)):
+        for p in range(span):
+            slots[group[p]] = choose(mine, [parts[m ^ p][at] for m in range(span)])
+    return slots
+
+
+def stages(count):
+    bits = count.bit_length() - 1
+    return [(0, 1)] + [(low, min(2, bits - low)) for low in range(1, bits, 2)]
+
+
+def return_body(count, before, after, *refs):
+    parts, outs = refs[: 1 << before[1]], refs[1 << before[1] :]
+    part_slots(merge_slots(parts, count, "gy", *before), "gy", *after, outs)
+
+
+def send_back(parts, count):
+    plan = stages(count)
+    for i, stage in enumerate(plan):
+        parts = [parts[0]] + [swap(p, "gy", v, stage[0]) for v, p in enumerate(parts) if v]
+        if i + 1 < len(plan):
+            after = plan[i + 1]
+            piece = jax.ShapeDtypeStruct((count >> after[1],) + parts[0].shape[1:], F32)
+            parts = call(
+                functools.partial(return_body, count, stage, after),
+                (piece,) * (1 << after[1]),
+                [],
+                *parts,
+            )
+    return parts
 
 
 def records_out_body(n_gx, n_gy, cell, s_owner, obs, block, a_owner, ctrl, foot, send, keep, s_meta, a_meta, out):
@@ -285,7 +328,7 @@
     return centre, rim_tile(halo, group)
 
 
-def source_tile(n_gy, height, wide_y, records_in, planes, out, stacked, placing):
+def source_tile(n_gy, height, wide_y, records_in, planes, skip, out, stacked, placing, turned):
     records = n_gy * SLOT_ROWS
     blocks_y = wide_y // FY
     r_of, r_to = iota((records, records), 0), iota((records, records), 1)
@@ -300,7 +343,7 @@
     meta_t = meta.T
     block_row = meta_t[BLOCK_AT : BLOCK_AT + 1, :].astype(jnp.int32) - 1
     bz_row = block_row // blocks_y
-    foot_t = pick(unpack, records_in, ((1,), (1,)), 2)
+    turned[...] = pick(unpack, records_in, ((1,), (1,)), 2)
     block_col = meta[:, BLOCK_AT : BLOCK_AT + 1].astype(jnp.int32) - 1
     by = block_col % blocks_y
     usable = (block_col >= 0) & (
@@ -313,29 +356,30 @@
     wide_lane = iota((records, 2 * wide_y), 1)
     for fy in range(FY):
         placing[fy * records : (fy + 1) * records, :] = (wide_lane == start + fy).astype(BF16)
-    rows_out = len(planes) * height
+    rows_out = planes * height
     for s in range(2):
         force = meta_t[CTRL_AT + s : CTRL_AT + s + 1, :]
         for fy in range(FY):
             lanes = slice(fy * records, (fy + 1) * records)
-            for i, x in enumerate(planes):
-                scaled = foot_t[fy * 32 + x * FZ : fy * 32 + (x + 1) * FZ, :] * force
+            for i in range(planes):
+                at = pl.multiple_of(fy * 32 + (i + skip) * FZ, FZ)
+                scaled = turned[pl.ds(at, FZ), :] * force
                 for bz in range(height // FZ):
                     at = i * height + bz * FZ
                     stacked[at : at + FZ, lanes] = jnp.where(bz_row == bz, scaled, 0.0)
         value = spread(placing[...], stacked[:rows_out, :], count=2)
-        for i in range(len(planes)):
+        for i in range(planes):
             out[s, i] = value[i * height : (i + 1) * height]
     return meta, meta_t
 
 
-def own_source_body(n_gy, height, wide_y, got, source, foot_hot, foot_own, stacked, placing):
+def own_source_body(n_gy, height, wide_y, got, source, foot_hot, foot_own, stacked, placing, turned):
     records = n_gy * SLOT_ROWS
     blocks_y = wide_y // FY
     base = 3 * height
     records_in = got[base : base + records, :]
     meta, meta_t = source_tile(
-        n_gy, height, wide_y, records_in, range(FX), source, stacked, placing
+        n_gy, height, wide_y, records_in, FX, 0, source, stacked, placing, turned
     )
     held = n_gy * CAPA
     r_of, r_to = iota((held, records), 0), iota((held, records), 1)
@@ -358,12 +402,13 @@
                 foot_own[at : at + FZ, lanes] = jnp.where(bz_row == bz, piece, 0.0)
 
 
-def side_source_body(n_gy, height, wide_y, got_e, got_o, source, stacked, placing):
-    is_odd = lax.rem(lax.axis_index("gx"), 2) == 1
-    rows = slice(3 * height, 3 * height + n_gy * SLOT_ROWS)
-    low, high = low_high(got_e[rows, :], got_o[rows, :], is_odd)
-    for q, (records_in, planes) in enumerate(((low, range(1, FX)), (high, range(FX - 1)))):
-        source_tile(n_gy, height, wide_y, records_in, planes, source.at[q], stacked, placing)
+def side_source_body(n_gy, height, wide_y, low_parity, got, source, stacked, placing, turned):
+    is_low = lax.rem(lax.axis_index("gx"), 2) == low_parity
+    records_in = got[3 * height : 3 * height + n_gy * SLOT_ROWS, :]
+    skip = jnp.where(is_low, 1, 0)
+    source_tile(
+        n_gy, height, wide_y, records_in, FX - 1, skip, source, stacked, placing, turned
+    )
 
 
 def sensors_body(height, keep, got, spot_hot, lane_hot, z_hot, rim_hot, readings, table):
@@ -507,7 +552,7 @@
     return lambda x: low if x < FX else (lanes_in if x < 2 * FX else high)
 
 
-def forward_body(n_gx, n_gy, steps, coeffs, start, rim_target, own_source, side_source, spot_hot, lane_hot, z_hot, rim_hot, readings, target, final, sent, residuals, cur):
+def forward_body(n_gx, n_gy, steps, coeffs, start, rim_target, own_source, source_e, source_o, spot_hot, lane_hot, z_hot, rim_hot, readings, target, final, sent, residuals, cur):
     height = start.shape[2]
     wide = 3 * FX
     cells = FX * height
@@ -518,14 +563,17 @@
     fields = [start, cur.at[0], cur.at[1], cur.at[0], cur.at[1]]
     residuals[...] = jnp.zeros(residuals.shape, F32)
     live = (readings[8:9, :] > 0.5).astype(F32)
+    is_odd = lax.rem(lax.axis_index("gx"), 2) == 1
     lane_pair, rim_pair = paired(lane_hot[...]), paired(rim_hot[...])
     spots = spot_hot[...].astype(F32)
     heights = z_hot[...].astype(F32)
 
     def source(s, x):
         if x < FX:
-            return side_source[0, s, x - 1]
-        return own_source[s, x - FX] if x < 2 * FX else side_source[1, s, x - 2 * FX]
+            return jnp.where(is_odd, source_e[s, x - 1], source_o[s, x - 1])
+        if x < 2 * FX:
+            return own_source[s, x - FX]
+        return jnp.where(is_odd, source_o[s, x - 2 * FX], source_e[s, x - 2 * FX])
 
     for n in range(steps):
         before, after = fields[n], fields[n + 1]
@@ -594,7 +642,7 @@
                 puts[n, s, p, :, LANES:] = rim_tile(put_rim, s * FX + p)
 
 
-def adjoint_body(n_gx, n_gy, steps, coeffs, sent, sent_e, sent_o, own_puts, foot_hot, foot_own, gradient, second, cur, puts, summed):
+def adjoint_body(n_gx, n_gy, steps, coeffs, sent, sent_e, sent_o, own_puts, foot_hot, foot_own, back_keep, back_send, second, cur, puts, summed):
     is_odd = lax.rem(lax.axis_index("gx"), 2) == 1
     height = coeffs.shape[3]
     wide = 3 * FX
@@ -659,14 +707,17 @@
     seen = spread(foot_hot[...], summed[...], ((1,), (1,)), count=2)
     width = foot_own.shape[1]
     held = width // FY
-    out_row = iota((n_gy, width), 0)
-    out_from = iota((n_gy, width), 1) // CAPA
+    out_from = iota((1, width), 1) // CAPA
+    totals = []
     for s in range(2):
         row = jnp.sum(seen[s * cells : (s + 1) * cells] * foot_own[...], axis=0, keepdims=True)
         total = row
         for fy in range(1, FY):
             total = total + roll(row, -fy * held, 1)
-        gradient[:, s, :] = jnp.where(out_row == out_from, total, 0.0)
+        totals.append(total)
+    block = jnp.concatenate(totals + [jnp.zeros((6, width), F32)], axis=0)
+    slots = [jnp.where(out_from == d, block, 0.0) for d in range(n_gy)]
+    part_slots(slots, "gy", 0, 1, (back_keep, back_send))
 
 
 def adjoint_value(coeffs, field, s, x, shift):
@@ -686,13 +737,16 @@
             first[s, x - FX] = adjoint_value(coeffs, second, s, x, steps - 1)[:, :LANES]
 
 
-def returned_body(got, owner, out):
-    n_gy, _, records = got.shape
+def returned_body(n_gy, *refs):
+    low, width = stages(n_gy)[-1]
+    parts, (owner, out) = refs[: 1 << width], refs[1 << width :]
+    slots = merge_slots(parts, n_gy, "gy", low, width)
+    records = slots[0].shape[1]
     base = lax.axis_index("gy") * CAPA
     choice = slot_choices(owner[...], n_gy, CAPA)
     lane = iota((n_gy, records), 1)
     for s in range(2):
-        rows = got[:, s, :]
+        rows = jnp.concatenate([slot[s : s + 1] for slot in slots], axis=0)
         total = jnp.zeros(choice[0].shape, F32)
         for k in range(CAPA):
             column = jnp.sum(jnp.where(lane == base + k, rows, 0.0), axis=1, keepdims=True)
@@ -760,7 +814,7 @@
     )
     main_e, main_o = exchange(main, "gx")
     strips_e, strips_o = exchange(strips, "gy")
-    acts_keep, acts_got = route(acts_keep, swap(acts_send, "gy", 0), "gy")
+    acts_keep, acts_got = route(acts_keep, swap(acts_send, "gy", 1, 0), "gy")
     rim, rim_target, sens_keep = call(
         functools.partial(rim_body, n_gx),
         (
@@ -773,7 +827,11 @@
     )
     rim_e, rim_o = exchange(rim, "gx")
     held = n_gy * CAPA
-    scratch = [vmem((cells, FY * records), F32), vmem((FY * records, 2 * LANES), BF16)]
+    scratch = [
+        vmem((cells, FY * records), F32),
+        vmem((FY * records, 2 * LANES), BF16),
+        vmem((FOOT, records), F32),
+    ]
     own_source, foot_hot, foot_own = call(
         functools.partial(own_source_body, n_gy, height, wide_y),
         (
@@ -785,13 +843,16 @@
         rim,
         us=1.5,
     )
-    side_source = call(
-        functools.partial(side_source_body, n_gy, height, wide_y),
-        shape((2, 2, FX - 1, height, 2 * LANES), F32),
-        scratch,
-        rim_e, rim_o,
-        us=1.5,
-    )
+    source_e, source_o = [
+        call(
+            functools.partial(side_source_body, n_gy, height, wide_y, low_parity),
+            shape((2, FX - 1, height, 2 * LANES), F32),
+            scratch,
+            got,
+            us=0.8,
+        )
+        for low_parity, got in ((1, rim_e), (0, rim_o))
+    ]
     sens_keep, sens_got = route(sens_keep, rim_e, "gx", after=foot_hot)
     coeffs, start = call(
         coeffs_body,
@@ -827,7 +888,7 @@
             shape((16, slots), F32),
         ),
         [vmem((2, 2, wide, height, 2 * LANES), F32)],
-        coeffs, start, rim_target, own_source, side_source, *hots, readings, target,
+        coeffs, start, rim_target, own_source, source_e, source_o, *hots, readings, target,
         us=5.0,
     )
     sent_e, sent_o = exchange(sent, "gx")
@@ -838,10 +899,11 @@
         *hots, residuals,
         us=0.7,
     )
-    gradient, second = call(
+    back_keep, back_send, second = call(
         functools.partial(adjoint_body, n_gx, n_gy, steps),
         (
-            shape((n_gy, 2, FY * held), F32),
+            shape((n_gy // 2, 8, FY * held), F32),
+            shape((n_gy // 2, 8, FY * held), F32),
             shape((2, wide - 2 * steps + 2, height, 2 * LANES), F32),
         ),
         [
@@ -852,7 +914,7 @@
         coeffs, sent, sent_e, sent_o, own_puts, foot_hot, foot_own,
         us=4.0,
     )
-    back = lax.all_to_all(gradient, "gy", split_axis=0, concat_axis=0, tiled=True)
+    back = send_back([back_keep, back_send], n_gy)
     first = call(
         functools.partial(last_body, steps),
         shape((2, FX, height, LANES), F32),
@@ -860,7 +922,9 @@
         coeffs, second,
         us=1.0,
     )
-    returned = call(returned_body, shape((2, acts), F32), [], back, a_owner_row)
+    returned = call(
+        functools.partial(returned_body, n_gy), shape((2, acts), F32), [], *back, a_owner_row
+    )
     return (final, first, returned.T)
 
 

time: 55.7 us -> 54.2 us (0.973); the launches traced: 54.6 us -> 54 us
  waiting for transfers between devices: 11.4 us -> 15.8 us
  local copies, waits for them, and re-layouts: 3.39 us -> 0.05 us
  starting transfers between devices: 22.7 us -> 21.3 us
    all_to_all x1 -> x0, starting transfers between devices: 5.23 us -> none  [per_device(): lax.all_to_all(gradient, 'gy', split_axis=0, concat_axis=0, tiled=True)]
    ppermute x4 -> x8, waiting for transfers between devices: 1.23 us -> 5.8 us  [swap(): lax.ppermute(values, axis, [(i, i ^ pattern << low) for i in range(count)])]
    ppermute x4 -> x8, starting transfers between devices: 3.33 us -> 6.96 us  [swap(): lax.ppermute(values, axis, [(i, i ^ pattern << low) for i in range(count)])]
    unnamed x26 -> x22, local copies, waits for them, and re-layouts: 3.39 us -> 0.05 us
    pallas_call x15 -> x17, Pallas kernels: 14.9 us -> 14.6 us  [call(): pl.pallas_call(body, cost_estimate=pl.CostEstimate(flops=0, transcendenta...]
  transfers between devices with their start and end apart: 13 -> 16, of which waited for: 5 -> 7; matrix products, arithmetic and copies ran while one was open for 0% -> 0% of each run, Pallas kernels for 13% -> 13%
where the time goes in v3:
time: 54.2 us; the launch traced here: 54 us
  starting transfers between devices  21.3 us (39%)
  waiting for transfers between devices  15.8 us (29%)
  Pallas kernels  14.6 us (27%)
  other arithmetic  1.28 us (2%)
  between operations  1 us (2%)
    pallas_call x17, Pallas kernels, call(): pl.pallas_call(body, cost_estimate=pl.CostEstimate(flops=0, transcendenta...  14.6 us
    ppermute x8, starting transfers between devices, exchange(): return (lax.ppermute(values, axis, even), lax.ppermute(values, axis, odd))  14.3 us
    ppermute x8, waiting for transfers between devices, exchange(): return (lax.ppermute(values, axis, even), lax.ppermute(values, axis, odd))  9.96 us
    ppermute x8, starting transfers between devices, swap(): lax.ppermute(values, axis, [(i, i ^ pattern << low) for i in range(count)])  6.96 us
    ppermute x8, waiting for transfers between devices, swap(): lax.ppermute(values, axis, [(i, i ^ pattern << low) for i in range(count)])  5.8 us
    concatenate x1, other arithmetic, per_device(): jnp.concatenate([initial_state, eddy_diffusivity[None], velocity], axis=0)  1.28 us
  transfers between devices with their start and end apart: 16, of which 7 were waited for; matrix products, arithmetic and copies ran while one was open for 0% of the time, Pallas kernels for 13%

profile of v3, /device:TPU:20, one launch (start us, length us, event | category | flops | bytes accessed | tf_op | source)
XLA Modules:
  0.0 54.0 jit_solution(12435968094018357881)
XLA Ops:
  0.6 0.0 copy-start.1
  0.6 0.0 copy-start
  0.7 0.0 copy-start.3
  0.7 0.0 copy-start.6
  0.7 0.0 copy-start.8
  0.7 0.0 copy-start.9
  0.7 0.0 copy-start.5
  0.7 0.0 copy-start.10
  0.7 0.0 copy-start.7
  0.7 0.0 copy-start.4
  0.7 0.0 copy-start.2
  0.7 1.3 %pad_maximum_fusion.main = f32[6,4,48,128]{3,2,1,0:T(8,128)S(1)} fusion(f32[3,4,48,128]{3,2,1,0:T(8,128)} %vel.1, f32[1,4,48,128]{3,2,1,0:T(8,128)} %bitcast.8, f32[2,4,48,128]{3,2,1,0:T(8,128)} %state.1), kind=kLoop, calls=%fused_computation | loop fusion | flops 294912 | bytes 1179648 | tf_op jit(solution)/shard_map/concatenate | solution.py:782
  2.0 1.6 %collective-permute-start = (f32[6,4,48,128]{3,2,1,0:T(8,128)S(1)}, f32[6,4,48,128]{3,2,1,0:T(8,128)S(1)}, u32[]{:S(2)}, u32[]{:S(2)}) collective-permute-start(f32[6,4,48,128]{3,2,1,0:T(8,128)S(1)} %pad_maximum_fusion.main), channel_id=1, source_target_pairs={{0,8},{8,0},{16,24},{24,16},{1,9},{9,1},{17,25},{25,17},{2,10},{10... | collective-permute-start | bytes 1769480 | tf_op jit(solution)/shard_map/ppermute | solution.py:80
  3.7 1.9 %collective-permute-start.1 = (f32[6,4,48,128]{3,2,1,0:T(8,128)S(1)}, f32[6,4,48,128]{3,2,1,0:T(8,128)S(1)}, u32[]{:S(2)}, u32[]{:S(2)}) collective-permute-start(f32[6,4,48,128]{3,2,1,0:T(8,128)S(1)} %pad_maximum_fusion.main), channel_id=1, source_target_pairs={{8,16},{16,8},{9,17},{17,9},{10,18},{18,10},{11,19},{19,11},{12,20... | collective-permute-start | bytes 1769480 | tf_op jit(solution)/shard_map/ppermute | solution.py:80
  5.6 0.0 copy-done.6
  5.6 0.0 copy-done.8
  5.6 0.0 copy-done.9
  5.6 0.0 copy-done.5
  5.6 0.0 copy-done.10
  5.6 0.0 copy-done.7
  5.7 0.8 %shard_map.131 = (f32[96,128]{1,0:T(8,128)S(1)}, f32[4,24,128]{2,1,0:T(8,128)S(1)}) custom-call(s32[1,64]{1,0:T(1,128)S(1)} %bitcast.13, s32[1,64]{1,0:T(1,128)S(1)} %bitcast.14, f32[2,4,64]{2,1,0:T(4,128)S(1)} %bitcast.9, s32[1,16]{1,0:T(1,128)S(1)} %bitcast.15, s32[1,16]{1,0:T(1,128)S(1)} %bitcast.10, f32[2,16]{1,0:T(2,128)S(1)} %bitcast.12, ...), custom_call_target="tpu_custom_call" | custom-call | bytes 720000 | tf_op jit(solution)/shard_map/pallas_call | solution.py:88
  6.4 0.1 collective-permute-start.4
  6.5 1.2 %collective-permute-done.4.got = f32[96,128]{1,0:T(8,128)S(1)} collective-permute-done((f32[96,128]{1,0:T(8,128)S(1)}, f32[96,128]{1,0:T(8,128)S(1)}, u32[]{:S(2)}, u32[]{:S(2)}) %collective-permute-start.4) | collective-permute-done | bytes 49184 | tf_op jit(solution)/shard_map/ppermute | solution.py:154
  7.8 1.6 %collective-permute-start.5 = (f32[96,128]{1,0:T(8,128)S(1)}, f32[96,128]{1,0:T(8,128)S(1)}, u32[]{:S(2)}, u32[]{:S(2)}) collective-permute-start(f32[96,128]{1,0:T(8,128)S(1)} %get-tuple-element.40), channel_id=1, source_target_pairs={{0,2},{1,3},{2,0},{3,1},{4,6},{5,7},{6,4},{7,5},{8,10},{9,11},{10,... | collective-permute-start | bytes 147464 | tf_op jit(solution)/shard_map/ppermute | solution.py:154
  9.3 0.0 copy-done.2
  9.3 0.3 shard_map.130
  9.6 0.1 collective-permute-start.2
  9.7 2.5 %collective-permute-start.3 = (f32[192,128]{1,0:T(8,128)S(1)}, f32[192,128]{1,0:T(8,128)S(1)}, u32[]{:S(2)}, u32[]{:S(2)}) collective-permute-start(f32[192,128]{1,0:T(8,128)S(1)} %shard_map.130), channel_id=1, source_target_pairs={{1,2},{2,1},{3,4},{4,3},{5,6},{6,5},{9,10},{10,9},{11,12},{12,11},... | collective-permute-start | bytes 294920 | tf_op jit(solution)/shard_map/ppermute | solution.py:80
  12.2 0.0 collective-permute-done.5.got
  12.2 0.3 collective-permute-start.6
  12.5 0.0 collective-permute-done.2.even
  12.5 4.8 %collective-permute-done.3.odd = f32[192,128]{1,0:T(8,128)S(1)} collective-permute-done((f32[192,128]{1,0:T(8,128)S(1)}, f32[192,128]{1,0:T(8,128)S(1)}, u32[]{:S(2)}, u32[]{:S(2)}) %collective-permute-start.3) | collective-permute-done | bytes 98336 | tf_op jit(solution)/shard_map/ppermute | solution.py:80
  17.3 0.0 collective-permute-done.6.got
  17.3 0.1 shard_map.134
  17.4 0.1 collective-permute-start.7
  17.5 3.9 %collective-permute-start.8 = (f32[288,128]{1,0:T(8,128)S(1)}, f32[288,128]{1,0:T(8,128)S(1)}, u32[]{:S(2)}, u32[]{:S(2)}) collective-permute-start(f32[288,128]{1,0:T(8,128)S(1)} %get-tuple-element.43.rim.got), channel_id=1, source_target_pairs={{8,16},{16,8},{9,17},{17,9},{10,18},{18,10},{11,19},{19,11},{12,20... | collective-permute-start | bytes 442376 | tf_op jit(solution)/shard_map/ppermute | solution.py:80
  21.4 1.3 %shard_map.137 = (f32[2,4,48,256]{3,2,1,0:T(8,128)S(1)}, bf16[128,128]{1,0:T(8,128)(2,1)S(1)}, f32[192,128]{1,0:T(8,128)S(1)}) custom-call(f32[288,128]{1,0:T(8,128)S(1)} %get-tuple-element.43.rim.got), custom_call_target="tpu_custom_call" | custom-call | bytes 5400000 | tf_op jit(solution)/shard_map/pallas_call | solution.py:88
  22.7 0.0 collective-permute-done.7.rim_e.got
  22.7 1.4 %collective-permute-start.9 = (f32[16,128]{1,0:T(8,128)S(1)}, f32[16,128]{1,0:T(8,128)S(1)}, u32[]{:S(2)}, u32[]{:S(2)}) collective-permute-start(f32[16,128]{1,0:T(8,128)S(1)} %get-tuple-element.54), channel_id=1, source_target_pairs={{0,16},{8,24},{16,0},{24,8},{1,17},{9,25},{17,1},{25,9},{2,18},{10... | collective-permute-start | bytes 24584 | tf_op jit(solution)/shard_map/ppermute | solution.py:154
  24.1 0.9 %shard_map.138.source_e = f32[2,3,48,256]{3,2,1,0:T(8,128)S(1)} custom-call(f32[288,128]{1,0:T(8,128)S(1)} %collective-permute-done.7.rim_e.got), custom_call_target="tpu_custom_call" | custom-call | bytes 2880000 | tf_op jit(solution)/shard_map/pallas_call | solution.py:88
  25.0 0.0 collective-permute-done.8.rim_o.got
  25.0 0.9 %shard_map.139.source_o = f32[2,3,48,256]{3,2,1,0:T(8,128)S(1)} custom-call(f32[288,128]{1,0:T(8,128)S(1)} %collective-permute-done.8.rim_o.got), custom_call_target="tpu_custom_call" | custom-call | bytes 2880000 | tf_op jit(solution)/shard_map/pallas_call | solution.py:88
  25.9 0.0 collective-permute-done.main_e
  25.9 0.0 collective-permute-done.1.main_o
  25.9 1.5 %shard_map.135 = (f32[2,7,12,48,256]{4,3,2,1,0:T(8,128)S(1)}, f32[2,12,48,256]{3,2,1,0:T(8,128)S(1)}) custom-call(f32[6,4,48,128]{3,2,1,0:T(8,128)S(1)} %pad_maximum_fusion.main, f32[6,4,48,128]{3,2,1,0:T(8,128)S(1)} %collective-permute-done.main_e, f32[6,4,48,128]{3,2,1,0:T(8,128)S(1)} %collective-permute-done.1.main_o, ...), custom_call_target="tpu_custom_call" | custom-call | bytes 5760000 | tf_op jit(solution)/shard_map/pallas_call | solution.py:88
  27.5 0.0 collective-permute-done.9.got
  27.5 0.3 shard_map.140
  27.7 3.8 %shard_map.141 = (f32[2,4,48,128]{3,2,1,0:T(8,128)}, f32[456,128]{1,0:T(8,128)S(1)}, f32[16,384]{1,0:T(8,128)S(1)}) custom-call(f32[2,7,12,48,256]{4,3,2,1,0:T(8,128)S(1)} %get-tuple-element.44.coeffs, f32[2,12,48,256]{3,2,1,0:T(8,128)S(1)} %get-tuple-element.48.start, f32[48,128]{1,0:T(8,128)S(1)} %get-tuple-element.49.rim_target, ...), custom_call_target="tpu_custom_call" | custom-call | bytes 18000000 | tf_op jit(solution)/shard_map/pallas_call | solution.py:88
  31.5 2.0 %collective-permute-start.10 = (f32[456,128]{1,0:T(8,128)S(1)}, f32[456,128]{1,0:T(8,128)S(1)}, u32[]{:S(2)}, u32[]{:S(2)}) collective-permute-start(f32[456,128]{1,0:T(8,128)S(1)} %get-tuple-element.61.sent), channel_id=1, source_target_pairs={{0,8},{8,0},{16,24},{24,16},{1,9},{9,1},{17,25},{25,17},{2,10},{10... | collective-permute-start | bytes 700424 | tf_op jit(solution)/shard_map/ppermute | solution.py:80
  33.5 2.2 %collective-permute-start.11 = (f32[456,128]{1,0:T(8,128)S(1)}, f32[456,128]{1,0:T(8,128)S(1)}, u32[]{:S(2)}, u32[]{:S(2)}) collective-permute-start(f32[456,128]{1,0:T(8,128)S(1)} %get-tuple-element.61.sent), channel_id=1, source_target_pairs={{8,16},{16,8},{9,17},{17,9},{10,18},{18,10},{11,19},{19,11},{12,20... | collective-permute-start | bytes 700424 | tf_op jit(solution)/shard_map/ppermute | solution.py:80
  35.7 0.5 shard_map.142.own_puts
  36.3 1.3 %collective-permute-done.10.sent_e = f32[456,128]{1,0:T(8,128)S(1)} collective-permute-done((f32[456,128]{1,0:T(8,128)S(1)}, f32[456,128]{1,0:T(8,128)S(1)}, u32[]{:S(2)}, u32[]{:S(2)}) %collective-permute-start.10) | collective-permute-done | bytes 233504 | tf_op jit(solution)/shard_map/ppermute | solution.py:80
  37.6 3.9 %collective-permute-done.11.sent_o = f32[456,128]{1,0:T(8,128)S(1)} collective-permute-done((f32[456,128]{1,0:T(8,128)S(1)}, f32[456,128]{1,0:T(8,128)S(1)}, u32[]{:S(2)}, u32[]{:S(2)}) %collective-permute-start.11) | collective-permute-done | bytes 233504 | tf_op jit(solution)/shard_map/ppermute | solution.py:80
  41.5 2.6 %shard_map.143 = (f32[4,8,128]{2,1,0:T(8,128)S(1)}, f32[4,8,128]{2,1,0:T(8,128)S(1)}, f32[2,6,48,256]{3,2,1,0:T(8,128)S(1)}) custom-call(f32[2,7,12,48,256]{4,3,2,1,0:T(8,128)S(1)} %get-tuple-element.44.coeffs, f32[456,128]{1,0:T(8,128)S(1)} %get-tuple-element.61.sent, f32[456,128]{1,0:T(8,128)S(1)} %collective-permute-done.10.sent_e, ...), custom_call_target="tpu_custom_call" | custom-call | bytes 14400000 | tf_op jit(solution)/shard_map/pallas_call | solution.py:88
  44.1 0.1 collective-permute-start.12
  44.2 1.2 %collective-permute-done.12.refs_1_ = f32[4,8,128]{2,1,0:T(8,128)S(1)} collective-permute-done((f32[4,8,128]{2,1,0:T(8,128)S(1)}, f32[4,8,128]{2,1,0:T(8,128)S(1)}, u32[]{:S(2)}, u32[]{:S(2)}) %collective-permute-start.12) | collective-permute-done | bytes 16416 | tf_op jit(solution)/shard_map/ppermute | solution.py:154
  45.4 0.7 %collective-permute-start.13 = (f32[2,8,128]{2,1,0:T(8,128)S(1)}, f32[2,8,128]{2,1,0:T(8,128)S(1)}, u32[]{:S(2)}, u32[]{:S(2)}) collective-permute-start(f32[2,8,128]{2,1,0:T(8,128)S(1)} %get-tuple-element.68), channel_id=1, source_target_pairs={{0,2},{1,3},{2,0},{3,1},{4,6},{5,7},{6,4},{7,5},{8,10},{9,11},{10,... | collective-permute-start | bytes 24584 | tf_op jit(solution)/shard_map/ppermute | solution.py:154
  46.1 2.7 %collective-permute-start.14 = (f32[2,8,128]{2,1,0:T(8,128)S(1)}, f32[2,8,128]{2,1,0:T(8,128)S(1)}, u32[]{:S(2)}, u32[]{:S(2)}) collective-permute-start(f32[2,8,128]{2,1,0:T(8,128)S(1)} %get-tuple-element.69), channel_id=1, source_target_pairs={{0,4},{1,5},{2,6},{3,7},{4,0},{5,1},{6,2},{7,3},{8,12},{9,13},{10,... | collective-permute-start | bytes 24584 | tf_op jit(solution)/shard_map/ppermute | solution.py:154
  48.8 0.2 collective-permute-start.15
  48.9 1.0 %shard_map.144 = f32[2,4,48,128]{3,2,1,0:T(8,128)} custom-call(f32[2,7,12,48,256]{4,3,2,1,0:T(8,128)S(1)} %get-tuple-element.44.coeffs, f32[2,6,48,256]{3,2,1,0:T(8,128)S(1)} %get-tuple-element.64.second), custom_call_target="tpu_custom_call" | custom-call | bytes 3600000 | tf_op jit(solution)/shard_map/pallas_call | solution.py:88
  49.9 0.0 collective-permute-done.13.refs_1_
  49.9 0.5 collective-permute-done.14.refs_2_
  50.4 2.9 %collective-permute-done.15.refs_3_ = f32[2,8,128]{2,1,0:T(8,128)S(1)} collective-permute-done((f32[2,8,128]{2,1,0:T(8,128)S(1)}, f32[2,8,128]{2,1,0:T(8,128)S(1)}, u32[]{:S(2)}, u32[]{:S(2)}) %collective-permute-start.15) | collective-permute-done | bytes 8224 | tf_op jit(solution)/shard_map/ppermute | solution.py:154
  53.3 0.7 %shard_map.146 = f32[2,16]{1,0:T(2,128)} custom-call(f32[2,8,128]{2,1,0:T(8,128)S(1)} %get-tuple-element.67.refs_0_, f32[2,8,128]{2,1,0:T(8,128)S(1)} %collective-permute-done.13.refs_1_, f32[2,8,128]{2,1,0:T(8,128)S(1)} %collective-permute-done.14.refs_2_, f32[2,8,128]{2,1,0:T(8,128)S(1)} %collective-permute-done.15.refs_3_, s32[1,16]{1,0:T(1,128)S(1)} %bitcast.11), custom_call_target="tpu_custom_call" | custom-call | bytes 720000 | tf_op jit(solution)/shard_map/pallas_call | solution.py:88
  (8 shorter events, 0.1 us)
Async XLA Ops:
  0.6 8.7 %copy-start.1 = (f32[2,4,48,128]{3,2,1,0:T(8,128)S(1)}, f32[2,4,48,128]{3,2,1,0:T(8,128)}, u32[]{:S(2)}) copy-start(f32[2,4,48,128]{3,2,1,0:T(8,128)} %state.1) | copy-start | bytes 589828
  0.6 8.7 %copy-start = (f32[3,4,48,128]{3,2,1,0:T(8,128)S(1)}, f32[3,4,48,128]{3,2,1,0:T(8,128)}, u32[]{:S(2)}) copy-start(f32[3,4,48,128]{3,2,1,0:T(8,128)} %vel.1) | copy-start | bytes 884740
  0.7 8.7 %copy-start.3 = (f32[4,48,128]{2,1,0:T(8,128)S(1)}, f32[4,48,128]{2,1,0:T(8,128)}, u32[]{:S(2)}) copy-start(f32[4,48,128]{2,1,0:T(8,128)} %kappa.1) | copy-start | bytes 294916
  0.7 4.9 %copy-start.6 = (s32[16,1]{0,1:T(1,128)S(1)}, s32[16,1]{0,1:T(1,128)}, u32[]{:S(2)}) copy-start(s32[16,1]{0,1:T(1,128)} %param.19) | copy-start | bytes 196
  0.7 4.9 %copy-start.8 = (s32[64]{0:T(128)S(1)}, s32[64]{0:T(128)}, u32[]{:S(2)}) copy-start(s32[64]{0:T(128)} %param.15) | copy-start | bytes 772
  0.7 4.9 %copy-start.9 = (s32[64,1]{0,1:T(1,128)S(1)}, s32[64,1]{0,1:T(1,128)}, u32[]{:S(2)}) copy-start(s32[64,1]{0,1:T(1,128)} %param.16) | copy-start | bytes 772
  0.7 4.9 %copy-start.5 = (f32[64,2,4]{0,2,1:T(4,128)S(1)}, f32[64,2,4]{0,2,1:T(4,128)}, u32[]{:S(2)}) copy-start(f32[64,2,4]{0,2,1:T(4,128)} %param.17) | copy-start | bytes 6148
  0.7 4.9 %copy-start.10 = (s32[16]{0:T(128)S(1)}, s32[16]{0:T(128)}, u32[]{:S(2)}) copy-start(s32[16]{0:T(128)} %param.18) | copy-start | bytes 196
  0.7 4.9 %copy-start.7 = (f32[16,2]{0,1:T(2,128)S(1)}, f32[16,2]{0,1:T(2,128)}, u32[]{:S(2)}) copy-start(f32[16,2]{0,1:T(2,128)} %param.20) | copy-start | bytes 388
  0.7 4.9 %copy-start.4 = (f32[16,128]{1,0:T(8,128)S(1)}, f32[16,128]{1,0:T(8,128)}, u32[]{:S(2)}) copy-start(f32[16,128]{1,0:T(8,128)} %foot.1) | copy-start | bytes 24580
  0.7 8.6 %copy-start.2 = (f32[2,4,48,128]{3,2,1,0:T(8,128)S(1)}, f32[2,4,48,128]{3,2,1,0:T(8,128)}, u32[]{:S(2)}) copy-start(f32[2,4,48,128]{3,2,1,0:T(8,128)} %target.3) | copy-start | bytes 589828
  2.0 23.9 %collective-permute-start = (f32[6,4,48,128]{3,2,1,0:T(8,128)S(1)}, f32[6,4,48,128]{3,2,1,0:T(8,128)S(1)}, u32[]{:S(2)}, u32[]{:S(2)}) collective-permute-start(f32[6,4,48,128]{3,2,1,0:T(8,128)S(1)} %pad_maximum_fusion.main), channel_id=1, source_target_pairs={{0,8},{8,0},{16,24},{24,16},{1,9},{9,1},{17,25},{25,17},{2,10},{10... | collective-permute-start | bytes 1769480 | tf_op jit(solution)/shard_map/ppermute | solution.py:80
  3.7 22.2 %collective-permute-start.1 = (f32[6,4,48,128]{3,2,1,0:T(8,128)S(1)}, f32[6,4,48,128]{3,2,1,0:T(8,128)S(1)}, u32[]{:S(2)}, u32[]{:S(2)}) collective-permute-start(f32[6,4,48,128]{3,2,1,0:T(8,128)S(1)} %pad_maximum_fusion.main), channel_id=1, source_target_pairs={{8,16},{16,8},{9,17},{17,9},{10,18},{18,10},{11,19},{19,11},{12,20... | collective-permute-start | bytes 1769480 | tf_op jit(solution)/shard_map/ppermute | solution.py:80
  6.4 1.3 %collective-permute-start.4 = (f32[96,128]{1,0:T(8,128)S(1)}, f32[96,128]{1,0:T(8,128)S(1)}, u32[]{:S(2)}, u32[]{:S(2)}) collective-permute-start(f32[96,128]{1,0:T(8,128)S(1)} %get-tuple-element.38), channel_id=1, source_target_pairs={{0,1},{1,0},{2,3},{3,2},{4,5},{5,4},{6,7},{7,6},{8,9},{9,8},{10,11... | collective-permute-start | bytes 147464 | tf_op jit(solution)/shard_map/ppermute | solution.py:154
  7.8 4.4 %collective-permute-start.5 = (f32[96,128]{1,0:T(8,128)S(1)}, f32[96,128]{1,0:T(8,128)S(1)}, u32[]{:S(2)}, u32[]{:S(2)}) collective-permute-start(f32[96,128]{1,0:T(8,128)S(1)} %get-tuple-element.40), channel_id=1, source_target_pairs={{0,2},{1,3},{2,0},{3,1},{4,6},{5,7},{6,4},{7,5},{8,10},{9,11},{10,... | collective-permute-start | bytes 147464 | tf_op jit(solution)/shard_map/ppermute | solution.py:154
  9.6 2.9 %collective-permute-start.2 = (f32[192,128]{1,0:T(8,128)S(1)}, f32[192,128]{1,0:T(8,128)S(1)}, u32[]{:S(2)}, u32[]{:S(2)}) collective-permute-start(f32[192,128]{1,0:T(8,128)S(1)} %shard_map.130), channel_id=1, source_target_pairs={{0,1},{1,0},{2,3},{3,2},{4,5},{5,4},{6,7},{7,6},{8,9},{9,8},{10,11... | collective-permute-start | bytes 294920 | tf_op jit(solution)/shard_map/ppermute | solution.py:80
  9.7 7.6 %collective-permute-start.3 = (f32[192,128]{1,0:T(8,128)S(1)}, f32[192,128]{1,0:T(8,128)S(1)}, u32[]{:S(2)}, u32[]{:S(2)}) collective-permute-start(f32[192,128]{1,0:T(8,128)S(1)} %shard_map.130), channel_id=1, source_target_pairs={{1,2},{2,1},{3,4},{4,3},{5,6},{6,5},{9,10},{10,9},{11,12},{12,11},... | collective-permute-start | bytes 294920 | tf_op jit(solution)/shard_map/ppermute | solution.py:80
  12.2 5.1 %collective-permute-start.6 = (f32[96,128]{1,0:T(8,128)S(1)}, f32[96,128]{1,0:T(8,128)S(1)}, u32[]{:S(2)}, u32[]{:S(2)}) collective-permute-start(f32[96,128]{1,0:T(8,128)S(1)} %get-tuple-element.42), channel_id=1, source_target_pairs={{0,4},{1,5},{2,6},{3,7},{4,0},{5,1},{6,2},{7,3},{8,12},{9,13},{10,... | collective-permute-start | bytes 147464 | tf_op jit(solution)/shard_map/ppermute | solution.py:154
  17.4 5.3 %collective-permute-start.7 = (f32[288,128]{1,0:T(8,128)S(1)}, f32[288,128]{1,0:T(8,128)S(1)}, u32[]{:S(2)}, u32[]{:S(2)}) collective-permute-start(f32[288,128]{1,0:T(8,128)S(1)} %get-tuple-element.43.rim.got), channel_id=1, source_target_pairs={{0,8},{8,0},{16,24},{24,16},{1,9},{9,1},{17,25},{25,17},{2,10},{10... | collective-permute-start | bytes 442376 | tf_op jit(solution)/shard_map/ppermute | solution.py:80
  17.5 7.5 %collective-permute-start.8 = (f32[288,128]{1,0:T(8,128)S(1)}, f32[288,128]{1,0:T(8,128)S(1)}, u32[]{:S(2)}, u32[]{:S(2)}) collective-permute-start(f32[288,128]{1,0:T(8,128)S(1)} %get-tuple-element.43.rim.got), channel_id=1, source_target_pairs={{8,16},{16,8},{9,17},{17,9},{10,18},{18,10},{11,19},{19,11},{12,20... | collective-permute-start | bytes 442376 | tf_op jit(solution)/shard_map/ppermute | solution.py:80
  22.7 4.7 %collective-permute-start.9 = (f32[16,128]{1,0:T(8,128)S(1)}, f32[16,128]{1,0:T(8,128)S(1)}, u32[]{:S(2)}, u32[]{:S(2)}) collective-permute-start(f32[16,128]{1,0:T(8,128)S(1)} %get-tuple-element.54), channel_id=1, source_target_pairs={{0,16},{8,24},{16,0},{24,8},{1,17},{9,25},{17,1},{25,9},{2,18},{10... | collective-permute-start | bytes 24584 | tf_op jit(solution)/shard_map/ppermute | solution.py:154
  31.5 6.1 %collective-permute-start.10 = (f32[456,128]{1,0:T(8,128)S(1)}, f32[456,128]{1,0:T(8,128)S(1)}, u32[]{:S(2)}, u32[]{:S(2)}) collective-permute-start(f32[456,128]{1,0:T(8,128)S(1)} %get-tuple-element.61.sent), channel_id=1, source_target_pairs={{0,8},{8,0},{16,24},{24,16},{1,9},{9,1},{17,25},{25,17},{2,10},{10... | collective-permute-start | bytes 700424 | tf_op jit(solution)/shard_map/ppermute | solution.py:80
  33.5 7.9 %collective-permute-start.11 = (f32[456,128]{1,0:T(8,128)S(1)}, f32[456,128]{1,0:T(8,128)S(1)}, u32[]{:S(2)}, u32[]{:S(2)}) collective-permute-start(f32[456,128]{1,0:T(8,128)S(1)} %get-tuple-element.61.sent), channel_id=1, source_target_pairs={{8,16},{16,8},{9,17},{17,9},{10,18},{18,10},{11,19},{19,11},{12,20... | collective-permute-start | bytes 700424 | tf_op jit(solution)/shard_map/ppermute | solution.py:80
  44.1 1.2 %collective-permute-start.12 = (f32[4,8,128]{2,1,0:T(8,128)S(1)}, f32[4,8,128]{2,1,0:T(8,128)S(1)}, u32[]{:S(2)}, u32[]{:S(2)}) collective-permute-start(f32[4,8,128]{2,1,0:T(8,128)S(1)} %get-tuple-element.66), channel_id=1, source_target_pairs={{0,1},{1,0},{2,3},{3,2},{4,5},{5,4},{6,7},{7,6},{8,9},{9,8},{10,11... | collective-permute-start | bytes 49160 | tf_op jit(solution)/shard_map/ppermute | solution.py:154
  45.4 4.5 %collective-permute-start.13 = (f32[2,8,128]{2,1,0:T(8,128)S(1)}, f32[2,8,128]{2,1,0:T(8,128)S(1)}, u32[]{:S(2)}, u32[]{:S(2)}) collective-permute-start(f32[2,8,128]{2,1,0:T(8,128)S(1)} %get-tuple-element.68), channel_id=1, source_target_pairs={{0,2},{1,3},{2,0},{3,1},{4,6},{5,7},{6,4},{7,5},{8,10},{9,11},{10,... | collective-permute-start | bytes 24584 | tf_op jit(solution)/shard_map/ppermute | solution.py:154
  46.1 4.3 %collective-permute-start.14 = (f32[2,8,128]{2,1,0:T(8,128)S(1)}, f32[2,8,128]{2,1,0:T(8,128)S(1)}, u32[]{:S(2)}, u32[]{:S(2)}) collective-permute-start(f32[2,8,128]{2,1,0:T(8,128)S(1)} %get-tuple-element.69), channel_id=1, source_target_pairs={{0,4},{1,5},{2,6},{3,7},{4,0},{5,1},{6,2},{7,3},{8,12},{9,13},{10,... | collective-permute-start | bytes 24584 | tf_op jit(solution)/shard_map/ppermute | solution.py:154
  48.8 4.5 %collective-permute-start.15 = (f32[2,8,128]{2,1,0:T(8,128)S(1)}, f32[2,8,128]{2,1,0:T(8,128)S(1)}, u32[]{:S(2)}, u32[]{:S(2)}) collective-permute-start(f32[2,8,128]{2,1,0:T(8,128)S(1)} %get-tuple-element.70), channel_id=1, source_target_pairs={{0,6},{1,7},{2,4},{3,5},{4,2},{5,3},{6,0},{7,1},{8,14},{9,15},{10,... | collective-permute-start | bytes 24584 | tf_op jit(solution)/shard_map/ppermute | solution.py:154

commit v4 on v3

--- a/solution.py
+++ b/solution.py
@@ -309,23 +309,47 @@
 
 def rim_tile(packed, group):
     lane = iota(packed.shape, 1)
-    right = roll(packed, -2 * RIM * group, 1)
-    left = roll(packed, LANES - 2 * RIM - 2 * RIM * group, 1)
+    if isinstance(group, int):
+        right = roll(packed, -2 * RIM * group, 1)
+        left = roll(packed, LANES - 2 * RIM - 2 * RIM * group, 1)
+    else:
+        right = pltpu.roll(packed, lax.rem(LANES - 2 * RIM * group, LANES), 1)
+        left = pltpu.roll(packed, LANES - 2 * RIM - 2 * RIM * group, 1)
     return jnp.where(lane < RIM, right, jnp.where(lane >= LANES - RIM, left, 0.0))
 
 
-def extended(field, main, main_e, main_o, rim, rim_e, rim_o, is_odd, x):
+def x_odd():
+    return lax.rem(lax.axis_index("gx"), 2) == 1
+
+
+def flip(plane):
+    return jnp.where(x_odd(), plane, FX - 1 - plane)
+
+
+class planes:
+    def __init__(self, axis, *parts):
+        self.axis, self.parts = axis, parts
+
+    def find(self, key):
+        at = key[self.axis]
+        for ref, first in self.parts:
+            if first <= at < first + ref.shape[self.axis]:
+                return ref, key[: self.axis] + (at - first,) + key[self.axis + 1 :]
+
+    def __getitem__(self, key):
+        ref, key = self.find(key)
+        return ref[key]
+
+    def __setitem__(self, key, value):
+        ref, key = self.find(key)
+        ref[key] = value
+
+
+def extended(field, main, rim, w):
     height = main.shape[2]
-    at, group = pl.ds(field // 2 * height, height), (field % 2) * FX + x % FX
-    if x // FX == 1:
-        centre, halo = main[field, x % FX], rim[at]
-    elif x // FX == 0:
-        centre = jnp.where(is_odd, main_e[field, x], main_o[field, x])
-        halo = jnp.where(is_odd, rim_e[at], rim_o[at])
-    else:
-        centre = jnp.where(is_odd, main_o[field, x - 2 * FX], main_e[field, x - 2 * FX])
-        halo = jnp.where(is_odd, rim_o[at], rim_e[at])
-    return centre, rim_tile(halo, group)
+    p = flip(w % FX)
+    rows = slice(field // 2 * height, (field // 2 + 1) * height)
+    return main[field, p], rim_tile(rim[rows, :], (field % 2) * FX + p)
 
 
 def source_tile(n_gy, height, wide_y, records_in, planes, skip, out, stacked, placing, turned):
@@ -497,26 +521,29 @@
     return packed
 
 
-def coeffs_body(main, main_e, main_o, rim, rim_e, rim_o, coeffs, start, half_k):
-    refs = (main, main_e, main_o, rim, rim_e, rim_o)
-    is_odd = lax.rem(lax.axis_index("gx"), 2) == 1
-    wide = 3 * FX
+def coeffs_body(first, last, sources, *refs):
+    count = 2 * len(sources)
+    ins, (coeffs, start, half_k) = refs[:count], refs[count:]
+    main_of = {at: (ins[2 * i], ins[2 * i + 1]) for i, at in enumerate(sources)}
     height = half_k.shape[1]
-    shape = (height, 2 * LANES)
-    z = iota(shape, 0)
-    for x in range(wide):
-        centre, halo = extended(2, *refs, is_odd, x)
-        half_k[x, :, :LANES] = 0.5 * centre
-        half_k[x, :, LANES:] = 0.5 * halo
+    z = iota((height, 2 * LANES), 0)
+    sign = jnp.where(x_odd(), 0.5, -0.5)
+    lowest, highest = sources[0] * FX, sources[-1] * FX + FX - 1
+    for w in range(max(lowest, first - 1), min(highest, last + 1) + 1):
+        centre, halo = extended(2, *main_of[w // FX], w)
+        half_k[w, :, :LANES] = 0.5 * centre
+        half_k[w, :, LANES:] = 0.5 * halo
+    for i in range(start.shape[1]):
+        w = start_first(first) + i
         for s in range(2):
-            centre, halo = extended(s, *refs, is_odd, x)
-            start[s, x, :, :LANES] = centre
-            start[s, x, :, LANES:] = halo
-    for x in range(wide):
-        k = half_k[x]
+            centre, halo = extended(s, *main_of[w // FX], w)
+            start[s, i, :, :LANES] = centre
+            start[s, i, :, LANES:] = halo
+    for w in range(first, last + 1):
+        k = half_k[w]
         faces = (
-            k + half_k[min(x + 1, wide - 1)],
-            k + half_k[max(x - 1, 0)],
+            k + half_k[min(w + 1, highest)],
+            k + half_k[max(w - 1, lowest)],
             k + roll(k, -1, 1),
             k + roll(k, 1, 1),
             k + jnp.where(z == height - 1, 0.0, roll(k, -1, 0)),
@@ -525,10 +552,11 @@
         total = (faces[0] + faces[1]) + (faces[2] + faces[3]) + (faces[4] + faces[5])
         drift = []
         for axis in range(3):
-            centre, halo = extended(3 + axis, *refs, is_odd, x)
-            drift.append(0.5 * jnp.concatenate([centre, halo], axis=1))
+            centre, halo = extended(3 + axis, *main_of[w // FX], w)
+            drift.append((0.5 if axis else sign) * jnp.concatenate([centre, halo], axis=1))
+        at = w - first
         for s in range(2):
-            coeffs[s, 6, x] = 1.0 - SCALES[s] * total
+            coeffs[s, 6, at] = 1.0 - SCALES[s] * total
             for face in range(6):
                 value = faces[face] if s == 0 else SCALES[s] * faces[face]
                 value = value - drift[face // 2] if face % 2 == 0 else value + drift[face // 2]
@@ -536,7 +564,11 @@
                     value = jnp.where(z == height - 1, 0.0, value)
                 if face == 5:
                     value = jnp.where(z == 0, 0.0, value)
-                coeffs[s, face, x] = value
+                coeffs[s, face, at] = value
+
+
+def start_first(first):
+    return 0 if first == 0 else 2 * FX
 
 
 def inside_rows(n_gx, n_gy):
@@ -547,33 +579,24 @@
         | ((lane < LANES + RIM) & (col_id < n_gy - 1))
         | ((lane >= 2 * LANES - RIM) & (col_id > 0))
     ).astype(F32)
-    low = jnp.where(row_id > 0, lanes_in, 0.0)
-    high = jnp.where(row_id < n_gx - 1, lanes_in, 0.0)
-    return lambda x: low if x < FX else (lanes_in if x < 2 * FX else high)
-
-
-def forward_body(n_gx, n_gy, steps, coeffs, start, rim_target, own_source, source_e, source_o, spot_hot, lane_hot, z_hot, rim_hot, readings, target, final, sent, residuals, cur):
-    height = start.shape[2]
+    beyond = jnp.where(x_odd(), row_id < n_gx - 1, row_id > 0)
+    far = jnp.where(beyond, lanes_in, 0.0)
+    return lambda w: lanes_in if w < 2 * FX else far
+
+
+def forward_body(n_gx, n_gy, steps, coeffs_e, coeffs_o, start_e, start_o, rim_target, own_source, source_e, source_o, spot_hot, lane_hot, z_hot, rim_hot, readings, target, final, sent, residuals, cur, kept):
     wide = 3 * FX
-    cells = FX * height
-    slots = readings.shape[1]
-    own = slots // 3
-    rest = slots - own
     inside = inside_rows(n_gx, n_gy)
+    coeffs = planes(2, (coeffs_e, 0), (coeffs_o, coeffs_e.shape[2]))
+    start = planes(1, (start_e, 0), (start_o, 2 * FX))
     fields = [start, cur.at[0], cur.at[1], cur.at[0], cur.at[1]]
-    residuals[...] = jnp.zeros(residuals.shape, F32)
-    live = (readings[8:9, :] > 0.5).astype(F32)
-    is_odd = lax.rem(lax.axis_index("gx"), 2) == 1
-    lane_pair, rim_pair = paired(lane_hot[...]), paired(rim_hot[...])
-    spots = spot_hot[...].astype(F32)
-    heights = z_hot[...].astype(F32)
-
-    def source(s, x):
-        if x < FX:
-            return jnp.where(is_odd, source_e[s, x - 1], source_o[s, x - 1])
-        if x < 2 * FX:
-            return own_source[s, x - FX]
-        return jnp.where(is_odd, source_o[s, x - 2 * FX], source_e[s, x - 2 * FX])
+
+    def source(s, w):
+        if w < FX:
+            return source_e[s, jnp.where(x_odd(), w - 1, FX - 1 - w)]
+        if w < 2 * FX:
+            return own_source[s, flip(w - FX)]
+        return source_o[s, jnp.where(x_odd(), w - 2 * FX, 3 * FX - 2 - w)]
 
     for n in range(steps):
         before, after = fields[n], fields[n + 1]
@@ -588,12 +611,34 @@
                 value = value + coeffs[s, 3, x] * roll(c, 1, 1)
                 value = value + coeffs[s, 4, x] * roll(c, -1, 0)
                 value = value + coeffs[s, 5, x] * roll(c, 1, 0)
-                after[s, x] = value * row
+                value = value * row
+                if n < steps - 1:
+                    after[s, x] = value
+                if FX <= x < 2 * FX:
+                    kept[n, s, flip(x - FX)] = value
+    misfits(
+        steps, kept, rim_target, spot_hot, lane_hot, z_hot, rim_hot, readings, target, sent, residuals
+    )
+    final[...] = kept[steps - 1, :, :, :, :LANES]
+
+
+def misfits(steps, kept, rim_target, spot_hot, lane_hot, z_hot, rim_hot, readings, target, sent, residuals):
+    height = kept.shape[3]
+    cells = FX * height
+    slots = readings.shape[1]
+    own = slots // 3
+    rest = slots - own
+    residuals[...] = jnp.zeros(residuals.shape, F32)
+    live = (readings[8:9, :] > 0.5).astype(F32)
+    lane_pair, rim_pair = paired(lane_hot[...]), paired(rim_hot[...])
+    spots = spot_hot[...].astype(F32)
+    heights = z_hot[...].astype(F32)
+    for n in range(steps):
         both = jnp.concatenate(
-            [after[s, FX : 2 * FX, :, :LANES].reshape(cells, LANES) for s in range(2)], axis=1
+            [kept[n, s, :, :, :LANES].reshape(cells, LANES) for s in range(2)], axis=1
         )
         seen = spread(lane_pair, both)
-        packed = pack_rims([after[s, FX + p, :, LANES:] for s in range(2) for p in range(FX)])
+        packed = pack_rims([kept[n, s, p, :, LANES:] for s in range(2) for p in range(FX)])
         seen_rim = spread(rim_pair, packed)
         for s in range(2):
             at = s * steps + n
@@ -604,15 +649,13 @@
             value = (value - readings[at : at + 1, own:]) * live[:, own:]
             residuals[at : at + 1, own:] = value
     residuals[8:16, :] = readings[8:16, :]
-    last = fields[steps]
     ends = [residuals[s * steps + steps - 1 : (s + 1) * steps, :] for s in range(2)]
     put = inject(spot_hot[...], lane_hot[...], [end[:, :own] for end in ends])
     put_rim = inject(z_hot[...], rim_hot[...], [end[:, own:] for end in ends])
     for s in range(2):
         for p in range(FX):
             rows = slice(p * height, (p + 1) * height)
-            got = last[s, FX + p, :, :LANES]
-            final[s, p] = got
+            got = kept[steps - 1, s, p, :, :LANES]
             g = s * FX + p
             sent[g * height : (g + 1) * height, :] = (
                 got - target[s, p] + put[rows, s * LANES : (s + 1) * LANES]
@@ -627,83 +670,89 @@
             sent[base + 8 * part + i : base + 8 * part + i + 1, :] = values
 
 
-def own_puts_body(steps, spot_hot, lane_hot, z_hot, rim_hot, residuals, puts):
+def unpack_fields(sent, fields):
+    height = fields.shape[2]
+    base = 2 * FX * height
+    packed = sent[base : base + height, :]
+    for s in range(2):
+        for p in range(FX):
+            g = s * FX + p
+            fields[s, flip(p), :, :LANES] = sent[g * height : (g + 1) * height, :]
+            fields[s, flip(p), :, LANES:] = rim_tile(packed, g)
+
+
+def own_adjoint_body(steps, spot_hot, lane_hot, z_hot, rim_hot, residuals, sent, puts, fields):
+    unpack_fields(sent, fields)
     slots = residuals.shape[1]
     own = slots // 3
-    _, _, planes, height, _ = puts.shape
+    height = puts.shape[3]
     for n in range(steps - 1):
         values = [residuals[s * steps + n : s * steps + n + 1, :] for s in range(2)]
         put = inject(spot_hot[...], lane_hot[...], [value[:, :own] for value in values])
         put_rim = inject(z_hot[...], rim_hot[...], [value[:, own:] for value in values])
         for s in range(2):
-            for p in range(planes):
+            for p in range(FX):
                 rows = slice(p * height, (p + 1) * height)
-                puts[n, s, p, :, :LANES] = put[rows, s * LANES : (s + 1) * LANES]
-                puts[n, s, p, :, LANES:] = rim_tile(put_rim, s * FX + p)
-
-
-def adjoint_body(n_gx, n_gy, steps, coeffs, sent, sent_e, sent_o, own_puts, foot_hot, foot_own, back_keep, back_send, second, cur, puts, summed):
-    is_odd = lax.rem(lax.axis_index("gx"), 2) == 1
-    height = coeffs.shape[3]
+                puts[n, s, flip(p), :, :LANES] = put[rows, s * LANES : (s + 1) * LANES]
+                puts[n, s, flip(p), :, LANES:] = rim_tile(put_rim, s * FX + p)
+
+
+def side_adjoint_body(steps, low_parity, sent, puts, fields):
+    unpack_fields(sent, fields)
+    height = puts.shape[3]
+    cells = FX * height
+    table = 2 * cells + height
+    slots = (sent.shape[0] - table) // 8 * LANES
+    own = slots // 3
+    is_low = lax.rem(lax.axis_index("gx"), 2) == low_parity
+    rows = jnp.concatenate(
+        [sent[table + 8 * i : table + 8 * i + 8, :] for i in range(slots // LANES)], axis=1
+    )
+    cell = rows[7:8, :].astype(jnp.int32) - 1
+    spot, lane = own_hot(cell[:, :own], height)
+    z, rim = rim_hot_pair(cell[:, own:], height)
+    for n in range(steps - 1):
+        reach = (n + 1) * height
+        near = jnp.where(is_low, spot[cells - reach :].astype(F32), spot[:reach].astype(F32))
+        values = [rows[s * (steps - 1) + n : s * (steps - 1) + n + 1, :] for s in range(2)]
+        put = inject(near.astype(BF16), lane, [value[:, :own] for value in values])
+        put_rim = inject(z, rim, [value[:, own:] for value in values])
+        for s in range(2):
+            for i in range(n + 1):
+                p = jnp.where(is_low, FX - n - 1 + i, i)
+                puts[n, s, flip(p), :, :LANES] = put[
+                    i * height : (i + 1) * height, s * LANES : (s + 1) * LANES
+                ]
+                puts[n, s, flip(p), :, LANES:] = rim_tile(put_rim, s * FX + p)
+
+
+def adjoint_body(n_gx, n_gy, steps, coeffs_e, coeffs_o, puts_own, fields_own, puts_e, fields_e, puts_o, fields_o, foot_hot, foot_own, back_keep, back_send, second, cur, summed):
+    height = coeffs_e.shape[3]
     wide = 3 * FX
     cells = FX * height
-    base = 2 * FX * height
-    table = base + height
-    slots = (sent.shape[0] - table) // 8 * LANES
-    own = slots // 3
     inside = inside_rows(n_gx, n_gy)
-    for q in (1, 0, 2):
-        def take(lo, hi):
-            if q == 1:
-                return sent[lo:hi, :]
-            if q == 0:
-                return jnp.where(is_odd, sent_e[lo:hi, :], sent_o[lo:hi, :])
-            return jnp.where(is_odd, sent_o[lo:hi, :], sent_e[lo:hi, :])
-        packed_rim = take(base, base + height)
-        for s in range(2):
-            for p in range(FX):
-                g = s * FX + p
-                cur[0, s, q * FX + p, :, :LANES] = take(g * height, (g + 1) * height)
-                cur[0, s, q * FX + p, :, LANES:] = rim_tile(packed_rim, g)
-        if q == 1:
-            continue
-        rows = jnp.concatenate(
-            [take(table + 8 * i, table + 8 * i + 8) for i in range(slots // LANES)], axis=1
-        )
-        cell = rows[7:8, :].astype(jnp.int32) - 1
-        spot, lane = own_hot(cell[:, :own], height)
-        z, rim = rim_hot_pair(cell[:, own:], height)
-        for n in range(steps - 1):
-            reach = (n + 1) * height
-            part = slice(cells - reach, cells) if q == 0 else slice(0, reach)
-            first = FX - n - 1 if q == 0 else 0
-            values = [rows[s * (steps - 1) + n : s * (steps - 1) + n + 1, :] for s in range(2)]
-            put = inject(spot[part], lane, [value[:, :own] for value in values])
-            put_rim = inject(z, rim, [value[:, own:] for value in values])
-            for s in range(2):
-                for i in range(n + 1):
-                    x = q * FX + first + i
-                    puts[n, s, x, :, :LANES] = put[
-                        i * height : (i + 1) * height, s * LANES : (s + 1) * LANES
-                    ]
-                    puts[n, s, x, :, LANES:] = rim_tile(put_rim, s * FX + first + i)
+    coeffs = planes(2, (coeffs_e, 0), (coeffs_o, coeffs_e.shape[2]))
+    puts = planes(2, (puts_e, 0), (puts_own, FX), (puts_o, 2 * FX))
+    start = planes(1, (fields_e, 0), (fields_own, FX), (fields_o, 2 * FX))
     for s in range(2):
-        summed[s * cells : (s + 1) * cells, :] = sent[s * cells : (s + 1) * cells, :]
+        for p in range(FX):
+            at = s * cells + p * height
+            summed[at : at + height, :] = fields_own[s, flip(p), :, :LANES]
     for turn in range(steps - 1):
-        now, later = turn % 2, (turn + 1) % 2
+        field = start if turn == 0 else cur.at[turn % 2]
         n = steps - 2 - turn
         for x in range(turn + 1, wide - turn - 1):
             for s in range(2):
-                put = own_puts[n, s, x - FX] if FX <= x < 2 * FX else puts[n, s, x]
-                value = adjoint_value(coeffs, cur.at[now], s, x, 0) + put
+                value = adjoint_value(coeffs, field, s, x, 0) + puts[n, s, x]
                 value = value * inside(x)
                 if turn == steps - 2:
                     second[s, x - steps + 1] = value
                 else:
-                    cur[later, s, x] = value
+                    cur[(turn + 1) % 2, s, x] = value
                 if FX <= x < 2 * FX:
-                    at = s * cells + (x - FX) * height
-                    summed[at : at + height, :] = summed[at : at + height, :] + value[:, :LANES]
+                    at = pl.multiple_of(s * cells + flip(x - FX) * height, 8)
+                    rows = pl.ds(at, height)
+                    summed[rows, :] = summed[rows, :] + value[:, :LANES]
     seen = spread(foot_hot[...], summed[...], ((1,), (1,)), count=2)
     width = foot_own.shape[1]
     held = width // FY
@@ -731,10 +780,11 @@
     return value + roll(coeffs[s, 4, x] * w, 1, 0)
 
 
-def last_body(steps, coeffs, second, first):
+def last_body(steps, coeffs_e, coeffs_o, second, first):
+    coeffs = planes(2, (coeffs_e, 0), (coeffs_o, coeffs_e.shape[2]))
     for x in range(FX, 2 * FX):
         for s in range(2):
-            first[s, x - FX] = adjoint_value(coeffs, second, s, x, steps - 1)[:, :LANES]
+            first[s, flip(x - FX)] = adjoint_value(coeffs, second, s, x, steps - 1)[:, :LANES]
 
 
 def returned_body(n_gy, *refs):
@@ -843,28 +893,44 @@
         rim,
         us=1.5,
     )
-    source_e, source_o = [
-        call(
-            functools.partial(side_source_body, n_gy, height, wide_y, low_parity),
-            shape((2, FX - 1, height, 2 * LANES), F32),
-            scratch,
-            got,
-            us=0.8,
-        )
-        for low_parity, got in ((1, rim_e), (0, rim_o))
-    ]
-    sens_keep, sens_got = route(sens_keep, rim_e, "gx", after=foot_hot)
-    coeffs, start = call(
-        coeffs_body,
+    split = 2 * FX - 1
+    coeffs_e, start_e = call(
+        functools.partial(coeffs_body, 0, split - 1, (0, 1)),
         (
-            shape((2, 7, wide, height, 2 * LANES), F32),
-            shape((2, wide, height, 2 * LANES), F32),
+            shape((2, 7, split, height, 2 * LANES), F32),
+            shape((2, 2 * FX, height, 2 * LANES), F32),
         ),
         [vmem((wide, height, 2 * LANES), F32)],
-        main, main_e, main_o, rim, rim_e, rim_o,
-        us=1.6,
-    )
-    sens_keep, start = lax.optimization_barrier((sens_keep, start))
+        main_e, rim_e, main, rim,
+        us=1.0,
+    )
+    source_e = call(
+        functools.partial(side_source_body, n_gy, height, wide_y, 1),
+        shape((2, FX - 1, height, 2 * LANES), F32),
+        scratch,
+        rim_e,
+        us=0.9,
+    )
+    rim_o, start_e, source_e = lax.optimization_barrier((rim_o, start_e, source_e))
+    source_o = call(
+        functools.partial(side_source_body, n_gy, height, wide_y, 0),
+        shape((2, FX - 1, height, 2 * LANES), F32),
+        scratch,
+        rim_o,
+        us=0.9,
+    )
+    sens_keep, sens_got = route(sens_keep, rim_e, "gx", after=foot_hot)
+    coeffs_o, start_o = call(
+        functools.partial(coeffs_body, split, wide - 1, (1, 2)),
+        (
+            shape((2, 7, wide - split, height, 2 * LANES), F32),
+            shape((2, FX, height, 2 * LANES), F32),
+        ),
+        [vmem((wide, height, 2 * LANES), F32)],
+        main, rim, main_o, rim_o,
+        us=0.7,
+    )
+    sens_keep, start_o = lax.optimization_barrier((sens_keep, start_o))
     own_slots = slots // 3
     rest = slots - own_slots
     *hots, readings = call(
@@ -887,18 +953,25 @@
             shape((sent_rows, LANES), F32),
             shape((16, slots), F32),
         ),
-        [vmem((2, 2, wide, height, 2 * LANES), F32)],
-        coeffs, start, rim_target, own_source, source_e, source_o, *hots, readings, target,
+        [
+            vmem((2, 2, wide, height, 2 * LANES), F32),
+            vmem((steps, 2, FX, height, 2 * LANES), F32),
+        ],
+        coeffs_e, coeffs_o, start_e, start_o, rim_target, own_source, source_e, source_o, *hots, readings, target,
         us=5.0,
     )
     sent_e, sent_o = exchange(sent, "gx")
-    own_puts = call(
-        functools.partial(own_puts_body, steps),
+    side = (
         shape((steps - 1, 2, FX, height, 2 * LANES), F32),
-        [],
-        *hots, residuals,
-        us=0.7,
-    )
+        shape((2, FX, height, 2 * LANES), F32),
+    )
+    own_side = call(
+        functools.partial(own_adjoint_body, steps), side, [], *hots, residuals, sent, us=0.7
+    )
+    even_side, odd_side = [
+        call(functools.partial(side_adjoint_body, steps, parity), side, [], got, us=0.5)
+        for parity, got in ((1, sent_e), (0, sent_o))
+    ]
     back_keep, back_send, second = call(
         functools.partial(adjoint_body, n_gx, n_gy, steps),
         (
@@ -906,20 +979,16 @@
             shape((n_gy // 2, 8, FY * held), F32),
             shape((2, wide - 2 * steps + 2, height, 2 * LANES), F32),
         ),
-        [
-            vmem((2, 2, wide, height, 2 * LANES), F32),
-            vmem((steps - 1, 2, wide, height, 2 * LANES), F32),
-            vmem((2 * cells, LANES), F32),
-        ],
-        coeffs, sent, sent_e, sent_o, own_puts, foot_hot, foot_own,
-        us=4.0,
+        [vmem((2, 2, wide, height, 2 * LANES), F32), vmem((2 * cells, LANES), F32)],
+        coeffs_e, coeffs_o, *own_side, *even_side, *odd_side, foot_hot, foot_own,
+        us=3.0,
     )
     back = send_back([back_keep, back_send], n_gy)
     first = call(
         functools.partial(last_body, steps),
         shape((2, FX, height, LANES), F32),
         [],
-        coeffs, second,
+        coeffs_e, coeffs_o, second,
         us=1.0,
     )
     returned = call(

time: 54.2 us -> 53.5 us (0.987)
  waiting for transfers between devices: 15.8 us -> 13.9 us
  Pallas kernels: 14.6 us -> 15.5 us
    ppermute x8, waiting for transfers between devices: 9.96 us -> 8.5 us  [exchange(): return (lax.ppermute(values, axis, even), lax.ppermute(values, axis, odd))]
    pallas_call x17 -> x20, Pallas kernels: 14.6 us -> 15.5 us  [call(): pl.pallas_call(body, cost_estimate=pl.CostEstimate(flops=0, transcendenta...]
  transfers between devices with their start and end apart: 16 -> 16, of which waited for: 7 -> 7; matrix products, arithmetic and copies ran while one was open for 0% -> 0% of each run, Pallas kernels for 13% -> 15%
where the time goes in v4:
time: 53.5 us; the launch traced here: 53.3 us
  starting transfers between devices  21.6 us (40%)
  Pallas kernels  15.5 us (29%)
  waiting for transfers between devices  13.9 us (26%)
  other arithmetic  1.28 us (2%)
  between operations  1.01 us (2%)
    pallas_call x20, Pallas kernels, call(): pl.pallas_call(body, cost_estimate=pl.CostEstimate(flops=0, transcendenta...  15.5 us
    ppermute x8, starting transfers between devices, exchange(): return (lax.ppermute(values, axis, even), lax.ppermute(values, axis, odd))  14.4 us
    ppermute x8, waiting for transfers between devices, exchange(): return (lax.ppermute(values, axis, even), lax.ppermute(values, axis, odd))  8.5 us
    ppermute x8, starting transfers between devices, swap(): lax.ppermute(values, axis, [(i, i ^ pattern << low) for i in range(count)])  7.22 us
    ppermute x8, waiting for transfers between devices, swap(): lax.ppermute(values, axis, [(i, i ^ pattern << low) for i in range(count)])  5.37 us
    concatenate x1, other arithmetic, per_device(): jnp.concatenate([initial_state, eddy_diffusivity[None], velocity], axis=0)  1.28 us
  transfers between devices with their start and end apart: 16, of which 7 were waited for; matrix products, arithmetic and copies ran while one was open for 0% of the time, Pallas kernels for 15%

profile of v4, /device:TPU:20, one launch (start us, length us, event | category | flops | bytes accessed | tf_op | source)
XLA Modules:
  0.0 53.3 jit_solution(13480562377523681012)
XLA Ops:
  0.6 0.0 copy-start
  0.6 0.0 copy-start.1
  0.7 0.0 copy-start.3
  0.7 0.0 copy-start.4
  0.7 0.0 copy-start.7
  0.7 0.0 copy-start.6
  0.7 0.0 copy-start.10
  0.7 1.3 %pad_maximum_fusion.refs_2_.refs_0_ = f32[6,4,48,128]{3,2,1,0:T(8,128)S(1)} fusion(f32[3,4,48,128]{3,2,1,0:T(8,128)} %vel.1, f32[1,4,48,128]{3,2,1,0:T(8,128)} %bitcast.8, f32[2,4,48,128]{3,2,1,0:T(8,128)} %state.1), kind=kLoop, calls=%fused_computation | loop fusion | flops 294912 | bytes 1179648 | tf_op jit(solution)/shard_map/concatenate | solution.py:832
  2.0 1.6 %collective-permute-start = (f32[6,4,48,128]{3,2,1,0:T(8,128)S(1)}, f32[6,4,48,128]{3,2,1,0:T(8,128)S(1)}, u32[]{:S(2)}, u32[]{:S(2)}) collective-permute-start(f32[6,4,48,128]{3,2,1,0:T(8,128)S(1)} %pad_maximum_fusion.refs_2_.refs_0_), channel_id=1, source_target_pairs={{0,8},{8,0},{16,24},{24,16},{1,9},{9,1},{17,25},{25,17},{2,10},{10... | collective-permute-start | bytes 1769480 | tf_op jit(solution)/shard_map/ppermute | solution.py:80
  3.7 1.9 %collective-permute-start.7 = (f32[6,4,48,128]{3,2,1,0:T(8,128)S(1)}, f32[6,4,48,128]{3,2,1,0:T(8,128)S(1)}, u32[]{:S(2)}, u32[]{:S(2)}) collective-permute-start(f32[6,4,48,128]{3,2,1,0:T(8,128)S(1)} %pad_maximum_fusion.refs_2_.refs_0_), channel_id=1, source_target_pairs={{8,16},{16,8},{9,17},{17,9},{10,18},{18,10},{11,19},{19,11},{12,20... | collective-permute-start | bytes 1769480 | tf_op jit(solution)/shard_map/ppermute | solution.py:80
  5.6 0.0 copy-done.4
  5.6 0.0 copy-done.7
  5.6 0.0 copy-done.6
  5.6 0.0 copy-done.10
  5.6 0.0 copy-done.5
  5.6 0.0 copy-done.9
  5.6 0.0 copy-done.8
  5.7 0.8 %shard_map.131 = (f32[96,128]{1,0:T(8,128)S(1)}, f32[4,24,128]{2,1,0:T(8,128)S(1)}) custom-call(s32[1,64]{1,0:T(1,128)S(1)} %bitcast.13, s32[1,64]{1,0:T(1,128)S(1)} %bitcast.14, f32[2,4,64]{2,1,0:T(4,128)S(1)} %bitcast.9, s32[1,16]{1,0:T(1,128)S(1)} %bitcast.15, s32[1,16]{1,0:T(1,128)S(1)} %bitcast.10, f32[2,16]{1,0:T(2,128)S(1)} %bitcast.12, ...), custom_call_target="tpu_custom_call" | custom-call | bytes 720000 | tf_op jit(solution)/shard_map/pallas_call | solution.py:88
  6.4 0.1 collective-permute-start.3
  6.5 1.2 %collective-permute-done.3.got = f32[96,128]{1,0:T(8,128)S(1)} collective-permute-done((f32[96,128]{1,0:T(8,128)S(1)}, f32[96,128]{1,0:T(8,128)S(1)}, u32[]{:S(2)}, u32[]{:S(2)}) %collective-permute-start.3) | collective-permute-done | bytes 49184 | tf_op jit(solution)/shard_map/ppermute | solution.py:154
  7.8 1.6 %collective-permute-start.4 = (f32[96,128]{1,0:T(8,128)S(1)}, f32[96,128]{1,0:T(8,128)S(1)}, u32[]{:S(2)}, u32[]{:S(2)}) collective-permute-start(f32[96,128]{1,0:T(8,128)S(1)} %get-tuple-element.51), channel_id=1, source_target_pairs={{0,2},{1,3},{2,0},{3,1},{4,6},{5,7},{6,4},{7,5},{8,10},{9,11},{10,... | collective-permute-start | bytes 147464 | tf_op jit(solution)/shard_map/ppermute | solution.py:154
  9.3 0.0 copy-done.3
  9.3 0.3 shard_map.130
  9.6 1.9 %collective-permute-start.2 = (f32[192,128]{1,0:T(8,128)S(1)}, f32[192,128]{1,0:T(8,128)S(1)}, u32[]{:S(2)}, u32[]{:S(2)}) collective-permute-start(f32[192,128]{1,0:T(8,128)S(1)} %shard_map.130), channel_id=1, source_target_pairs={{1,2},{2,1},{3,4},{4,3},{5,6},{6,5},{9,10},{10,9},{11,12},{12,11},... | collective-permute-start | bytes 294920 | tf_op jit(solution)/shard_map/ppermute | solution.py:80
  11.5 0.7 %collective-permute-start.1 = (f32[192,128]{1,0:T(8,128)S(1)}, f32[192,128]{1,0:T(8,128)S(1)}, u32[]{:S(2)}, u32[]{:S(2)}) collective-permute-start(f32[192,128]{1,0:T(8,128)S(1)} %shard_map.130), channel_id=1, source_target_pairs={{0,1},{1,0},{2,3},{3,2},{4,5},{5,4},{6,7},{7,6},{8,9},{9,8},{10,11... | collective-permute-start | bytes 294920 | tf_op jit(solution)/shard_map/ppermute | solution.py:80
  12.2 0.0 collective-permute-done.4.got
  12.2 0.6 %collective-permute-start.5 = (f32[96,128]{1,0:T(8,128)S(1)}, f32[96,128]{1,0:T(8,128)S(1)}, u32[]{:S(2)}, u32[]{:S(2)}) collective-permute-start(f32[96,128]{1,0:T(8,128)S(1)} %get-tuple-element.53), channel_id=1, source_target_pairs={{0,4},{1,5},{2,6},{3,7},{4,0},{5,1},{6,2},{7,3},{8,12},{9,13},{10,... | collective-permute-start | bytes 147464 | tf_op jit(solution)/shard_map/ppermute | solution.py:154
  12.8 3.8 %collective-permute-done.2.odd = f32[192,128]{1,0:T(8,128)S(1)} collective-permute-done((f32[192,128]{1,0:T(8,128)S(1)}, f32[192,128]{1,0:T(8,128)S(1)}, u32[]{:S(2)}, u32[]{:S(2)}) %collective-permute-start.2) | collective-permute-done | bytes 98336 | tf_op jit(solution)/shard_map/ppermute | solution.py:80
  16.6 0.0 collective-permute-done.1.even
  16.6 0.5 collective-permute-done.5.got
  17.1 0.1 shard_map.134
  17.2 0.1 collective-permute-start.6
  17.3 3.9 %collective-permute-start.8 = (f32[288,128]{1,0:T(8,128)S(1)}, f32[288,128]{1,0:T(8,128)S(1)}, u32[]{:S(2)}, u32[]{:S(2)}) collective-permute-start(f32[288,128]{1,0:T(8,128)S(1)} %get-tuple-element.54.refs_3_.refs_1_.got), channel_id=1, source_target_pairs={{8,16},{16,8},{9,17},{17,9},{10,18},{18,10},{11,19},{19,11},{12,20... | collective-permute-start | bytes 442376 | tf_op jit(solution)/shard_map/ppermute | solution.py:80
  21.2 1.3 %shard_map.139 = (f32[2,4,48,256]{3,2,1,0:T(8,128)S(1)}, bf16[128,128]{1,0:T(8,128)(2,1)S(1)}, f32[192,128]{1,0:T(8,128)S(1)}) custom-call(f32[288,128]{1,0:T(8,128)S(1)} %get-tuple-element.54.refs_3_.refs_1_.got), custom_call_target="tpu_custom_call" | custom-call | bytes 5400000 | tf_op jit(solution)/shard_map/pallas_call | solution.py:88
  22.5 0.0 collective-permute-done.6.refs_1_.got
  22.6 1.4 %collective-permute-start.9 = (f32[16,128]{1,0:T(8,128)S(1)}, f32[16,128]{1,0:T(8,128)S(1)}, u32[]{:S(2)}, u32[]{:S(2)}) collective-permute-start(f32[16,128]{1,0:T(8,128)S(1)} %get-tuple-element.70), channel_id=1, source_target_pairs={{0,16},{8,24},{16,0},{24,8},{1,17},{9,25},{17,1},{25,9},{2,18},{10... | collective-permute-start | bytes 24584 | tf_op jit(solution)/shard_map/ppermute | solution.py:154
  24.0 0.9 %shard_map.136.source_e = f32[2,3,48,256]{3,2,1,0:T(8,128)S(1)} custom-call(f32[288,128]{1,0:T(8,128)S(1)} %collective-permute-done.6.refs_1_.got), custom_call_target="tpu_custom_call" | custom-call | bytes 3240000 | tf_op jit(solution)/shard_map/pallas_call | solution.py:88
  24.8 0.0 collective-permute-done.refs_0_
  24.8 1.0 %shard_map.135 = (f32[2,7,7,48,256]{4,3,2,1,0:T(8,128)S(1)}, f32[2,8,48,256]{3,2,1,0:T(8,128)S(1)}) custom-call(f32[6,4,48,128]{3,2,1,0:T(8,128)S(1)} %collective-permute-done.refs_0_, f32[288,128]{1,0:T(8,128)S(1)} %collective-permute-done.6.refs_1_.got, f32[6,4,48,128]{3,2,1,0:T(8,128)S(1)} %pad_maximum_fusion.refs_2_.refs_0_, ...), custom_call_target="tpu_custom_call" | custom-call | bytes 3600000 | tf_op jit(solution)/shard_map/pallas_call | solution.py:88
  25.9 0.0 collective-permute-done.8.refs_3_.got
  25.9 0.9 %shard_map.140.source_o = f32[2,3,48,256]{3,2,1,0:T(8,128)S(1)} custom-call(f32[288,128]{1,0:T(8,128)S(1)} %collective-permute-done.8.refs_3_.got), custom_call_target="tpu_custom_call" | custom-call | bytes 3240000 | tf_op jit(solution)/shard_map/pallas_call | solution.py:88
  26.8 0.0 collective-permute-done.7.refs_2_
  26.8 0.7 %shard_map.137 = (f32[2,7,5,48,256]{4,3,2,1,0:T(8,128)S(1)}, f32[2,4,48,256]{3,2,1,0:T(8,128)S(1)}) custom-call(f32[6,4,48,128]{3,2,1,0:T(8,128)S(1)} %pad_maximum_fusion.refs_2_.refs_0_, f32[288,128]{1,0:T(8,128)S(1)} %get-tuple-element.54.refs_3_.refs_1_.got, f32[6,4,48,128]{3,2,1,0:T(8,128)S(1)} %collective-permute-done.7.refs_2_, ...), custom_call_target="tpu_custom_call" | custom-call | bytes 2520000 | tf_op jit(solution)/shard_map/pallas_call | solution.py:88
  27.5 0.0 collective-permute-done.9.got
  27.5 0.3 shard_map.141
  27.7 3.9 %shard_map.142 = (f32[2,4,48,128]{3,2,1,0:T(8,128)}, f32[456,128]{1,0:T(8,128)S(1)}, f32[16,384]{1,0:T(8,128)S(1)}) custom-call(f32[2,7,7,48,256]{4,3,2,1,0:T(8,128)S(1)} %get-tuple-element.55.coeffs_e, f32[2,7,5,48,256]{4,3,2,1,0:T(8,128)S(1)} %get-tuple-element.58.coeffs_o, f32[2,8,48,256]{3,2,1,0:T(8,128)S(1)} %get-tuple-element.59.start_e, ...), custom_call_target="tpu_custom_call" | custom-call | bytes 18000000 | tf_op jit(solution)/shard_map/pallas_call | solution.py:88
  31.6 2.0 %collective-permute-start.10 = (f32[456,128]{1,0:T(8,128)S(1)}, f32[456,128]{1,0:T(8,128)S(1)}, u32[]{:S(2)}, u32[]{:S(2)}) collective-permute-start(f32[456,128]{1,0:T(8,128)S(1)} %get-tuple-element.78.sent), channel_id=1, source_target_pairs={{0,8},{8,0},{16,24},{24,16},{1,9},{9,1},{17,25},{25,17},{2,10},{10... | collective-permute-start | bytes 700424 | tf_op jit(solution)/shard_map/ppermute | solution.py:80
  33.6 2.2 %collective-permute-start.11 = (f32[456,128]{1,0:T(8,128)S(1)}, f32[456,128]{1,0:T(8,128)S(1)}, u32[]{:S(2)}, u32[]{:S(2)}) collective-permute-start(f32[456,128]{1,0:T(8,128)S(1)} %get-tuple-element.78.sent), channel_id=1, source_target_pairs={{8,16},{16,8},{9,17},{17,9},{10,18},{18,10},{11,19},{19,11},{12,20... | collective-permute-start | bytes 700424 | tf_op jit(solution)/shard_map/ppermute | solution.py:80
  35.8 0.5 %shard_map.143 = (f32[3,2,4,48,256]{4,3,2,1,0:T(8,128)S(1)}, f32[2,4,48,256]{3,2,1,0:T(8,128)S(1)}) custom-call(bf16[192,128]{1,0:T(8,128)(2,1)S(1)} %get-tuple-element.71.spot_hot, bf16[128,128]{1,0:T(8,128)(2,1)S(1)} %get-tuple-element.72.lane_hot, bf16[48,256]{1,0:T(8,128)(2,1)S(1)} %get-tuple-element.73.z_hot, ...), custom_call_target="tpu_custom_call" | custom-call | bytes 2520000 | tf_op jit(solution)/shard_map/pallas_call | solution.py:88
  36.4 1.3 %collective-permute-done.10.sent = f32[456,128]{1,0:T(8,128)S(1)} collective-permute-done((f32[456,128]{1,0:T(8,128)S(1)}, f32[456,128]{1,0:T(8,128)S(1)}, u32[]{:S(2)}, u32[]{:S(2)}) %collective-permute-start.10) | collective-permute-done | bytes 233504 | tf_op jit(solution)/shard_map/ppermute | solution.py:80
  37.7 0.5 shard_map.144
  38.2 3.4 %collective-permute-done.11.sent = f32[456,128]{1,0:T(8,128)S(1)} collective-permute-done((f32[456,128]{1,0:T(8,128)S(1)}, f32[456,128]{1,0:T(8,128)S(1)}, u32[]{:S(2)}, u32[]{:S(2)}) %collective-permute-start.11) | collective-permute-done | bytes 233504 | tf_op jit(solution)/shard_map/ppermute | solution.py:80
  41.6 0.5 shard_map.145
  42.1 2.2 %shard_map.146 = (f32[4,8,128]{2,1,0:T(8,128)S(1)}, f32[4,8,128]{2,1,0:T(8,128)S(1)}, f32[2,6,48,256]{3,2,1,0:T(8,128)S(1)}) custom-call(f32[2,7,7,48,256]{4,3,2,1,0:T(8,128)S(1)} %get-tuple-element.55.coeffs_e, f32[2,7,5,48,256]{4,3,2,1,0:T(8,128)S(1)} %get-tuple-element.58.coeffs_o, f32[3,2,4,48,256]{4,3,2,1,0:T(8,128)S(1)} %get-tuple-element.79.puts_own, ...), custom_call_target="tpu_custom_call" | custom-call | bytes 10800000 | tf_op jit(solution)/shard_map/pallas_call | solution.py:88
  44.3 0.1 collective-permute-start.12
  44.4 1.2 %collective-permute-done.12.refs_1_ = f32[4,8,128]{2,1,0:T(8,128)S(1)} collective-permute-done((f32[4,8,128]{2,1,0:T(8,128)S(1)}, f32[4,8,128]{2,1,0:T(8,128)S(1)}, u32[]{:S(2)}, u32[]{:S(2)}) %collective-permute-start.12) | collective-permute-done | bytes 16416 | tf_op jit(solution)/shard_map/ppermute | solution.py:154
  45.6 0.5 collective-permute-start.13
  46.1 1.9 %collective-permute-start.14 = (f32[2,8,128]{2,1,0:T(8,128)S(1)}, f32[2,8,128]{2,1,0:T(8,128)S(1)}, u32[]{:S(2)}, u32[]{:S(2)}) collective-permute-start(f32[2,8,128]{2,1,0:T(8,128)S(1)} %get-tuple-element.91), channel_id=1, source_target_pairs={{0,4},{1,5},{2,6},{3,7},{4,0},{5,1},{6,2},{7,3},{8,12},{9,13},{10,... | collective-permute-start | bytes 24584 | tf_op jit(solution)/shard_map/ppermute | solution.py:154
  48.1 1.1 %collective-permute-start.15 = (f32[2,8,128]{2,1,0:T(8,128)S(1)}, f32[2,8,128]{2,1,0:T(8,128)S(1)}, u32[]{:S(2)}, u32[]{:S(2)}) collective-permute-start(f32[2,8,128]{2,1,0:T(8,128)S(1)} %get-tuple-element.92), channel_id=1, source_target_pairs={{0,6},{1,7},{2,4},{3,5},{4,2},{5,3},{6,0},{7,1},{8,14},{9,15},{10,... | collective-permute-start | bytes 24584 | tf_op jit(solution)/shard_map/ppermute | solution.py:154
  49.2 1.0 %shard_map.147 = f32[2,4,48,128]{3,2,1,0:T(8,128)} custom-call(f32[2,7,7,48,256]{4,3,2,1,0:T(8,128)S(1)} %get-tuple-element.55.coeffs_e, f32[2,7,5,48,256]{4,3,2,1,0:T(8,128)S(1)} %get-tuple-element.58.coeffs_o, f32[2,6,48,256]{3,2,1,0:T(8,128)S(1)} %get-tuple-element.86.second), custom_call_target="tpu_custom_call" | custom-call | bytes 3600000 | tf_op jit(solution)/shard_map/pallas_call | solution.py:88
  50.1 0.0 collective-permute-done.13.refs_1_
  50.1 0.0 collective-permute-done.14.refs_2_
  50.1 2.5 %collective-permute-done.15.refs_3_ = f32[2,8,128]{2,1,0:T(8,128)S(1)} collective-permute-done((f32[2,8,128]{2,1,0:T(8,128)S(1)}, f32[2,8,128]{2,1,0:T(8,128)S(1)}, u32[]{:S(2)}, u32[]{:S(2)}) %collective-permute-start.15) | collective-permute-done | bytes 8224 | tf_op jit(solution)/shard_map/ppermute | solution.py:154
  52.6 0.7 %shard_map.149 = f32[2,16]{1,0:T(2,128)} custom-call(f32[2,8,128]{2,1,0:T(8,128)S(1)} %get-tuple-element.89.refs_0_, f32[2,8,128]{2,1,0:T(8,128)S(1)} %collective-permute-done.13.refs_1_, f32[2,8,128]{2,1,0:T(8,128)S(1)} %collective-permute-done.14.refs_2_, f32[2,8,128]{2,1,0:T(8,128)S(1)} %collective-permute-done.15.refs_3_, s32[1,16]{1,0:T(1,128)S(1)} %bitcast.11), custom_call_target="tpu_custom_call" | custom-call | bytes 720000 | tf_op jit(solution)/shard_map/pallas_call | solution.py:88
  (11 shorter events, 0.1 us)
Async XLA Ops:
  0.6 8.7 %copy-start = (f32[3,4,48,128]{3,2,1,0:T(8,128)S(1)}, f32[3,4,48,128]{3,2,1,0:T(8,128)}, u32[]{:S(2)}) copy-start(f32[3,4,48,128]{3,2,1,0:T(8,128)} %vel.1) | copy-start | bytes 884740
  0.6 8.7 %copy-start.1 = (f32[2,4,48,128]{3,2,1,0:T(8,128)S(1)}, f32[2,4,48,128]{3,2,1,0:T(8,128)}, u32[]{:S(2)}) copy-start(f32[2,4,48,128]{3,2,1,0:T(8,128)} %state.1) | copy-start | bytes 589828
  0.7 8.7 %copy-start.3 = (f32[4,48,128]{2,1,0:T(8,128)S(1)}, f32[4,48,128]{2,1,0:T(8,128)}, u32[]{:S(2)}) copy-start(f32[4,48,128]{2,1,0:T(8,128)} %kappa.1) | copy-start | bytes 294916
  0.7 4.9 %copy-start.4 = (f32[16,128]{1,0:T(8,128)S(1)}, f32[16,128]{1,0:T(8,128)}, u32[]{:S(2)}) copy-start(f32[16,128]{1,0:T(8,128)} %foot.1) | copy-start | bytes 24580
  0.7 4.9 %copy-start.7 = (f32[16,2]{0,1:T(2,128)S(1)}, f32[16,2]{0,1:T(2,128)}, u32[]{:S(2)}) copy-start(f32[16,2]{0,1:T(2,128)} %param.20) | copy-start | bytes 388
  0.7 4.9 %copy-start.6 = (s32[16,1]{0,1:T(1,128)S(1)}, s32[16,1]{0,1:T(1,128)}, u32[]{:S(2)}) copy-start(s32[16,1]{0,1:T(1,128)} %param.19) | copy-start | bytes 196
  0.7 4.9 %copy-start.10 = (s32[16]{0:T(128)S(1)}, s32[16]{0:T(128)}, u32[]{:S(2)}) copy-start(s32[16]{0:T(128)} %param.18) | copy-start | bytes 196
  0.7 4.9 %copy-start.5 = (f32[64,2,4]{0,2,1:T(4,128)S(1)}, f32[64,2,4]{0,2,1:T(4,128)}, u32[]{:S(2)}) copy-start(f32[64,2,4]{0,2,1:T(4,128)} %param.17) | copy-start | bytes 6148
  0.7 4.9 %copy-start.9 = (s32[64,1]{0,1:T(1,128)S(1)}, s32[64,1]{0,1:T(1,128)}, u32[]{:S(2)}) copy-start(s32[64,1]{0,1:T(1,128)} %param.16) | copy-start | bytes 772
  0.7 4.9 %copy-start.8 = (s32[64]{0:T(128)S(1)}, s32[64]{0:T(128)}, u32[]{:S(2)}) copy-start(s32[64]{0:T(128)} %param.15) | copy-start | bytes 772
  0.7 8.6 %copy-start.2 = (f32[2,4,48,128]{3,2,1,0:T(8,128)S(1)}, f32[2,4,48,128]{3,2,1,0:T(8,128)}, u32[]{:S(2)}) copy-start(f32[2,4,48,128]{3,2,1,0:T(8,128)} %target.3) | copy-start | bytes 589828
  2.0 22.8 %collective-permute-start = (f32[6,4,48,128]{3,2,1,0:T(8,128)S(1)}, f32[6,4,48,128]{3,2,1,0:T(8,128)S(1)}, u32[]{:S(2)}, u32[]{:S(2)}) collective-permute-start(f32[6,4,48,128]{3,2,1,0:T(8,128)S(1)} %pad_maximum_fusion.refs_2_.refs_0_), channel_id=1, source_target_pairs={{0,8},{8,0},{16,24},{24,16},{1,9},{9,1},{17,25},{25,17},{2,10},{10... | collective-permute-start | bytes 1769480 | tf_op jit(solution)/shard_map/ppermute | solution.py:80
  3.7 23.1 %collective-permute-start.7 = (f32[6,4,48,128]{3,2,1,0:T(8,128)S(1)}, f32[6,4,48,128]{3,2,1,0:T(8,128)S(1)}, u32[]{:S(2)}, u32[]{:S(2)}) collective-permute-start(f32[6,4,48,128]{3,2,1,0:T(8,128)S(1)} %pad_maximum_fusion.refs_2_.refs_0_), channel_id=1, source_target_pairs={{8,16},{16,8},{9,17},{17,9},{10,18},{18,10},{11,19},{19,11},{12,20... | collective-permute-start | bytes 1769480 | tf_op jit(solution)/shard_map/ppermute | solution.py:80
  6.4 1.3 %collective-permute-start.3 = (f32[96,128]{1,0:T(8,128)S(1)}, f32[96,128]{1,0:T(8,128)S(1)}, u32[]{:S(2)}, u32[]{:S(2)}) collective-permute-start(f32[96,128]{1,0:T(8,128)S(1)} %get-tuple-element.49), channel_id=1, source_target_pairs={{0,1},{1,0},{2,3},{3,2},{4,5},{5,4},{6,7},{7,6},{8,9},{9,8},{10,11... | collective-permute-start | bytes 147464 | tf_op jit(solution)/shard_map/ppermute | solution.py:154
  7.8 4.5 %collective-permute-start.4 = (f32[96,128]{1,0:T(8,128)S(1)}, f32[96,128]{1,0:T(8,128)S(1)}, u32[]{:S(2)}, u32[]{:S(2)}) collective-permute-start(f32[96,128]{1,0:T(8,128)S(1)} %get-tuple-element.51), channel_id=1, source_target_pairs={{0,2},{1,3},{2,0},{3,1},{4,6},{5,7},{6,4},{7,5},{8,10},{9,11},{10,... | collective-permute-start | bytes 147464 | tf_op jit(solution)/shard_map/ppermute | solution.py:154
  9.6 7.1 %collective-permute-start.2 = (f32[192,128]{1,0:T(8,128)S(1)}, f32[192,128]{1,0:T(8,128)S(1)}, u32[]{:S(2)}, u32[]{:S(2)}) collective-permute-start(f32[192,128]{1,0:T(8,128)S(1)} %shard_map.130), channel_id=1, source_target_pairs={{1,2},{2,1},{3,4},{4,3},{5,6},{6,5},{9,10},{10,9},{11,12},{12,11},... | collective-permute-start | bytes 294920 | tf_op jit(solution)/shard_map/ppermute | solution.py:80
  11.5 5.1 %collective-permute-start.1 = (f32[192,128]{1,0:T(8,128)S(1)}, f32[192,128]{1,0:T(8,128)S(1)}, u32[]{:S(2)}, u32[]{:S(2)}) collective-permute-start(f32[192,128]{1,0:T(8,128)S(1)} %shard_map.130), channel_id=1, source_target_pairs={{0,1},{1,0},{2,3},{3,2},{4,5},{5,4},{6,7},{7,6},{8,9},{9,8},{10,11... | collective-permute-start | bytes 294920 | tf_op jit(solution)/shard_map/ppermute | solution.py:80
  12.2 4.9 %collective-permute-start.5 = (f32[96,128]{1,0:T(8,128)S(1)}, f32[96,128]{1,0:T(8,128)S(1)}, u32[]{:S(2)}, u32[]{:S(2)}) collective-permute-start(f32[96,128]{1,0:T(8,128)S(1)} %get-tuple-element.53), channel_id=1, source_target_pairs={{0,4},{1,5},{2,6},{3,7},{4,0},{5,1},{6,2},{7,3},{8,12},{9,13},{10,... | collective-permute-start | bytes 147464 | tf_op jit(solution)/shard_map/ppermute | solution.py:154
  17.2 5.3 %collective-permute-start.6 = (f32[288,128]{1,0:T(8,128)S(1)}, f32[288,128]{1,0:T(8,128)S(1)}, u32[]{:S(2)}, u32[]{:S(2)}) collective-permute-start(f32[288,128]{1,0:T(8,128)S(1)} %get-tuple-element.54.refs_3_.refs_1_.got), channel_id=1, source_target_pairs={{0,8},{8,0},{16,24},{24,16},{1,9},{9,1},{17,25},{25,17},{2,10},{10... | collective-permute-start | bytes 442376 | tf_op jit(solution)/shard_map/ppermute | solution.py:80
  17.3 8.6 %collective-permute-start.8 = (f32[288,128]{1,0:T(8,128)S(1)}, f32[288,128]{1,0:T(8,128)S(1)}, u32[]{:S(2)}, u32[]{:S(2)}) collective-permute-start(f32[288,128]{1,0:T(8,128)S(1)} %get-tuple-element.54.refs_3_.refs_1_.got), channel_id=1, source_target_pairs={{8,16},{16,8},{9,17},{17,9},{10,18},{18,10},{11,19},{19,11},{12,20... | collective-permute-start | bytes 442376 | tf_op jit(solution)/shard_map/ppermute | solution.py:80
  22.6 4.9 %collective-permute-start.9 = (f32[16,128]{1,0:T(8,128)S(1)}, f32[16,128]{1,0:T(8,128)S(1)}, u32[]{:S(2)}, u32[]{:S(2)}) collective-permute-start(f32[16,128]{1,0:T(8,128)S(1)} %get-tuple-element.70), channel_id=1, source_target_pairs={{0,16},{8,24},{16,0},{24,8},{1,17},{9,25},{17,1},{25,9},{2,18},{10... | collective-permute-start | bytes 24584 | tf_op jit(solution)/shard_map/ppermute | solution.py:154
  31.6 6.1 %collective-permute-start.10 = (f32[456,128]{1,0:T(8,128)S(1)}, f32[456,128]{1,0:T(8,128)S(1)}, u32[]{:S(2)}, u32[]{:S(2)}) collective-permute-start(f32[456,128]{1,0:T(8,128)S(1)} %get-tuple-element.78.sent), channel_id=1, source_target_pairs={{0,8},{8,0},{16,24},{24,16},{1,9},{9,1},{17,25},{25,17},{2,10},{10... | collective-permute-start | bytes 700424 | tf_op jit(solution)/shard_map/ppermute | solution.py:80
  33.6 7.9 %collective-permute-start.11 = (f32[456,128]{1,0:T(8,128)S(1)}, f32[456,128]{1,0:T(8,128)S(1)}, u32[]{:S(2)}, u32[]{:S(2)}) collective-permute-start(f32[456,128]{1,0:T(8,128)S(1)} %get-tuple-element.78.sent), channel_id=1, source_target_pairs={{8,16},{16,8},{9,17},{17,9},{10,18},{18,10},{11,19},{19,11},{12,20... | collective-permute-start | bytes 700424 | tf_op jit(solution)/shard_map/ppermute | solution.py:80
  44.3 1.2 %collective-permute-start.12 = (f32[4,8,128]{2,1,0:T(8,128)S(1)}, f32[4,8,128]{2,1,0:T(8,128)S(1)}, u32[]{:S(2)}, u32[]{:S(2)}) collective-permute-start(f32[4,8,128]{2,1,0:T(8,128)S(1)} %get-tuple-element.88), channel_id=1, source_target_pairs={{0,1},{1,0},{2,3},{3,2},{4,5},{5,4},{6,7},{7,6},{8,9},{9,8},{10,11... | collective-permute-start | bytes 49160 | tf_op jit(solution)/shard_map/ppermute | solution.py:154
  45.6 4.5 %collective-permute-start.13 = (f32[2,8,128]{2,1,0:T(8,128)S(1)}, f32[2,8,128]{2,1,0:T(8,128)S(1)}, u32[]{:S(2)}, u32[]{:S(2)}) collective-permute-start(f32[2,8,128]{2,1,0:T(8,128)S(1)} %get-tuple-element.90), channel_id=1, source_target_pairs={{0,2},{1,3},{2,0},{3,1},{4,6},{5,7},{6,4},{7,5},{8,10},{9,11},{10,... | collective-permute-start | bytes 24584 | tf_op jit(solution)/shard_map/ppermute | solution.py:154
  46.1 4.0 %collective-permute-start.14 = (f32[2,8,128]{2,1,0:T(8,128)S(1)}, f32[2,8,128]{2,1,0:T(8,128)S(1)}, u32[]{:S(2)}, u32[]{:S(2)}) collective-permute-start(f32[2,8,128]{2,1,0:T(8,128)S(1)} %get-tuple-element.91), channel_id=1, source_target_pairs={{0,4},{1,5},{2,6},{3,7},{4,0},{5,1},{6,2},{7,3},{8,12},{9,13},{10,... | collective-permute-start | bytes 24584 | tf_op jit(solution)/shard_map/ppermute | solution.py:154
  48.1 4.5 %collective-permute-start.15 = (f32[2,8,128]{2,1,0:T(8,128)S(1)}, f32[2,8,128]{2,1,0:T(8,128)S(1)}, u32[]{:S(2)}, u32[]{:S(2)}) collective-permute-start(f32[2,8,128]{2,1,0:T(8,128)S(1)} %get-tuple-element.92), channel_id=1, source_target_pairs={{0,6},{1,7},{2,4},{3,5},{4,2},{5,3},{6,0},{7,1},{8,14},{9,15},{10,... | collective-permute-start | bytes 24584 | tf_op jit(solution)/shard_map/ppermute | solution.py:154

commit v5 on v4

--- a/solution.py
+++ b/solution.py
@@ -360,7 +360,7 @@
     meta = jnp.zeros((records, LANES), F32)
     for k in range(CAPA):
         move = (slot < 12) & (slot % 4 == k) & (r_to == r_of - slot + 12 + slot // 4)
-        meta = meta + pick(move.astype(BF16), roll(records_in, -32 * k, 1))
+        meta = meta + pick(move.astype(BF16), roll(records_in, -32 * k, 1), count=2)
     q_of, l_of = iota((FOOT, FOOT), 0), iota((FOOT, FOOT), 1)
     unpack = (l_of == (q_of % 32) * FY + q_of // 32).astype(BF16)
     side = (iota((records, 1), 0) % SLOT_ROWS) // 4
@@ -637,9 +637,9 @@
         both = jnp.concatenate(
             [kept[n, s, :, :, :LANES].reshape(cells, LANES) for s in range(2)], axis=1
         )
-        seen = spread(lane_pair, both)
+        seen = spread(lane_pair, both, count=2)
         packed = pack_rims([kept[n, s, p, :, LANES:] for s in range(2) for p in range(FX)])
-        seen_rim = spread(rim_pair, packed)
+        seen_rim = spread(rim_pair, packed, count=2)
         for s in range(2):
             at = s * steps + n
             value = jnp.sum(seen[:, s * own : (s + 1) * own] * spots, axis=0, keepdims=True)

time: 53.5 us -> 53.3 us (level)
  transfers between devices with their start and end apart: 16 -> 16, of which waited for: 7 -> 7; matrix products, arithmetic and copies ran while one was open for 0% -> 0% of each run, Pallas kernels for 15% -> 14%
where the time goes in v5:
time: 53.3 us; the launch traced here: 53.1 us
  starting transfers between devices  21.6 us (41%)
  Pallas kernels  15.1 us (28%)
  waiting for transfers between devices  14 us (26%)
  other arithmetic  1.28 us (2%)
  between operations  1 us (2%)
    pallas_call x20, Pallas kernels, call(): pl.pallas_call(body, cost_estimate=pl.CostEstimate(flops=0, transcendenta...  15.1 us
    ppermute x8, starting transfers between devices, exchange(): return (lax.ppermute(values, axis, even), lax.ppermute(values, axis, odd))  14.3 us
    ppermute x8, waiting for transfers between devices, exchange(): return (lax.ppermute(values, axis, even), lax.ppermute(values, axis, odd))  8.64 us
    ppermute x8, starting transfers between devices, swap(): lax.ppermute(values, axis, [(i, i ^ pattern << low) for i in range(count)])  7.33 us
    ppermute x8, waiting for transfers between devices, swap(): lax.ppermute(values, axis, [(i, i ^ pattern << low) for i in range(count)])  5.37 us
    concatenate x1, other arithmetic, per_device(): jnp.concatenate([initial_state, eddy_diffusivity[None], velocity], axis=0)  1.28 us
  transfers between devices with their start and end apart: 16, of which 7 were waited for; matrix products, arithmetic and copies ran while one was open for 0% of the time, Pallas kernels for 14%

profile of v5, /device:TPU:20, one launch (start us, length us, event | category | flops | bytes accessed | tf_op | source)
XLA Modules:
  0.0 53.1 jit_solution(14869984809304855279)
XLA Ops:
  0.6 0.0 copy-start
  0.6 0.0 copy-start.1
  0.7 0.0 copy-start.3
  0.7 0.0 copy-start.4
  0.7 0.0 copy-start.7
  0.7 0.0 copy-start.6
  0.7 0.0 copy-start.10
  0.7 1.3 %pad_maximum_fusion.refs_2_.refs_0_ = f32[6,4,48,128]{3,2,1,0:T(8,128)S(1)} fusion(f32[3,4,48,128]{3,2,1,0:T(8,128)} %vel.1, f32[1,4,48,128]{3,2,1,0:T(8,128)} %bitcast.8, f32[2,4,48,128]{3,2,1,0:T(8,128)} %state.1), kind=kLoop, calls=%fused_computation | loop fusion | flops 294912 | bytes 1179648 | tf_op jit(solution)/shard_map/concatenate | solution.py:832
  2.0 1.6 %collective-permute-start = (f32[6,4,48,128]{3,2,1,0:T(8,128)S(1)}, f32[6,4,48,128]{3,2,1,0:T(8,128)S(1)}, u32[]{:S(2)}, u32[]{:S(2)}) collective-permute-start(f32[6,4,48,128]{3,2,1,0:T(8,128)S(1)} %pad_maximum_fusion.refs_2_.refs_0_), channel_id=1, source_target_pairs={{0,8},{8,0},{16,24},{24,16},{1,9},{9,1},{17,25},{25,17},{2,10},{10... | collective-permute-start | bytes 1769480 | tf_op jit(solution)/shard_map/ppermute | solution.py:80
  3.7 1.9 %collective-permute-start.7 = (f32[6,4,48,128]{3,2,1,0:T(8,128)S(1)}, f32[6,4,48,128]{3,2,1,0:T(8,128)S(1)}, u32[]{:S(2)}, u32[]{:S(2)}) collective-permute-start(f32[6,4,48,128]{3,2,1,0:T(8,128)S(1)} %pad_maximum_fusion.refs_2_.refs_0_), channel_id=1, source_target_pairs={{8,16},{16,8},{9,17},{17,9},{10,18},{18,10},{11,19},{19,11},{12,20... | collective-permute-start | bytes 1769480 | tf_op jit(solution)/shard_map/ppermute | solution.py:80
  5.6 0.0 copy-done.4
  5.6 0.0 copy-done.7
  5.6 0.0 copy-done.6
  5.6 0.0 copy-done.10
  5.6 0.0 copy-done.5
  5.6 0.0 copy-done.9
  5.6 0.0 copy-done.8
  5.7 0.8 %shard_map.131 = (f32[96,128]{1,0:T(8,128)S(1)}, f32[4,24,128]{2,1,0:T(8,128)S(1)}) custom-call(s32[1,64]{1,0:T(1,128)S(1)} %bitcast.13, s32[1,64]{1,0:T(1,128)S(1)} %bitcast.14, f32[2,4,64]{2,1,0:T(4,128)S(1)} %bitcast.9, s32[1,16]{1,0:T(1,128)S(1)} %bitcast.15, s32[1,16]{1,0:T(1,128)S(1)} %bitcast.10, f32[2,16]{1,0:T(2,128)S(1)} %bitcast.12, ...), custom_call_target="tpu_custom_call" | custom-call | bytes 720000 | tf_op jit(solution)/shard_map/pallas_call | solution.py:88
  6.4 0.1 collective-permute-start.3
  6.5 1.2 %collective-permute-done.3.got = f32[96,128]{1,0:T(8,128)S(1)} collective-permute-done((f32[96,128]{1,0:T(8,128)S(1)}, f32[96,128]{1,0:T(8,128)S(1)}, u32[]{:S(2)}, u32[]{:S(2)}) %collective-permute-start.3) | collective-permute-done | bytes 49184 | tf_op jit(solution)/shard_map/ppermute | solution.py:154
  7.8 1.6 %collective-permute-start.4 = (f32[96,128]{1,0:T(8,128)S(1)}, f32[96,128]{1,0:T(8,128)S(1)}, u32[]{:S(2)}, u32[]{:S(2)}) collective-permute-start(f32[96,128]{1,0:T(8,128)S(1)} %get-tuple-element.51), channel_id=1, source_target_pairs={{0,2},{1,3},{2,0},{3,1},{4,6},{5,7},{6,4},{7,5},{8,10},{9,11},{10,... | collective-permute-start | bytes 147464 | tf_op jit(solution)/shard_map/ppermute | solution.py:154
  9.3 0.0 copy-done.3
  9.3 0.3 shard_map.130
  9.6 1.9 %collective-permute-start.2 = (f32[192,128]{1,0:T(8,128)S(1)}, f32[192,128]{1,0:T(8,128)S(1)}, u32[]{:S(2)}, u32[]{:S(2)}) collective-permute-start(f32[192,128]{1,0:T(8,128)S(1)} %shard_map.130), channel_id=1, source_target_pairs={{1,2},{2,1},{3,4},{4,3},{5,6},{6,5},{9,10},{10,9},{11,12},{12,11},... | collective-permute-start | bytes 294920 | tf_op jit(solution)/shard_map/ppermute | solution.py:80
  11.5 0.7 %collective-permute-start.1 = (f32[192,128]{1,0:T(8,128)S(1)}, f32[192,128]{1,0:T(8,128)S(1)}, u32[]{:S(2)}, u32[]{:S(2)}) collective-permute-start(f32[192,128]{1,0:T(8,128)S(1)} %shard_map.130), channel_id=1, source_target_pairs={{0,1},{1,0},{2,3},{3,2},{4,5},{5,4},{6,7},{7,6},{8,9},{9,8},{10,11... | collective-permute-start | bytes 294920 | tf_op jit(solution)/shard_map/ppermute | solution.py:80
  12.2 0.0 collective-permute-done.4.got
  12.2 0.6 %collective-permute-start.5 = (f32[96,128]{1,0:T(8,128)S(1)}, f32[96,128]{1,0:T(8,128)S(1)}, u32[]{:S(2)}, u32[]{:S(2)}) collective-permute-start(f32[96,128]{1,0:T(8,128)S(1)} %get-tuple-element.53), channel_id=1, source_target_pairs={{0,4},{1,5},{2,6},{3,7},{4,0},{5,1},{6,2},{7,3},{8,12},{9,13},{10,... | collective-permute-start | bytes 147464 | tf_op jit(solution)/shard_map/ppermute | solution.py:154
  12.8 3.8 %collective-permute-done.2.odd = f32[192,128]{1,0:T(8,128)S(1)} collective-permute-done((f32[192,128]{1,0:T(8,128)S(1)}, f32[192,128]{1,0:T(8,128)S(1)}, u32[]{:S(2)}, u32[]{:S(2)}) %collective-permute-start.2) | collective-permute-done | bytes 98336 | tf_op jit(solution)/shard_map/ppermute | solution.py:80
  16.6 0.0 collective-permute-done.1.even
  16.6 0.5 collective-permute-done.5.got
  17.1 0.1 shard_map.134
  17.2 0.1 collective-permute-start.6
  17.3 3.9 %collective-permute-start.8 = (f32[288,128]{1,0:T(8,128)S(1)}, f32[288,128]{1,0:T(8,128)S(1)}, u32[]{:S(2)}, u32[]{:S(2)}) collective-permute-start(f32[288,128]{1,0:T(8,128)S(1)} %get-tuple-element.54.refs_3_.refs_1_.got), channel_id=1, source_target_pairs={{8,16},{16,8},{9,17},{17,9},{10,18},{18,10},{11,19},{19,11},{12,20... | collective-permute-start | bytes 442376 | tf_op jit(solution)/shard_map/ppermute | solution.py:80
  21.2 1.2 %shard_map.139 = (f32[2,4,48,256]{3,2,1,0:T(8,128)S(1)}, bf16[128,128]{1,0:T(8,128)(2,1)S(1)}, f32[192,128]{1,0:T(8,128)S(1)}) custom-call(f32[288,128]{1,0:T(8,128)S(1)} %get-tuple-element.54.refs_3_.refs_1_.got), custom_call_target="tpu_custom_call" | custom-call | bytes 5400000 | tf_op jit(solution)/shard_map/pallas_call | solution.py:88
  22.4 0.0 collective-permute-done.6.refs_1_.got
  22.5 1.5 %collective-permute-start.9 = (f32[16,128]{1,0:T(8,128)S(1)}, f32[16,128]{1,0:T(8,128)S(1)}, u32[]{:S(2)}, u32[]{:S(2)}) collective-permute-start(f32[16,128]{1,0:T(8,128)S(1)} %get-tuple-element.70), channel_id=1, source_target_pairs={{0,16},{8,24},{16,0},{24,8},{1,17},{9,25},{17,1},{25,9},{2,18},{10... | collective-permute-start | bytes 24584 | tf_op jit(solution)/shard_map/ppermute | solution.py:154
  24.0 0.8 %shard_map.136.source_e = f32[2,3,48,256]{3,2,1,0:T(8,128)S(1)} custom-call(f32[288,128]{1,0:T(8,128)S(1)} %collective-permute-done.6.refs_1_.got), custom_call_target="tpu_custom_call" | custom-call | bytes 3240000 | tf_op jit(solution)/shard_map/pallas_call | solution.py:88
  24.8 0.0 collective-permute-done.refs_0_
  24.8 1.0 %shard_map.135 = (f32[2,7,7,48,256]{4,3,2,1,0:T(8,128)S(1)}, f32[2,8,48,256]{3,2,1,0:T(8,128)S(1)}) custom-call(f32[6,4,48,128]{3,2,1,0:T(8,128)S(1)} %collective-permute-done.refs_0_, f32[288,128]{1,0:T(8,128)S(1)} %collective-permute-done.6.refs_1_.got, f32[6,4,48,128]{3,2,1,0:T(8,128)S(1)} %pad_maximum_fusion.refs_2_.refs_0_, ...), custom_call_target="tpu_custom_call" | custom-call | bytes 3600000 | tf_op jit(solution)/shard_map/pallas_call | solution.py:88
  25.8 0.0 collective-permute-done.8.refs_3_.got
  25.8 0.8 %shard_map.140.source_o = f32[2,3,48,256]{3,2,1,0:T(8,128)S(1)} custom-call(f32[288,128]{1,0:T(8,128)S(1)} %collective-permute-done.8.refs_3_.got), custom_call_target="tpu_custom_call" | custom-call | bytes 3240000 | tf_op jit(solution)/shard_map/pallas_call | solution.py:88
  26.6 0.0 collective-permute-done.7.refs_2_
  26.7 0.7 %shard_map.137 = (f32[2,7,5,48,256]{4,3,2,1,0:T(8,128)S(1)}, f32[2,4,48,256]{3,2,1,0:T(8,128)S(1)}) custom-call(f32[6,4,48,128]{3,2,1,0:T(8,128)S(1)} %pad_maximum_fusion.refs_2_.refs_0_, f32[288,128]{1,0:T(8,128)S(1)} %get-tuple-element.54.refs_3_.refs_1_.got, f32[6,4,48,128]{3,2,1,0:T(8,128)S(1)} %collective-permute-done.7.refs_2_, ...), custom_call_target="tpu_custom_call" | custom-call | bytes 2520000 | tf_op jit(solution)/shard_map/pallas_call | solution.py:88
  27.4 0.0 collective-permute-done.9.got
  27.4 0.3 shard_map.141
  27.6 3.7 %shard_map.142 = (f32[2,4,48,128]{3,2,1,0:T(8,128)}, f32[456,128]{1,0:T(8,128)S(1)}, f32[16,384]{1,0:T(8,128)S(1)}) custom-call(f32[2,7,7,48,256]{4,3,2,1,0:T(8,128)S(1)} %get-tuple-element.55.coeffs_e, f32[2,7,5,48,256]{4,3,2,1,0:T(8,128)S(1)} %get-tuple-element.58.coeffs_o, f32[2,8,48,256]{3,2,1,0:T(8,128)S(1)} %get-tuple-element.59.start_e, ...), custom_call_target="tpu_custom_call" | custom-call | bytes 18000000 | tf_op jit(solution)/shard_map/pallas_call | solution.py:88
  31.4 2.0 %collective-permute-start.10 = (f32[456,128]{1,0:T(8,128)S(1)}, f32[456,128]{1,0:T(8,128)S(1)}, u32[]{:S(2)}, u32[]{:S(2)}) collective-permute-start(f32[456,128]{1,0:T(8,128)S(1)} %get-tuple-element.78.sent), channel_id=1, source_target_pairs={{0,8},{8,0},{16,24},{24,16},{1,9},{9,1},{17,25},{25,17},{2,10},{10... | collective-permute-start | bytes 700424 | tf_op jit(solution)/shard_map/ppermute | solution.py:80
  33.4 2.1 %collective-permute-start.11 = (f32[456,128]{1,0:T(8,128)S(1)}, f32[456,128]{1,0:T(8,128)S(1)}, u32[]{:S(2)}, u32[]{:S(2)}) collective-permute-start(f32[456,128]{1,0:T(8,128)S(1)} %get-tuple-element.78.sent), channel_id=1, source_target_pairs={{8,16},{16,8},{9,17},{17,9},{10,18},{18,10},{11,19},{19,11},{12,20... | collective-permute-start | bytes 700424 | tf_op jit(solution)/shard_map/ppermute | solution.py:80
  35.5 0.5 %shard_map.143 = (f32[3,2,4,48,256]{4,3,2,1,0:T(8,128)S(1)}, f32[2,4,48,256]{3,2,1,0:T(8,128)S(1)}) custom-call(bf16[192,128]{1,0:T(8,128)(2,1)S(1)} %get-tuple-element.71.spot_hot, bf16[128,128]{1,0:T(8,128)(2,1)S(1)} %get-tuple-element.72.lane_hot, bf16[48,256]{1,0:T(8,128)(2,1)S(1)} %get-tuple-element.73.z_hot, ...), custom_call_target="tpu_custom_call" | custom-call | bytes 2520000 | tf_op jit(solution)/shard_map/pallas_call | solution.py:88
  36.0 1.4 %collective-permute-done.10.sent = f32[456,128]{1,0:T(8,128)S(1)} collective-permute-done((f32[456,128]{1,0:T(8,128)S(1)}, f32[456,128]{1,0:T(8,128)S(1)}, u32[]{:S(2)}, u32[]{:S(2)}) %collective-permute-start.10) | collective-permute-done | bytes 233504 | tf_op jit(solution)/shard_map/ppermute | solution.py:80
  37.4 0.5 shard_map.144
  37.9 3.4 %collective-permute-done.11.sent = f32[456,128]{1,0:T(8,128)S(1)} collective-permute-done((f32[456,128]{1,0:T(8,128)S(1)}, f32[456,128]{1,0:T(8,128)S(1)}, u32[]{:S(2)}, u32[]{:S(2)}) %collective-permute-start.11) | collective-permute-done | bytes 233504 | tf_op jit(solution)/shard_map/ppermute | solution.py:80
  41.3 0.5 shard_map.145
  41.9 2.2 %shard_map.146 = (f32[4,8,128]{2,1,0:T(8,128)S(1)}, f32[4,8,128]{2,1,0:T(8,128)S(1)}, f32[2,6,48,256]{3,2,1,0:T(8,128)S(1)}) custom-call(f32[2,7,7,48,256]{4,3,2,1,0:T(8,128)S(1)} %get-tuple-element.55.coeffs_e, f32[2,7,5,48,256]{4,3,2,1,0:T(8,128)S(1)} %get-tuple-element.58.coeffs_o, f32[3,2,4,48,256]{4,3,2,1,0:T(8,128)S(1)} %get-tuple-element.79.puts_own, ...), custom_call_target="tpu_custom_call" | custom-call | bytes 10800000 | tf_op jit(solution)/shard_map/pallas_call | solution.py:88
  44.1 0.1 collective-permute-start.12
  44.2 1.2 %collective-permute-done.12.refs_1_ = f32[4,8,128]{2,1,0:T(8,128)S(1)} collective-permute-done((f32[4,8,128]{2,1,0:T(8,128)S(1)}, f32[4,8,128]{2,1,0:T(8,128)S(1)}, u32[]{:S(2)}, u32[]{:S(2)}) %collective-permute-start.12) | collective-permute-done | bytes 16416 | tf_op jit(solution)/shard_map/ppermute | solution.py:154
  45.4 0.5 %collective-permute-start.13 = (f32[2,8,128]{2,1,0:T(8,128)S(1)}, f32[2,8,128]{2,1,0:T(8,128)S(1)}, u32[]{:S(2)}, u32[]{:S(2)}) collective-permute-start(f32[2,8,128]{2,1,0:T(8,128)S(1)} %get-tuple-element.90), channel_id=1, source_target_pairs={{0,2},{1,3},{2,0},{3,1},{4,6},{5,7},{6,4},{7,5},{8,10},{9,11},{10,... | collective-permute-start | bytes 24584 | tf_op jit(solution)/shard_map/ppermute | solution.py:154
  45.9 1.9 %collective-permute-start.14 = (f32[2,8,128]{2,1,0:T(8,128)S(1)}, f32[2,8,128]{2,1,0:T(8,128)S(1)}, u32[]{:S(2)}, u32[]{:S(2)}) collective-permute-start(f32[2,8,128]{2,1,0:T(8,128)S(1)} %get-tuple-element.91), channel_id=1, source_target_pairs={{0,4},{1,5},{2,6},{3,7},{4,0},{5,1},{6,2},{7,3},{8,12},{9,13},{10,... | collective-permute-start | bytes 24584 | tf_op jit(solution)/shard_map/ppermute | solution.py:154
  47.8 1.1 %collective-permute-start.15 = (f32[2,8,128]{2,1,0:T(8,128)S(1)}, f32[2,8,128]{2,1,0:T(8,128)S(1)}, u32[]{:S(2)}, u32[]{:S(2)}) collective-permute-start(f32[2,8,128]{2,1,0:T(8,128)S(1)} %get-tuple-element.92), channel_id=1, source_target_pairs={{0,6},{1,7},{2,4},{3,5},{4,2},{5,3},{6,0},{7,1},{8,14},{9,15},{10,... | collective-permute-start | bytes 24584 | tf_op jit(solution)/shard_map/ppermute | solution.py:154
  48.9 1.0 %shard_map.147 = f32[2,4,48,128]{3,2,1,0:T(8,128)} custom-call(f32[2,7,7,48,256]{4,3,2,1,0:T(8,128)S(1)} %get-tuple-element.55.coeffs_e, f32[2,7,5,48,256]{4,3,2,1,0:T(8,128)S(1)} %get-tuple-element.58.coeffs_o, f32[2,6,48,256]{3,2,1,0:T(8,128)S(1)} %get-tuple-element.86.second), custom_call_target="tpu_custom_call" | custom-call | bytes 3600000 | tf_op jit(solution)/shard_map/pallas_call | solution.py:88
  49.9 0.0 collective-permute-done.13.refs_1_
  49.9 0.0 collective-permute-done.14.refs_2_
  49.9 2.5 %collective-permute-done.15.refs_3_ = f32[2,8,128]{2,1,0:T(8,128)S(1)} collective-permute-done((f32[2,8,128]{2,1,0:T(8,128)S(1)}, f32[2,8,128]{2,1,0:T(8,128)S(1)}, u32[]{:S(2)}, u32[]{:S(2)}) %collective-permute-start.15) | collective-permute-done | bytes 8224 | tf_op jit(solution)/shard_map/ppermute | solution.py:154
  52.4 0.7 %shard_map.149 = f32[2,16]{1,0:T(2,128)} custom-call(f32[2,8,128]{2,1,0:T(8,128)S(1)} %get-tuple-element.89.refs_0_, f32[2,8,128]{2,1,0:T(8,128)S(1)} %collective-permute-done.13.refs_1_, f32[2,8,128]{2,1,0:T(8,128)S(1)} %collective-permute-done.14.refs_2_, f32[2,8,128]{2,1,0:T(8,128)S(1)} %collective-permute-done.15.refs_3_, s32[1,16]{1,0:T(1,128)S(1)} %bitcast.11), custom_call_target="tpu_custom_call" | custom-call | bytes 720000 | tf_op jit(solution)/shard_map/pallas_call | solution.py:88
  (11 shorter events, 0.1 us)
Async XLA Ops:
  0.6 8.7 %copy-start = (f32[3,4,48,128]{3,2,1,0:T(8,128)S(1)}, f32[3,4,48,128]{3,2,1,0:T(8,128)}, u32[]{:S(2)}) copy-start(f32[3,4,48,128]{3,2,1,0:T(8,128)} %vel.1) | copy-start | bytes 884740
  0.6 8.7 %copy-start.1 = (f32[2,4,48,128]{3,2,1,0:T(8,128)S(1)}, f32[2,4,48,128]{3,2,1,0:T(8,128)}, u32[]{:S(2)}) copy-start(f32[2,4,48,128]{3,2,1,0:T(8,128)} %state.1) | copy-start | bytes 589828
  0.7 8.7 %copy-start.3 = (f32[4,48,128]{2,1,0:T(8,128)S(1)}, f32[4,48,128]{2,1,0:T(8,128)}, u32[]{:S(2)}) copy-start(f32[4,48,128]{2,1,0:T(8,128)} %kappa.1) | copy-start | bytes 294916
  0.7 4.9 %copy-start.4 = (f32[16,128]{1,0:T(8,128)S(1)}, f32[16,128]{1,0:T(8,128)}, u32[]{:S(2)}) copy-start(f32[16,128]{1,0:T(8,128)} %foot.1) | copy-start | bytes 24580
  0.7 4.9 %copy-start.7 = (f32[16,2]{0,1:T(2,128)S(1)}, f32[16,2]{0,1:T(2,128)}, u32[]{:S(2)}) copy-start(f32[16,2]{0,1:T(2,128)} %param.20) | copy-start | bytes 388
  0.7 4.9 %copy-start.6 = (s32[16,1]{0,1:T(1,128)S(1)}, s32[16,1]{0,1:T(1,128)}, u32[]{:S(2)}) copy-start(s32[16,1]{0,1:T(1,128)} %param.19) | copy-start | bytes 196
  0.7 4.9 %copy-start.10 = (s32[16]{0:T(128)S(1)}, s32[16]{0:T(128)}, u32[]{:S(2)}) copy-start(s32[16]{0:T(128)} %param.18) | copy-start | bytes 196
  0.7 4.9 %copy-start.5 = (f32[64,2,4]{0,2,1:T(4,128)S(1)}, f32[64,2,4]{0,2,1:T(4,128)}, u32[]{:S(2)}) copy-start(f32[64,2,4]{0,2,1:T(4,128)} %param.17) | copy-start | bytes 6148
  0.7 4.9 %copy-start.9 = (s32[64,1]{0,1:T(1,128)S(1)}, s32[64,1]{0,1:T(1,128)}, u32[]{:S(2)}) copy-start(s32[64,1]{0,1:T(1,128)} %param.16) | copy-start | bytes 772
  0.7 4.9 %copy-start.8 = (s32[64]{0:T(128)S(1)}, s32[64]{0:T(128)}, u32[]{:S(2)}) copy-start(s32[64]{0:T(128)} %param.15) | copy-start | bytes 772
  0.7 8.6 %copy-start.2 = (f32[2,4,48,128]{3,2,1,0:T(8,128)S(1)}, f32[2,4,48,128]{3,2,1,0:T(8,128)}, u32[]{:S(2)}) copy-start(f32[2,4,48,128]{3,2,1,0:T(8,128)} %target.3) | copy-start | bytes 589828
  2.0 22.8 %collective-permute-start = (f32[6,4,48,128]{3,2,1,0:T(8,128)S(1)}, f32[6,4,48,128]{3,2,1,0:T(8,128)S(1)}, u32[]{:S(2)}, u32[]{:S(2)}) collective-permute-start(f32[6,4,48,128]{3,2,1,0:T(8,128)S(1)} %pad_maximum_fusion.refs_2_.refs_0_), channel_id=1, source_target_pairs={{0,8},{8,0},{16,24},{24,16},{1,9},{9,1},{17,25},{25,17},{2,10},{10... | collective-permute-start | bytes 1769480 | tf_op jit(solution)/shard_map/ppermute | solution.py:80
  3.7 23.0 %collective-permute-start.7 = (f32[6,4,48,128]{3,2,1,0:T(8,128)S(1)}, f32[6,4,48,128]{3,2,1,0:T(8,128)S(1)}, u32[]{:S(2)}, u32[]{:S(2)}) collective-permute-start(f32[6,4,48,128]{3,2,1,0:T(8,128)S(1)} %pad_maximum_fusion.refs_2_.refs_0_), channel_id=1, source_target_pairs={{8,16},{16,8},{9,17},{17,9},{10,18},{18,10},{11,19},{19,11},{12,20... | collective-permute-start | bytes 1769480 | tf_op jit(solution)/shard_map/ppermute | solution.py:80
  6.4 1.3 %collective-permute-start.3 = (f32[96,128]{1,0:T(8,128)S(1)}, f32[96,128]{1,0:T(8,128)S(1)}, u32[]{:S(2)}, u32[]{:S(2)}) collective-permute-start(f32[96,128]{1,0:T(8,128)S(1)} %get-tuple-element.49), channel_id=1, source_target_pairs={{0,1},{1,0},{2,3},{3,2},{4,5},{5,4},{6,7},{7,6},{8,9},{9,8},{10,11... | collective-permute-start | bytes 147464 | tf_op jit(solution)/shard_map/ppermute | solution.py:154
  7.8 4.5 %collective-permute-start.4 = (f32[96,128]{1,0:T(8,128)S(1)}, f32[96,128]{1,0:T(8,128)S(1)}, u32[]{:S(2)}, u32[]{:S(2)}) collective-permute-start(f32[96,128]{1,0:T(8,128)S(1)} %get-tuple-element.51), channel_id=1, source_target_pairs={{0,2},{1,3},{2,0},{3,1},{4,6},{5,7},{6,4},{7,5},{8,10},{9,11},{10,... | collective-permute-start | bytes 147464 | tf_op jit(solution)/shard_map/ppermute | solution.py:154
  9.6 7.1 %collective-permute-start.2 = (f32[192,128]{1,0:T(8,128)S(1)}, f32[192,128]{1,0:T(8,128)S(1)}, u32[]{:S(2)}, u32[]{:S(2)}) collective-permute-start(f32[192,128]{1,0:T(8,128)S(1)} %shard_map.130), channel_id=1, source_target_pairs={{1,2},{2,1},{3,4},{4,3},{5,6},{6,5},{9,10},{10,9},{11,12},{12,11},... | collective-permute-start | bytes 294920 | tf_op jit(solution)/shard_map/ppermute | solution.py:80
  11.5 5.1 %collective-permute-start.1 = (f32[192,128]{1,0:T(8,128)S(1)}, f32[192,128]{1,0:T(8,128)S(1)}, u32[]{:S(2)}, u32[]{:S(2)}) collective-permute-start(f32[192,128]{1,0:T(8,128)S(1)} %shard_map.130), channel_id=1, source_target_pairs={{0,1},{1,0},{2,3},{3,2},{4,5},{5,4},{6,7},{7,6},{8,9},{9,8},{10,11... | collective-permute-start | bytes 294920 | tf_op jit(solution)/shard_map/ppermute | solution.py:80
  12.2 4.9 %collective-permute-start.5 = (f32[96,128]{1,0:T(8,128)S(1)}, f32[96,128]{1,0:T(8,128)S(1)}, u32[]{:S(2)}, u32[]{:S(2)}) collective-permute-start(f32[96,128]{1,0:T(8,128)S(1)} %get-tuple-element.53), channel_id=1, source_target_pairs={{0,4},{1,5},{2,6},{3,7},{4,0},{5,1},{6,2},{7,3},{8,12},{9,13},{10,... | collective-permute-start | bytes 147464 | tf_op jit(solution)/shard_map/ppermute | solution.py:154
  17.2 5.2 %collective-permute-start.6 = (f32[288,128]{1,0:T(8,128)S(1)}, f32[288,128]{1,0:T(8,128)S(1)}, u32[]{:S(2)}, u32[]{:S(2)}) collective-permute-start(f32[288,128]{1,0:T(8,128)S(1)} %get-tuple-element.54.refs_3_.refs_1_.got), channel_id=1, source_target_pairs={{0,8},{8,0},{16,24},{24,16},{1,9},{9,1},{17,25},{25,17},{2,10},{10... | collective-permute-start | bytes 442376 | tf_op jit(solution)/shard_map/ppermute | solution.py:80
  17.3 8.5 %collective-permute-start.8 = (f32[288,128]{1,0:T(8,128)S(1)}, f32[288,128]{1,0:T(8,128)S(1)}, u32[]{:S(2)}, u32[]{:S(2)}) collective-permute-start(f32[288,128]{1,0:T(8,128)S(1)} %get-tuple-element.54.refs_3_.refs_1_.got), channel_id=1, source_target_pairs={{8,16},{16,8},{9,17},{17,9},{10,18},{18,10},{11,19},{19,11},{12,20... | collective-permute-start | bytes 442376 | tf_op jit(solution)/shard_map/ppermute | solution.py:80
  22.5 4.9 %collective-permute-start.9 = (f32[16,128]{1,0:T(8,128)S(1)}, f32[16,128]{1,0:T(8,128)S(1)}, u32[]{:S(2)}, u32[]{:S(2)}) collective-permute-start(f32[16,128]{1,0:T(8,128)S(1)} %get-tuple-element.70), channel_id=1, source_target_pairs={{0,16},{8,24},{16,0},{24,8},{1,17},{9,25},{17,1},{25,9},{2,18},{10... | collective-permute-start | bytes 24584 | tf_op jit(solution)/shard_map/ppermute | solution.py:154
  31.4 6.1 %collective-permute-start.10 = (f32[456,128]{1,0:T(8,128)S(1)}, f32[456,128]{1,0:T(8,128)S(1)}, u32[]{:S(2)}, u32[]{:S(2)}) collective-permute-start(f32[456,128]{1,0:T(8,128)S(1)} %get-tuple-element.78.sent), channel_id=1, source_target_pairs={{0,8},{8,0},{16,24},{24,16},{1,9},{9,1},{17,25},{25,17},{2,10},{10... | collective-permute-start | bytes 700424 | tf_op jit(solution)/shard_map/ppermute | solution.py:80
  33.4 7.9 %collective-permute-start.11 = (f32[456,128]{1,0:T(8,128)S(1)}, f32[456,128]{1,0:T(8,128)S(1)}, u32[]{:S(2)}, u32[]{:S(2)}) collective-permute-start(f32[456,128]{1,0:T(8,128)S(1)} %get-tuple-element.78.sent), channel_id=1, source_target_pairs={{8,16},{16,8},{9,17},{17,9},{10,18},{18,10},{11,19},{19,11},{12,20... | collective-permute-start | bytes 700424 | tf_op jit(solution)/shard_map/ppermute | solution.py:80
  44.1 1.2 %collective-permute-start.12 = (f32[4,8,128]{2,1,0:T(8,128)S(1)}, f32[4,8,128]{2,1,0:T(8,128)S(1)}, u32[]{:S(2)}, u32[]{:S(2)}) collective-permute-start(f32[4,8,128]{2,1,0:T(8,128)S(1)} %get-tuple-element.88), channel_id=1, source_target_pairs={{0,1},{1,0},{2,3},{3,2},{4,5},{5,4},{6,7},{7,6},{8,9},{9,8},{10,11... | collective-permute-start | bytes 49160 | tf_op jit(solution)/shard_map/ppermute | solution.py:154
  45.4 4.5 %collective-permute-start.13 = (f32[2,8,128]{2,1,0:T(8,128)S(1)}, f32[2,8,128]{2,1,0:T(8,128)S(1)}, u32[]{:S(2)}, u32[]{:S(2)}) collective-permute-start(f32[2,8,128]{2,1,0:T(8,128)S(1)} %get-tuple-element.90), channel_id=1, source_target_pairs={{0,2},{1,3},{2,0},{3,1},{4,6},{5,7},{6,4},{7,5},{8,10},{9,11},{10,... | collective-permute-start | bytes 24584 | tf_op jit(solution)/shard_map/ppermute | solution.py:154
  45.9 4.0 %collective-permute-start.14 = (f32[2,8,128]{2,1,0:T(8,128)S(1)}, f32[2,8,128]{2,1,0:T(8,128)S(1)}, u32[]{:S(2)}, u32[]{:S(2)}) collective-permute-start(f32[2,8,128]{2,1,0:T(8,128)S(1)} %get-tuple-element.91), channel_id=1, source_target_pairs={{0,4},{1,5},{2,6},{3,7},{4,0},{5,1},{6,2},{7,3},{8,12},{9,13},{10,... | collective-permute-start | bytes 24584 | tf_op jit(solution)/shard_map/ppermute | solution.py:154
  47.8 4.5 %collective-permute-start.15 = (f32[2,8,128]{2,1,0:T(8,128)S(1)}, f32[2,8,128]{2,1,0:T(8,128)S(1)}, u32[]{:S(2)}, u32[]{:S(2)}) collective-permute-start(f32[2,8,128]{2,1,0:T(8,128)S(1)} %get-tuple-element.92), channel_id=1, source_target_pairs={{0,6},{1,7},{2,4},{3,5},{4,2},{5,3},{6,0},{7,1},{8,14},{9,15},{10,... | collective-permute-start | bytes 24584 | tf_op jit(solution)/shard_map/ppermute | solution.py:154
